TPU v7x, 512 devices: a whole 4x4x16 slice. The times are simulated.
512 devices in a mesh: lvl: 128 (over z, x, core), row: 4 (over y).
Axes of the slice: x: 4, y: 4, z: 16, core: 2. Of those that a mesh axis runs over, the one named last changes fastest.
Arguments:
- right_side: bfloat16 [7168, 64, 128], P(('lvl', 'row')), may hold values from -4 to 4
- factor_blocks: bfloat16 [7168, 3, 64, 64], P(('lvl', 'row')), may hold values from -0.3125 to 0.3125
- diag_inverse: bfloat16 [7168, 64, 64], P(('lvl', 'row')), may hold values from -1 to 2.5
- pattern: int32 [7168, 3], P(('lvl', 'row')), may hold values from 0 to 41, as said below
Outputs:
- forward_solution: bfloat16 [7168, 64, 128], P(('lvl', 'row'))
- backward_solution: bfloat16 [7168, 64, 128], P(('lvl', 'row'))
Inputs may be any that keep to these rules, and one draw needn't show every extreme that they name: `pattern`: entries of block rows of level 0 are not used. For a block row of rank 0 every entry is at least 14; for a block row of the last rank, 63, every entry is below 28.
All inputs are finite; a program needn't handle non-finite values.
Results may differ from a plain program's by a relative error of at most 0.02.
Values may be sent and summed in bfloat16 or wider, within the bound.
No kernel may reach another device: no remote copies, remote signals or barrier semaphores. Data moves between devices by JAX's collectives and lax.ppermute only.
A program may use at most 64 MiB of HBM per device.

v0:
```python
import jax
import jax.numpy as jnp
from jax import lax
from jax.sharding import PartitionSpec as P

LEVELS = 8


def from_behind(value, axis, steps):
    count = lax.axis_size(axis)
    pairs = [(source, (source + steps) % count) for source in range(count)]
    return lax.ppermute(value, axis, pairs)


def padded_2(array, sides, width):
    for axis, dim in sides:
        count, length = (lax.axis_size(axis), array.shape[dim])
        up = [(i, (i + 1) % count) for i in range(count)]
        down = [(j, i) for i, j in up]
        last = lax.slice_in_dim(array, length - width, length, axis=dim)
        leading = lax.slice_in_dim(array, 0, width, axis=dim)
        before = lax.ppermute(last, axis, up)
        after = lax.ppermute(leading, axis, down)
        array = jnp.concatenate([before, array, after], axis=dim)
    return array


def per_device(right_side, factor_blocks, diag_inverse, pattern):
    slot_count = right_side.shape[0]
    block_order = right_side.shape[1]
    column_count = right_side.shape[2]
    links = factor_blocks.shape[1]
    lvl_count = lax.axis_size("lvl")
    group_size = lvl_count // LEVELS
    rotation = group_size + group_size // 2
    own_level = (lax.axis_index("lvl") + rotation) % lvl_count // group_size
    block_count = 1
    block_width = column_count // block_count
    flat_width = block_order * block_width
    step_count = LEVELS + block_count - 1
    has_lower = (own_level > 0).astype(jnp.float32)
    has_upper = (own_level < LEVELS - 1).astype(jnp.float32)

    def forward_step(step_index, state_pair):
        latest, solved = state_pair
        rhs_block = step_index - own_level
        active = (rhs_block >= 0) & (rhs_block < block_count)
        earlier = from_behind(latest, "lvl", group_size)
        window = padded_2(earlier, ((("lvl", "row"), 0),), slot_count)
        picked = window[pattern].reshape(slot_count, links, block_order, block_width)
        coupled = jnp.einsum(
            "nkab,nkbw->naw", factor_blocks, picked, preferred_element_type=jnp.float32
        )
        rhs_part = right_side.astype(jnp.float32)
        reduced = (rhs_part - has_lower * coupled).astype(jnp.bfloat16)
        solved_now = jnp.einsum(
            "nab,nbw->naw", diag_inverse, reduced, preferred_element_type=jnp.float32
        ).astype(jnp.bfloat16)
        return (solved_now.reshape(slot_count, flat_width), jnp.where(active, solved_now, solved))

    start_pair = (jnp.zeros((slot_count, flat_width), jnp.bfloat16), jnp.zeros_like(right_side))
    forward_solution = lax.fori_loop(0, step_count, forward_step, start_pair)[1]

    def incoming_sum(latest):
        latest_blocks = latest.reshape(slot_count, block_order, block_width)
        products = jnp.einsum(
            "nkba,nbw->nkaw", factor_blocks, latest_blocks, preferred_element_type=jnp.float32
        )
        flat_terms = products.reshape(slot_count * links, flat_width)
        partial_value = jax.ops.segment_sum(
            flat_terms, pattern.reshape(-1), num_segments=3 * slot_count
        )
        partial_value = lax.optimization_barrier(partial_value.astype(jnp.bfloat16))
        arrived = from_behind(partial_value, "lvl", -group_size)
        side_parts = jnp.concatenate([arrived[:slot_count], arrived[2 * slot_count :]], 0)
        padded = padded_2(side_parts, ((("lvl", "row"), 0),), slot_count)
        own_part = arrived[slot_count : 2 * slot_count].astype(jnp.float32)
        total_sum = (
            own_part
            + padded[:slot_count].astype(jnp.float32)
            + padded[3 * slot_count :].astype(jnp.float32)
        )
        return total_sum.reshape(slot_count, block_order, block_width)

    def backward_step(step_index, state_pair):
        latest, solved = state_pair
        rhs_block = step_index - (LEVELS - 1 - own_level)
        active = (rhs_block >= 0) & (rhs_block < block_count)
        incoming = has_upper * incoming_sum(latest)
        rhs_part = forward_solution.astype(jnp.float32)
        reduced = (rhs_part - incoming).astype(jnp.bfloat16)
        solved_now = jnp.einsum(
            "nba,nbw->naw", diag_inverse, reduced, preferred_element_type=jnp.float32
        ).astype(jnp.bfloat16)
        return (solved_now.reshape(slot_count, flat_width), jnp.where(active, solved_now, solved))

    backward_solution = lax.fori_loop(0, step_count, backward_step, start_pair)[1]
    return (forward_solution, backward_solution)


def solution(mesh):
    return jax.shard_map(
        per_device,
        mesh=mesh,
        in_specs=(
            P(("lvl", "row"), None, None),
            P(("lvl", "row"), None, None, None),
            P(("lvl", "row"), None, None),
            P(("lvl", "row"), None),
        ),
        out_specs=(P(("lvl", "row"), None, None), P(("lvl", "row"), None, None)),
        check_vma=False,
    )
```

profile of v0, /device:TPU:384, one launch (start us, length us, event | category | flops | bytes accessed | tf_op | source)
XLA Modules:
  0.0 757.6 jit_solution(10246115301580305383)
XLA Ops:
  0.7 279.9 %while.35 = (s32[]{:T(128)}, bf16[14,8192]{1,0:T(8,128)(2,1)S(1)}, bf16[14,64,128]{2,1,0:T(8,128)(2,1)}, bf16[14,64,128]{2,1,0:T(8,128)(2,1)}, f32[]{:T(128)}, /...) while((s32[]{:T(128)}, bf16[14,8192]{1,0:T(8,128)(2,1)S(1)}, ...), condition=%wide.region_1.2_spmd.clone, body=%wide.region_0.1_spmd.clone.sunk | while | flops 61588612 | bytes 14292659 | solution.py:62
  4.1 14.3 %collective-permute-done = bf16[14,8192]{1,0:T(8,128)(2,1)S(1)} collective-permute-done((bf16[14,8192]{1,0:T(8,128)(2,1)S(1)}, bf16[14,8192]{1,0:T(8,128)(2,1)S(1)}, u32[]{:S(2)}, u32[]{:S(2)}) %collective-permute-start) | collective-permute-done | bytes 229408 | tf_op jit(solution)/shard_map/while/body/eval_jaxpr/ppermute | solution.py:12
  28.0 8.3 %collective-permute-done.2 = bf16[14,8192]{1,0:T(8,128)(2,1)S(1)} collective-permute-done((bf16[14,8192]{1,0:T(8,128)(2,1)S(1)}, bf16[14,8192]{1,0:T(8,128)(2,1)S(1)}, u32[]{:S(2)}, u32[]{:S(2)}) %collective-permute-start.2) | collective-permute-done | bytes 229408 | tf_op jit(solution)/shard_map/while/body/eval_jaxpr/ppermute | solution.py:22
  42.9 7.9 %collective-permute-done = bf16[14,8192]{1,0:T(8,128)(2,1)S(1)} collective-permute-done((bf16[14,8192]{1,0:T(8,128)(2,1)S(1)}, bf16[14,8192]{1,0:T(8,128)(2,1)S(1)}, u32[]{:S(2)}, u32[]{:S(2)}) %collective-permute-start) | collective-permute-done | bytes 229408 | tf_op jit(solution)/shard_map/while/body/eval_jaxpr/ppermute | solution.py:12
  59.0 8.0 %collective-permute-done.2 = bf16[14,8192]{1,0:T(8,128)(2,1)S(1)} collective-permute-done((bf16[14,8192]{1,0:T(8,128)(2,1)S(1)}, bf16[14,8192]{1,0:T(8,128)(2,1)S(1)}, u32[]{:S(2)}, u32[]{:S(2)}) %collective-permute-start.2) | collective-permute-done | bytes 229408 | tf_op jit(solution)/shard_map/while/body/eval_jaxpr/ppermute | solution.py:22
  74.9 7.4 collective-permute-done
  90.6 6.8 collective-permute-done.2
  102.3 8.1 %collective-permute-start = (bf16[14,8192]{1,0:T(8,128)(2,1)S(1)}, bf16[14,8192]{1,0:T(8,128)(2,1)S(1)}, u32[]{:S(2)}, u32[]{:S(2)}) collective-permute-start(bf16[14,8192]{1,0:T(8,128)(2,1)S(1)} %get-tuple-element.671), channel_id=1, source_target_pairs={{0,64},{4,68},{8,72},{12,76},{16,80},{20,84},{24,88},{28,92},{32,9... | collective-permute-start | bytes 688136 | tf_op jit(solution)/shard_map/while/body/eval_jaxpr/ppermute | solution.py:12
  110.4 6.7 collective-permute-done
  125.3 6.8 collective-permute-done.2
  136.9 7.5 collective-permute-start
  144.5 7.2 collective-permute-done
  151.7 5.3 collective-permute-start.1
  160.9 9.3 %collective-permute-done.2 = bf16[14,8192]{1,0:T(8,128)(2,1)S(1)} collective-permute-done((bf16[14,8192]{1,0:T(8,128)(2,1)S(1)}, bf16[14,8192]{1,0:T(8,128)(2,1)S(1)}, u32[]{:S(2)}, u32[]{:S(2)}) %collective-permute-start.2) | collective-permute-done | bytes 229408 | tf_op jit(solution)/shard_map/while/body/eval_jaxpr/ppermute | solution.py:22
  180.0 7.4 collective-permute-done
  187.4 5.2 collective-permute-start.1
  196.5 9.3 %collective-permute-done.2 = bf16[14,8192]{1,0:T(8,128)(2,1)S(1)} collective-permute-done((bf16[14,8192]{1,0:T(8,128)(2,1)S(1)}, bf16[14,8192]{1,0:T(8,128)(2,1)S(1)}, u32[]{:S(2)}, u32[]{:S(2)}) %collective-permute-start.2) | collective-permute-done | bytes 229408 | tf_op jit(solution)/shard_map/while/body/eval_jaxpr/ppermute | solution.py:22
  212.9 9.4 %collective-permute-done = bf16[14,8192]{1,0:T(8,128)(2,1)S(1)} collective-permute-done((bf16[14,8192]{1,0:T(8,128)(2,1)S(1)}, bf16[14,8192]{1,0:T(8,128)(2,1)S(1)}, u32[]{:S(2)}, u32[]{:S(2)}) %collective-permute-start) | collective-permute-done | bytes 229408 | tf_op jit(solution)/shard_map/while/body/eval_jaxpr/ppermute | solution.py:12
  222.3 5.9 collective-permute-start.1
  232.1 9.3 %collective-permute-done.2 = bf16[14,8192]{1,0:T(8,128)(2,1)S(1)} collective-permute-done((bf16[14,8192]{1,0:T(8,128)(2,1)S(1)}, bf16[14,8192]{1,0:T(8,128)(2,1)S(1)}, u32[]{:S(2)}, u32[]{:S(2)}) %collective-permute-start.2) | collective-permute-done | bytes 229408 | tf_op jit(solution)/shard_map/while/body/eval_jaxpr/ppermute | solution.py:22
  248.1 9.9 %collective-permute-done = bf16[14,8192]{1,0:T(8,128)(2,1)S(1)} collective-permute-done((bf16[14,8192]{1,0:T(8,128)(2,1)S(1)}, bf16[14,8192]{1,0:T(8,128)(2,1)S(1)}, u32[]{:S(2)}, u32[]{:S(2)}) %collective-permute-start) | collective-permute-done | bytes 229408 | tf_op jit(solution)/shard_map/while/body/eval_jaxpr/ppermute | solution.py:12
  266.5 9.3 %collective-permute-done.2 = bf16[14,8192]{1,0:T(8,128)(2,1)S(1)} collective-permute-done((bf16[14,8192]{1,0:T(8,128)(2,1)S(1)}, bf16[14,8192]{1,0:T(8,128)(2,1)S(1)}, u32[]{:S(2)}, u32[]{:S(2)}) %collective-permute-start.2) | collective-permute-done | bytes 229408 | tf_op jit(solution)/shard_map/while/body/eval_jaxpr/ppermute | solution.py:22
  284.0 473.5 %while.36 = (s32[]{:T(128)}, bf16[14,8192]{1,0:T(8,128)(2,1)S(1)}, bf16[14,64,128]{2,1,0:T(8,128)(2,1)}, bf16[14,64,128]{2,1,0:T(8,128)(2,1)}, f32[]{:T(128)}, /...) while((s32[]{:T(128)}, bf16[14,8192]{1,0:T(8,128)(2,1)S(1)}, ...), condition=%wide.wide.region_4.5_spmd.clone, body=%wide.wide.region_2.4_spmd.clone.sunk | while | flops 60784648 | bytes 27263400 | solution.py:97
  292.0 24.3 %collective-permute-done.3 = bf16[42,8192]{1,0:T(8,128)(2,1)S(1)} collective-permute-done((bf16[42,8192]{1,0:T(8,128)(2,1)S(1)}, bf16[42,8192]{1,0:T(8,128)(2,1)S(1)}, u32[]{:S(2)}, u32[]{:S(2)}) %collective-permute-start.3) | collective-permute-done | bytes 688160 | tf_op jit(solution)/shard_map/while/body/eval_jaxpr/ppermute | solution.py:12
  316.4 13.1 %collective-permute-start.4 = (bf16[14,8192]{1,0:T(8,128)(2,1)S(1)}, bf16[14,8192]{1,0:T(8,128)(2,1)S(1)}, u32[]{:S(2)}, u32[]{:S(2)}) collective-permute-start(bf16[14,8192]{1,0:T(8,128)(2,1)S(1)} %get-tuple-element.654), channel_id=1, source_target_pairs={{1,0},{2,1},{3,2},{4,3},{5,4},{6,5},{7,6},{8,7},{9,8},{10,9},{11,1... | collective-permute-start | bytes 688136 | tf_op jit(solution)/shard_map/while/body/eval_jaxpr/ppermute | solution.py:23
  333.3 9.3 %collective-permute-done.5 = bf16[14,8192]{1,0:T(8,128)(2,1)S(1)} collective-permute-done((bf16[14,8192]{1,0:T(8,128)(2,1)S(1)}, bf16[14,8192]{1,0:T(8,128)(2,1)S(1)}, u32[]{:S(2)}, u32[]{:S(2)}) %collective-permute-start.5) | collective-permute-done | bytes 229408 | tf_op jit(solution)/shard_map/while/body/eval_jaxpr/ppermute | solution.py:22
  351.3 20.8 %collective-permute-done.3 = bf16[42,8192]{1,0:T(8,128)(2,1)S(1)} collective-permute-done((bf16[42,8192]{1,0:T(8,128)(2,1)S(1)}, bf16[42,8192]{1,0:T(8,128)(2,1)S(1)}, u32[]{:S(2)}, u32[]{:S(2)}) %collective-permute-start.3) | collective-permute-done | bytes 688160 | tf_op jit(solution)/shard_map/while/body/eval_jaxpr/ppermute | solution.py:12
  372.2 15.1 %collective-permute-start.4 = (bf16[14,8192]{1,0:T(8,128)(2,1)S(1)}, bf16[14,8192]{1,0:T(8,128)(2,1)S(1)}, u32[]{:S(2)}, u32[]{:S(2)}) collective-permute-start(bf16[14,8192]{1,0:T(8,128)(2,1)S(1)} %get-tuple-element.654), channel_id=1, source_target_pairs={{1,0},{2,1},{3,2},{4,3},{5,4},{6,5},{7,6},{8,7},{9,8},{10,9},{11,1... | collective-permute-start | bytes 688136 | tf_op jit(solution)/shard_map/while/body/eval_jaxpr/ppermute | solution.py:23
  393.0 7.4 collective-permute-done.5
  409.2 17.6 %collective-permute-done.3 = bf16[42,8192]{1,0:T(8,128)(2,1)S(1)} collective-permute-done((bf16[42,8192]{1,0:T(8,128)(2,1)S(1)}, bf16[42,8192]{1,0:T(8,128)(2,1)S(1)}, u32[]{:S(2)}, u32[]{:S(2)}) %collective-permute-start.3) | collective-permute-done | bytes 688160 | tf_op jit(solution)/shard_map/while/body/eval_jaxpr/ppermute | solution.py:12
  426.9 20.5 %collective-permute-start.4 = (bf16[14,8192]{1,0:T(8,128)(2,1)S(1)}, bf16[14,8192]{1,0:T(8,128)(2,1)S(1)}, u32[]{:S(2)}, u32[]{:S(2)}) collective-permute-start(bf16[14,8192]{1,0:T(8,128)(2,1)S(1)} %get-tuple-element.654), channel_id=1, source_target_pairs={{1,0},{2,1},{3,2},{4,3},{5,4},{6,5},{7,6},{8,7},{9,8},{10,9},{11,1... | collective-permute-start | bytes 688136 | tf_op jit(solution)/shard_map/while/body/eval_jaxpr/ppermute | solution.py:23
  449.3 13.1 %collective-permute-done.4 = bf16[14,8192]{1,0:T(8,128)(2,1)S(1)} collective-permute-done((bf16[14,8192]{1,0:T(8,128)(2,1)S(1)}, bf16[14,8192]{1,0:T(8,128)(2,1)S(1)}, u32[]{:S(2)}, u32[]{:S(2)}) %collective-permute-start.4) | collective-permute-done | bytes 229408 | tf_op jit(solution)/shard_map/while/body/eval_jaxpr/ppermute | solution.py:23
  471.2 18.5 %collective-permute-done.3 = bf16[42,8192]{1,0:T(8,128)(2,1)S(1)} collective-permute-done((bf16[42,8192]{1,0:T(8,128)(2,1)S(1)}, bf16[42,8192]{1,0:T(8,128)(2,1)S(1)}, u32[]{:S(2)}, u32[]{:S(2)}) %collective-permute-start.3) | collective-permute-done | bytes 688160 | tf_op jit(solution)/shard_map/while/body/eval_jaxpr/ppermute | solution.py:12
  489.8 18.8 %collective-permute-start.4 = (bf16[14,8192]{1,0:T(8,128)(2,1)S(1)}, bf16[14,8192]{1,0:T(8,128)(2,1)S(1)}, u32[]{:S(2)}, u32[]{:S(2)}) collective-permute-start(bf16[14,8192]{1,0:T(8,128)(2,1)S(1)} %get-tuple-element.654), channel_id=1, source_target_pairs={{1,0},{2,1},{3,2},{4,3},{5,4},{6,5},{7,6},{8,7},{9,8},{10,9},{11,1... | collective-permute-start | bytes 688136 | tf_op jit(solution)/shard_map/while/body/eval_jaxpr/ppermute | solution.py:23
  510.6 11.6 %collective-permute-done.4 = bf16[14,8192]{1,0:T(8,128)(2,1)S(1)} collective-permute-done((bf16[14,8192]{1,0:T(8,128)(2,1)S(1)}, bf16[14,8192]{1,0:T(8,128)(2,1)S(1)}, u32[]{:S(2)}, u32[]{:S(2)}) %collective-permute-start.4) | collective-permute-done | bytes 229408 | tf_op jit(solution)/shard_map/while/body/eval_jaxpr/ppermute | solution.py:23
  530.9 15.3 %collective-permute-done.3 = bf16[42,8192]{1,0:T(8,128)(2,1)S(1)} collective-permute-done((bf16[42,8192]{1,0:T(8,128)(2,1)S(1)}, bf16[42,8192]{1,0:T(8,128)(2,1)S(1)}, u32[]{:S(2)}, u32[]{:S(2)}) %collective-permute-start.3) | collective-permute-done | bytes 688160 | tf_op jit(solution)/shard_map/while/body/eval_jaxpr/ppermute | solution.py:12
  546.3 19.4 %collective-permute-start.4 = (bf16[14,8192]{1,0:T(8,128)(2,1)S(1)}, bf16[14,8192]{1,0:T(8,128)(2,1)S(1)}, u32[]{:S(2)}, u32[]{:S(2)}) collective-permute-start(bf16[14,8192]{1,0:T(8,128)(2,1)S(1)} %get-tuple-element.654), channel_id=1, source_target_pairs={{1,0},{2,1},{3,2},{4,3},{5,4},{6,5},{7,6},{8,7},{9,8},{10,9},{11,1... | collective-permute-start | bytes 688136 | tf_op jit(solution)/shard_map/while/body/eval_jaxpr/ppermute | solution.py:23
  567.6 11.9 %collective-permute-done.4 = bf16[14,8192]{1,0:T(8,128)(2,1)S(1)} collective-permute-done((bf16[14,8192]{1,0:T(8,128)(2,1)S(1)}, bf16[14,8192]{1,0:T(8,128)(2,1)S(1)}, u32[]{:S(2)}, u32[]{:S(2)}) %collective-permute-start.4) | collective-permute-done | bytes 229408 | tf_op jit(solution)/shard_map/while/body/eval_jaxpr/ppermute | solution.py:23
  588.3 15.0 %collective-permute-done.3 = bf16[42,8192]{1,0:T(8,128)(2,1)S(1)} collective-permute-done((bf16[42,8192]{1,0:T(8,128)(2,1)S(1)}, bf16[42,8192]{1,0:T(8,128)(2,1)S(1)}, u32[]{:S(2)}, u32[]{:S(2)}) %collective-permute-start.3) | collective-permute-done | bytes 688160 | tf_op jit(solution)/shard_map/while/body/eval_jaxpr/ppermute | solution.py:12
  603.3 22.3 %collective-permute-start.4 = (bf16[14,8192]{1,0:T(8,128)(2,1)S(1)}, bf16[14,8192]{1,0:T(8,128)(2,1)S(1)}, u32[]{:S(2)}, u32[]{:S(2)}) collective-permute-start(bf16[14,8192]{1,0:T(8,128)(2,1)S(1)} %get-tuple-element.654), channel_id=1, source_target_pairs={{1,0},{2,1},{3,2},{4,3},{5,4},{6,5},{7,6},{8,7},{9,8},{10,9},{11,1... | collective-permute-start | bytes 688136 | tf_op jit(solution)/shard_map/while/body/eval_jaxpr/ppermute | solution.py:23
  627.6 8.3 %collective-permute-done.4 = bf16[14,8192]{1,0:T(8,128)(2,1)S(1)} collective-permute-done((bf16[14,8192]{1,0:T(8,128)(2,1)S(1)}, bf16[14,8192]{1,0:T(8,128)(2,1)S(1)}, u32[]{:S(2)}, u32[]{:S(2)}) %collective-permute-start.4) | collective-permute-done | bytes 229408 | tf_op jit(solution)/shard_map/while/body/eval_jaxpr/ppermute | solution.py:23
  647.5 20.6 %collective-permute-done.3 = bf16[42,8192]{1,0:T(8,128)(2,1)S(1)} collective-permute-done((bf16[42,8192]{1,0:T(8,128)(2,1)S(1)}, bf16[42,8192]{1,0:T(8,128)(2,1)S(1)}, u32[]{:S(2)}, u32[]{:S(2)}) %collective-permute-start.3) | collective-permute-done | bytes 688160 | tf_op jit(solution)/shard_map/while/body/eval_jaxpr/ppermute | solution.py:12
  668.2 16.1 %collective-permute-start.4 = (bf16[14,8192]{1,0:T(8,128)(2,1)S(1)}, bf16[14,8192]{1,0:T(8,128)(2,1)S(1)}, u32[]{:S(2)}, u32[]{:S(2)}) collective-permute-start(bf16[14,8192]{1,0:T(8,128)(2,1)S(1)} %get-tuple-element.654), channel_id=1, source_target_pairs={{1,0},{2,1},{3,2},{4,3},{5,4},{6,5},{7,6},{8,7},{9,8},{10,9},{11,1... | collective-permute-start | bytes 688136 | tf_op jit(solution)/shard_map/while/body/eval_jaxpr/ppermute | solution.py:23
  686.3 5.7 collective-permute-done.4
  692.0 5.4 collective-permute-done.5
  706.2 18.6 %collective-permute-done.3 = bf16[42,8192]{1,0:T(8,128)(2,1)S(1)} collective-permute-done((bf16[42,8192]{1,0:T(8,128)(2,1)S(1)}, bf16[42,8192]{1,0:T(8,128)(2,1)S(1)}, u32[]{:S(2)}, u32[]{:S(2)}) %collective-permute-start.3) | collective-permute-done | bytes 688160 | tf_op jit(solution)/shard_map/while/body/eval_jaxpr/ppermute | solution.py:12
  724.9 17.2 %collective-permute-start.4 = (bf16[14,8192]{1,0:T(8,128)(2,1)S(1)}, bf16[14,8192]{1,0:T(8,128)(2,1)S(1)}, u32[]{:S(2)}, u32[]{:S(2)}) collective-permute-start(bf16[14,8192]{1,0:T(8,128)(2,1)S(1)} %get-tuple-element.654), channel_id=1, source_target_pairs={{1,0},{2,1},{3,2},{4,3},{5,4},{6,5},{7,6},{8,7},{9,8},{10,9},{11,1... | collective-permute-start | bytes 688136 | tf_op jit(solution)/shard_map/while/body/eval_jaxpr/ppermute | solution.py:23
  746.0 9.3 %collective-permute-done.5 = bf16[14,8192]{1,0:T(8,128)(2,1)S(1)} collective-permute-done((bf16[14,8192]{1,0:T(8,128)(2,1)S(1)}, bf16[14,8192]{1,0:T(8,128)(2,1)S(1)}, u32[]{:S(2)}, u32[]{:S(2)}) %collective-permute-start.5) | collective-permute-done | bytes 229408 | tf_op jit(solution)/shard_map/while/body/eval_jaxpr/ppermute | solution.py:22
  (356 shorter events, 210.3 us)
Async XLA Ops:
  0.7 17.7 %collective-permute-start = (bf16[14,8192]{1,0:T(8,128)(2,1)S(1)}, bf16[14,8192]{1,0:T(8,128)(2,1)S(1)}, u32[]{:S(2)}, u32[]{:S(2)}) collective-permute-start(bf16[14,8192]{1,0:T(8,128)(2,1)S(1)} %get-tuple-element.671), channel_id=1, source_target_pairs={{0,64},{4,68},{8,72},{12,76},{16,80},{20,84},{24,88},{28,92},{32,9... | collective-permute-start | bytes 688136 | tf_op jit(solution)/shard_map/while/body/eval_jaxpr/ppermute | solution.py:12
  18.4 9.6 %collective-permute-start.1 = (bf16[14,8192]{1,0:T(8,128)(2,1)S(1)}, bf16[14,8192]{1,0:T(8,128)(2,1)S(1)}, u32[]{:S(2)}, u32[]{:S(2)}) collective-permute-start(bf16[14,8192]{1,0:T(8,128)(2,1)S(1)} %collective-permute-done), channel_id=1, source_target_pairs={{1,0},{2,1},{3,2},{4,3},{5,4},{6,5},{7,6},{8,7},{9,8},{10,9},{11,1... | collective-permute-start | bytes 688136 | tf_op jit(solution)/shard_map/while/body/eval_jaxpr/ppermute | solution.py:23
  23.2 13.1 %collective-permute-start.2 = (bf16[14,8192]{1,0:T(8,128)(2,1)S(1)}, bf16[14,8192]{1,0:T(8,128)(2,1)S(1)}, u32[]{:S(2)}, u32[]{:S(2)}) collective-permute-start(bf16[14,8192]{1,0:T(8,128)(2,1)S(1)} %collective-permute-done), channel_id=1, source_target_pairs={{0,1},{1,2},{2,3},{3,4},{4,5},{5,6},{6,7},{7,8},{8,9},{9,10},{10,1... | collective-permute-start | bytes 688136 | tf_op jit(solution)/shard_map/while/body/eval_jaxpr/ppermute | solution.py:22
  40.2 10.5 %collective-permute-start = (bf16[14,8192]{1,0:T(8,128)(2,1)S(1)}, bf16[14,8192]{1,0:T(8,128)(2,1)S(1)}, u32[]{:S(2)}, u32[]{:S(2)}) collective-permute-start(bf16[14,8192]{1,0:T(8,128)(2,1)S(1)} %get-tuple-element.671), channel_id=1, source_target_pairs={{0,64},{4,68},{8,72},{12,76},{16,80},{20,84},{24,88},{28,92},{32,9... | collective-permute-start | bytes 688136 | tf_op jit(solution)/shard_map/while/body/eval_jaxpr/ppermute | solution.py:12
  50.7 8.3 %collective-permute-start.1 = (bf16[14,8192]{1,0:T(8,128)(2,1)S(1)}, bf16[14,8192]{1,0:T(8,128)(2,1)S(1)}, u32[]{:S(2)}, u32[]{:S(2)}) collective-permute-start(bf16[14,8192]{1,0:T(8,128)(2,1)S(1)} %collective-permute-done), channel_id=1, source_target_pairs={{1,0},{2,1},{3,2},{4,3},{5,4},{6,5},{7,6},{8,7},{9,8},{10,9},{11,1... | collective-permute-start | bytes 688136 | tf_op jit(solution)/shard_map/while/body/eval_jaxpr/ppermute | solution.py:23
  53.9 13.1 %collective-permute-start.2 = (bf16[14,8192]{1,0:T(8,128)(2,1)S(1)}, bf16[14,8192]{1,0:T(8,128)(2,1)S(1)}, u32[]{:S(2)}, u32[]{:S(2)}) collective-permute-start(bf16[14,8192]{1,0:T(8,128)(2,1)S(1)} %collective-permute-done), channel_id=1, source_target_pairs={{0,1},{1,2},{2,3},{3,4},{4,5},{5,6},{6,7},{7,8},{8,9},{9,10},{10,1... | collective-permute-start | bytes 688136 | tf_op jit(solution)/shard_map/while/body/eval_jaxpr/ppermute | solution.py:22
  71.9 10.5 %collective-permute-start = (bf16[14,8192]{1,0:T(8,128)(2,1)S(1)}, bf16[14,8192]{1,0:T(8,128)(2,1)S(1)}, u32[]{:S(2)}, u32[]{:S(2)}) collective-permute-start(bf16[14,8192]{1,0:T(8,128)(2,1)S(1)} %get-tuple-element.671), channel_id=1, source_target_pairs={{0,64},{4,68},{8,72},{12,76},{16,80},{20,84},{24,88},{28,92},{32,9... | collective-permute-start | bytes 688136 | tf_op jit(solution)/shard_map/while/body/eval_jaxpr/ppermute | solution.py:12
  82.4 8.3 %collective-permute-start.1 = (bf16[14,8192]{1,0:T(8,128)(2,1)S(1)}, bf16[14,8192]{1,0:T(8,128)(2,1)S(1)}, u32[]{:S(2)}, u32[]{:S(2)}) collective-permute-start(bf16[14,8192]{1,0:T(8,128)(2,1)S(1)} %collective-permute-done), channel_id=1, source_target_pairs={{1,0},{2,1},{3,2},{4,3},{5,4},{6,5},{7,6},{8,7},{9,8},{10,9},{11,1... | collective-permute-start | bytes 688136 | tf_op jit(solution)/shard_map/while/body/eval_jaxpr/ppermute | solution.py:23
  84.3 13.1 %collective-permute-start.2 = (bf16[14,8192]{1,0:T(8,128)(2,1)S(1)}, bf16[14,8192]{1,0:T(8,128)(2,1)S(1)}, u32[]{:S(2)}, u32[]{:S(2)}) collective-permute-start(bf16[14,8192]{1,0:T(8,128)(2,1)S(1)} %collective-permute-done), channel_id=1, source_target_pairs={{0,1},{1,2},{2,3},{3,4},{4,5},{5,6},{6,7},{7,8},{8,9},{9,10},{10,1... | collective-permute-start | bytes 688136 | tf_op jit(solution)/shard_map/while/body/eval_jaxpr/ppermute | solution.py:22
  102.3 14.8 %collective-permute-start = (bf16[14,8192]{1,0:T(8,128)(2,1)S(1)}, bf16[14,8192]{1,0:T(8,128)(2,1)S(1)}, u32[]{:S(2)}, u32[]{:S(2)}) collective-permute-start(bf16[14,8192]{1,0:T(8,128)(2,1)S(1)} %get-tuple-element.671), channel_id=1, source_target_pairs={{0,64},{4,68},{8,72},{12,76},{16,80},{20,84},{24,88},{28,92},{32,9... | collective-permute-start | bytes 688136 | tf_op jit(solution)/shard_map/while/body/eval_jaxpr/ppermute | solution.py:12
  117.1 8.3 %collective-permute-start.1 = (bf16[14,8192]{1,0:T(8,128)(2,1)S(1)}, bf16[14,8192]{1,0:T(8,128)(2,1)S(1)}, u32[]{:S(2)}, u32[]{:S(2)}) collective-permute-start(bf16[14,8192]{1,0:T(8,128)(2,1)S(1)} %collective-permute-done), channel_id=1, source_target_pairs={{1,0},{2,1},{3,2},{4,3},{5,4},{6,5},{7,6},{8,7},{9,8},{10,9},{11,1... | collective-permute-start | bytes 688136 | tf_op jit(solution)/shard_map/while/body/eval_jaxpr/ppermute | solution.py:23
  119.0 13.1 %collective-permute-start.2 = (bf16[14,8192]{1,0:T(8,128)(2,1)S(1)}, bf16[14,8192]{1,0:T(8,128)(2,1)S(1)}, u32[]{:S(2)}, u32[]{:S(2)}) collective-permute-start(bf16[14,8192]{1,0:T(8,128)(2,1)S(1)} %collective-permute-done), channel_id=1, source_target_pairs={{0,1},{1,2},{2,3},{3,4},{4,5},{5,6},{6,7},{7,8},{8,9},{9,10},{10,1... | collective-permute-start | bytes 688136 | tf_op jit(solution)/shard_map/while/body/eval_jaxpr/ppermute | solution.py:22
  136.9 14.8 %collective-permute-start = (bf16[14,8192]{1,0:T(8,128)(2,1)S(1)}, bf16[14,8192]{1,0:T(8,128)(2,1)S(1)}, u32[]{:S(2)}, u32[]{:S(2)}) collective-permute-start(bf16[14,8192]{1,0:T(8,128)(2,1)S(1)} %get-tuple-element.671), channel_id=1, source_target_pairs={{0,64},{4,68},{8,72},{12,76},{16,80},{20,84},{24,88},{28,92},{32,9... | collective-permute-start | bytes 688136 | tf_op jit(solution)/shard_map/while/body/eval_jaxpr/ppermute | solution.py:12
  151.7 9.2 %collective-permute-start.1 = (bf16[14,8192]{1,0:T(8,128)(2,1)S(1)}, bf16[14,8192]{1,0:T(8,128)(2,1)S(1)}, u32[]{:S(2)}, u32[]{:S(2)}) collective-permute-start(bf16[14,8192]{1,0:T(8,128)(2,1)S(1)} %collective-permute-done), channel_id=1, source_target_pairs={{1,0},{2,1},{3,2},{4,3},{5,4},{6,5},{7,6},{8,7},{9,8},{10,9},{11,1... | collective-permute-start | bytes 688136 | tf_op jit(solution)/shard_map/while/body/eval_jaxpr/ppermute | solution.py:23
  157.0 13.1 %collective-permute-start.2 = (bf16[14,8192]{1,0:T(8,128)(2,1)S(1)}, bf16[14,8192]{1,0:T(8,128)(2,1)S(1)}, u32[]{:S(2)}, u32[]{:S(2)}) collective-permute-start(bf16[14,8192]{1,0:T(8,128)(2,1)S(1)} %collective-permute-done), channel_id=1, source_target_pairs={{0,1},{1,2},{2,3},{3,4},{4,5},{5,6},{6,7},{7,8},{8,9},{9,10},{10,1... | collective-permute-start | bytes 688136 | tf_op jit(solution)/shard_map/while/body/eval_jaxpr/ppermute | solution.py:22
  175.0 12.4 %collective-permute-start = (bf16[14,8192]{1,0:T(8,128)(2,1)S(1)}, bf16[14,8192]{1,0:T(8,128)(2,1)S(1)}, u32[]{:S(2)}, u32[]{:S(2)}) collective-permute-start(bf16[14,8192]{1,0:T(8,128)(2,1)S(1)} %get-tuple-element.671), channel_id=1, source_target_pairs={{0,64},{4,68},{8,72},{12,76},{16,80},{20,84},{24,88},{28,92},{32,9... | collective-permute-start | bytes 688136 | tf_op jit(solution)/shard_map/while/body/eval_jaxpr/ppermute | solution.py:12
  187.4 9.0 %collective-permute-start.1 = (bf16[14,8192]{1,0:T(8,128)(2,1)S(1)}, bf16[14,8192]{1,0:T(8,128)(2,1)S(1)}, u32[]{:S(2)}, u32[]{:S(2)}) collective-permute-start(bf16[14,8192]{1,0:T(8,128)(2,1)S(1)} %collective-permute-done), channel_id=1, source_target_pairs={{1,0},{2,1},{3,2},{4,3},{5,4},{6,5},{7,6},{8,7},{9,8},{10,9},{11,1... | collective-permute-start | bytes 688136 | tf_op jit(solution)/shard_map/while/body/eval_jaxpr/ppermute | solution.py:23
  192.6 13.1 %collective-permute-start.2 = (bf16[14,8192]{1,0:T(8,128)(2,1)S(1)}, bf16[14,8192]{1,0:T(8,128)(2,1)S(1)}, u32[]{:S(2)}, u32[]{:S(2)}) collective-permute-start(bf16[14,8192]{1,0:T(8,128)(2,1)S(1)} %collective-permute-done), channel_id=1, source_target_pairs={{0,1},{1,2},{2,3},{3,4},{4,5},{5,6},{6,7},{7,8},{8,9},{9,10},{10,1... | collective-permute-start | bytes 688136 | tf_op jit(solution)/shard_map/while/body/eval_jaxpr/ppermute | solution.py:22
  210.6 11.7 %collective-permute-start = (bf16[14,8192]{1,0:T(8,128)(2,1)S(1)}, bf16[14,8192]{1,0:T(8,128)(2,1)S(1)}, u32[]{:S(2)}, u32[]{:S(2)}) collective-permute-start(bf16[14,8192]{1,0:T(8,128)(2,1)S(1)} %get-tuple-element.671), channel_id=1, source_target_pairs={{0,64},{4,68},{8,72},{12,76},{16,80},{20,84},{24,88},{28,92},{32,9... | collective-permute-start | bytes 688136 | tf_op jit(solution)/shard_map/while/body/eval_jaxpr/ppermute | solution.py:12
  222.3 9.8 %collective-permute-start.1 = (bf16[14,8192]{1,0:T(8,128)(2,1)S(1)}, bf16[14,8192]{1,0:T(8,128)(2,1)S(1)}, u32[]{:S(2)}, u32[]{:S(2)}) collective-permute-start(bf16[14,8192]{1,0:T(8,128)(2,1)S(1)} %collective-permute-done), channel_id=1, source_target_pairs={{1,0},{2,1},{3,2},{4,3},{5,4},{6,5},{7,6},{8,7},{9,8},{10,9},{11,1... | collective-permute-start | bytes 688136 | tf_op jit(solution)/shard_map/while/body/eval_jaxpr/ppermute | solution.py:23
  228.2 13.1 %collective-permute-start.2 = (bf16[14,8192]{1,0:T(8,128)(2,1)S(1)}, bf16[14,8192]{1,0:T(8,128)(2,1)S(1)}, u32[]{:S(2)}, u32[]{:S(2)}) collective-permute-start(bf16[14,8192]{1,0:T(8,128)(2,1)S(1)} %collective-permute-done), channel_id=1, source_target_pairs={{0,1},{1,2},{2,3},{3,4},{4,5},{5,6},{6,7},{7,8},{8,9},{9,10},{10,1... | collective-permute-start | bytes 688136 | tf_op jit(solution)/shard_map/while/body/eval_jaxpr/ppermute | solution.py:22
  246.2 11.9 %collective-permute-start = (bf16[14,8192]{1,0:T(8,128)(2,1)S(1)}, bf16[14,8192]{1,0:T(8,128)(2,1)S(1)}, u32[]{:S(2)}, u32[]{:S(2)}) collective-permute-start(bf16[14,8192]{1,0:T(8,128)(2,1)S(1)} %get-tuple-element.671), channel_id=1, source_target_pairs={{0,64},{4,68},{8,72},{12,76},{16,80},{20,84},{24,88},{28,92},{32,9... | collective-permute-start | bytes 688136 | tf_op jit(solution)/shard_map/while/body/eval_jaxpr/ppermute | solution.py:12
  258.0 8.4 %collective-permute-start.1 = (bf16[14,8192]{1,0:T(8,128)(2,1)S(1)}, bf16[14,8192]{1,0:T(8,128)(2,1)S(1)}, u32[]{:S(2)}, u32[]{:S(2)}) collective-permute-start(bf16[14,8192]{1,0:T(8,128)(2,1)S(1)} %collective-permute-done), channel_id=1, source_target_pairs={{1,0},{2,1},{3,2},{4,3},{5,4},{6,5},{7,6},{8,7},{9,8},{10,9},{11,1... | collective-permute-start | bytes 688136 | tf_op jit(solution)/shard_map/while/body/eval_jaxpr/ppermute | solution.py:23
  262.6 13.1 %collective-permute-start.2 = (bf16[14,8192]{1,0:T(8,128)(2,1)S(1)}, bf16[14,8192]{1,0:T(8,128)(2,1)S(1)}, u32[]{:S(2)}, u32[]{:S(2)}) collective-permute-start(bf16[14,8192]{1,0:T(8,128)(2,1)S(1)} %collective-permute-done), channel_id=1, source_target_pairs={{0,1},{1,2},{2,3},{3,4},{4,5},{5,6},{6,7},{7,8},{8,9},{9,10},{10,1... | collective-permute-start | bytes 688136 | tf_op jit(solution)/shard_map/while/body/eval_jaxpr/ppermute | solution.py:22
  288.4 27.8 %collective-permute-start.3 = (bf16[42,8192]{1,0:T(8,128)(2,1)S(1)}, bf16[42,8192]{1,0:T(8,128)(2,1)S(1)}, u32[]{:S(2)}, u32[]{:S(2)}) collective-permute-start(bf16[42,8192]{1,0:T(8,128)(2,1)S(1)} %convert_element_type.159), channel_id=1, source_target_pairs={{0,448},{4,452},{8,456},{12,460},{16,464},{20,468},{24,472},{28,47... | collective-permute-start | bytes 2064392 | tf_op jit(solution)/shard_map/while/body/eval_jaxpr/ppermute | solution.py:12
  316.4 17.0 %collective-permute-start.4 = (bf16[14,8192]{1,0:T(8,128)(2,1)S(1)}, bf16[14,8192]{1,0:T(8,128)(2,1)S(1)}, u32[]{:S(2)}, u32[]{:S(2)}) collective-permute-start(bf16[14,8192]{1,0:T(8,128)(2,1)S(1)} %get-tuple-element.654), channel_id=1, source_target_pairs={{1,0},{2,1},{3,2},{4,3},{5,4},{6,5},{7,6},{8,7},{9,8},{10,9},{11,1... | collective-permute-start | bytes 688136 | tf_op jit(solution)/shard_map/while/body/eval_jaxpr/ppermute | solution.py:23
  329.5 13.1 %collective-permute-start.5 = (bf16[14,8192]{1,0:T(8,128)(2,1)S(1)}, bf16[14,8192]{1,0:T(8,128)(2,1)S(1)}, u32[]{:S(2)}, u32[]{:S(2)}) collective-permute-start(bf16[14,8192]{1,0:T(8,128)(2,1)S(1)} %get-tuple-element.655), channel_id=1, source_target_pairs={{0,1},{1,2},{2,3},{3,4},{4,5},{5,6},{6,7},{7,8},{8,9},{9,10},{10,1... | collective-permute-start | bytes 688136 | tf_op jit(solution)/shard_map/while/body/eval_jaxpr/ppermute | solution.py:22
  349.3 22.8 %collective-permute-start.3 = (bf16[42,8192]{1,0:T(8,128)(2,1)S(1)}, bf16[42,8192]{1,0:T(8,128)(2,1)S(1)}, u32[]{:S(2)}, u32[]{:S(2)}) collective-permute-start(bf16[42,8192]{1,0:T(8,128)(2,1)S(1)} %convert_element_type.159), channel_id=1, source_target_pairs={{0,448},{4,452},{8,456},{12,460},{16,464},{20,468},{24,472},{28,47... | collective-permute-start | bytes 2064392 | tf_op jit(solution)/shard_map/while/body/eval_jaxpr/ppermute | solution.py:12
  372.2 20.8 %collective-permute-start.4 = (bf16[14,8192]{1,0:T(8,128)(2,1)S(1)}, bf16[14,8192]{1,0:T(8,128)(2,1)S(1)}, u32[]{:S(2)}, u32[]{:S(2)}) collective-permute-start(bf16[14,8192]{1,0:T(8,128)(2,1)S(1)} %get-tuple-element.654), channel_id=1, source_target_pairs={{1,0},{2,1},{3,2},{4,3},{5,4},{6,5},{7,6},{8,7},{9,8},{10,9},{11,1... | collective-permute-start | bytes 688136 | tf_op jit(solution)/shard_map/while/body/eval_jaxpr/ppermute | solution.py:23
  387.3 13.1 %collective-permute-start.5 = (bf16[14,8192]{1,0:T(8,128)(2,1)S(1)}, bf16[14,8192]{1,0:T(8,128)(2,1)S(1)}, u32[]{:S(2)}, u32[]{:S(2)}) collective-permute-start(bf16[14,8192]{1,0:T(8,128)(2,1)S(1)} %get-tuple-element.655), channel_id=1, source_target_pairs={{0,1},{1,2},{2,3},{3,4},{4,5},{5,6},{6,7},{7,8},{8,9},{9,10},{10,1... | collective-permute-start | bytes 688136 | tf_op jit(solution)/shard_map/while/body/eval_jaxpr/ppermute | solution.py:22
  407.1 19.7 %collective-permute-start.3 = (bf16[42,8192]{1,0:T(8,128)(2,1)S(1)}, bf16[42,8192]{1,0:T(8,128)(2,1)S(1)}, u32[]{:S(2)}, u32[]{:S(2)}) collective-permute-start(bf16[42,8192]{1,0:T(8,128)(2,1)S(1)} %convert_element_type.159), channel_id=1, source_target_pairs={{0,448},{4,452},{8,456},{12,460},{16,464},{20,468},{24,472},{28,47... | collective-permute-start | bytes 2064392 | tf_op jit(solution)/shard_map/while/body/eval_jaxpr/ppermute | solution.py:12
  426.9 35.5 %collective-permute-start.4 = (bf16[14,8192]{1,0:T(8,128)(2,1)S(1)}, bf16[14,8192]{1,0:T(8,128)(2,1)S(1)}, u32[]{:S(2)}, u32[]{:S(2)}) collective-permute-start(bf16[14,8192]{1,0:T(8,128)(2,1)S(1)} %get-tuple-element.654), channel_id=1, source_target_pairs={{1,0},{2,1},{3,2},{4,3},{5,4},{6,5},{7,6},{8,7},{9,8},{10,9},{11,1... | collective-permute-start | bytes 688136 | tf_op jit(solution)/shard_map/while/body/eval_jaxpr/ppermute | solution.py:23
  447.4 15.0 %collective-permute-start.5 = (bf16[14,8192]{1,0:T(8,128)(2,1)S(1)}, bf16[14,8192]{1,0:T(8,128)(2,1)S(1)}, u32[]{:S(2)}, u32[]{:S(2)}) collective-permute-start(bf16[14,8192]{1,0:T(8,128)(2,1)S(1)} %get-tuple-element.655), channel_id=1, source_target_pairs={{0,1},{1,2},{2,3},{3,4},{4,5},{5,6},{6,7},{7,8},{8,9},{9,10},{10,1... | collective-permute-start | bytes 688136 | tf_op jit(solution)/shard_map/while/body/eval_jaxpr/ppermute | solution.py:22
  469.1 20.6 %collective-permute-start.3 = (bf16[42,8192]{1,0:T(8,128)(2,1)S(1)}, bf16[42,8192]{1,0:T(8,128)(2,1)S(1)}, u32[]{:S(2)}, u32[]{:S(2)}) collective-permute-start(bf16[42,8192]{1,0:T(8,128)(2,1)S(1)} %convert_element_type.159), channel_id=1, source_target_pairs={{0,448},{4,452},{8,456},{12,460},{16,464},{20,468},{24,472},{28,47... | collective-permute-start | bytes 2064392 | tf_op jit(solution)/shard_map/while/body/eval_jaxpr/ppermute | solution.py:12
  489.8 32.4 %collective-permute-start.4 = (bf16[14,8192]{1,0:T(8,128)(2,1)S(1)}, bf16[14,8192]{1,0:T(8,128)(2,1)S(1)}, u32[]{:S(2)}, u32[]{:S(2)}) collective-permute-start(bf16[14,8192]{1,0:T(8,128)(2,1)S(1)} %get-tuple-element.654), channel_id=1, source_target_pairs={{1,0},{2,1},{3,2},{4,3},{5,4},{6,5},{7,6},{8,7},{9,8},{10,9},{11,1... | collective-permute-start | bytes 688136 | tf_op jit(solution)/shard_map/while/body/eval_jaxpr/ppermute | solution.py:23
  508.6 13.5 %collective-permute-start.5 = (bf16[14,8192]{1,0:T(8,128)(2,1)S(1)}, bf16[14,8192]{1,0:T(8,128)(2,1)S(1)}, u32[]{:S(2)}, u32[]{:S(2)}) collective-permute-start(bf16[14,8192]{1,0:T(8,128)(2,1)S(1)} %get-tuple-element.655), channel_id=1, source_target_pairs={{0,1},{1,2},{2,3},{3,4},{4,5},{5,6},{6,7},{7,8},{8,9},{9,10},{10,1... | collective-permute-start | bytes 688136 | tf_op jit(solution)/shard_map/while/body/eval_jaxpr/ppermute | solution.py:22
  528.9 17.4 %collective-permute-start.3 = (bf16[42,8192]{1,0:T(8,128)(2,1)S(1)}, bf16[42,8192]{1,0:T(8,128)(2,1)S(1)}, u32[]{:S(2)}, u32[]{:S(2)}) collective-permute-start(bf16[42,8192]{1,0:T(8,128)(2,1)S(1)} %convert_element_type.159), channel_id=1, source_target_pairs={{0,448},{4,452},{8,456},{12,460},{16,464},{20,468},{24,472},{28,47... | collective-permute-start | bytes 2064392 | tf_op jit(solution)/shard_map/while/body/eval_jaxpr/ppermute | solution.py:12
  546.3 33.2 %collective-permute-start.4 = (bf16[14,8192]{1,0:T(8,128)(2,1)S(1)}, bf16[14,8192]{1,0:T(8,128)(2,1)S(1)}, u32[]{:S(2)}, u32[]{:S(2)}) collective-permute-start(bf16[14,8192]{1,0:T(8,128)(2,1)S(1)} %get-tuple-element.654), channel_id=1, source_target_pairs={{1,0},{2,1},{3,2},{4,3},{5,4},{6,5},{7,6},{8,7},{9,8},{10,9},{11,1... | collective-permute-start | bytes 688136 | tf_op jit(solution)/shard_map/while/body/eval_jaxpr/ppermute | solution.py:23
  565.7 13.9 %collective-permute-start.5 = (bf16[14,8192]{1,0:T(8,128)(2,1)S(1)}, bf16[14,8192]{1,0:T(8,128)(2,1)S(1)}, u32[]{:S(2)}, u32[]{:S(2)}) collective-permute-start(bf16[14,8192]{1,0:T(8,128)(2,1)S(1)} %get-tuple-element.655), channel_id=1, source_target_pairs={{0,1},{1,2},{2,3},{3,4},{4,5},{5,6},{6,7},{7,8},{8,9},{9,10},{10,1... | collective-permute-start | bytes 688136 | tf_op jit(solution)/shard_map/while/body/eval_jaxpr/ppermute | solution.py:22
  586.2 17.1 %collective-permute-start.3 = (bf16[42,8192]{1,0:T(8,128)(2,1)S(1)}, bf16[42,8192]{1,0:T(8,128)(2,1)S(1)}, u32[]{:S(2)}, u32[]{:S(2)}) collective-permute-start(bf16[42,8192]{1,0:T(8,128)(2,1)S(1)} %convert_element_type.159), channel_id=1, source_target_pairs={{0,448},{4,452},{8,456},{12,460},{16,464},{20,468},{24,472},{28,47... | collective-permute-start | bytes 2064392 | tf_op jit(solution)/shard_map/while/body/eval_jaxpr/ppermute | solution.py:12
  603.3 32.6 %collective-permute-start.4 = (bf16[14,8192]{1,0:T(8,128)(2,1)S(1)}, bf16[14,8192]{1,0:T(8,128)(2,1)S(1)}, u32[]{:S(2)}, u32[]{:S(2)}) collective-permute-start(bf16[14,8192]{1,0:T(8,128)(2,1)S(1)} %get-tuple-element.654), channel_id=1, source_target_pairs={{1,0},{2,1},{3,2},{4,3},{5,4},{6,5},{7,6},{8,7},{9,8},{10,9},{11,1... | collective-permute-start | bytes 688136 | tf_op jit(solution)/shard_map/while/body/eval_jaxpr/ppermute | solution.py:23
  625.6 13.1 %collective-permute-start.5 = (bf16[14,8192]{1,0:T(8,128)(2,1)S(1)}, bf16[14,8192]{1,0:T(8,128)(2,1)S(1)}, u32[]{:S(2)}, u32[]{:S(2)}) collective-permute-start(bf16[14,8192]{1,0:T(8,128)(2,1)S(1)} %get-tuple-element.655), channel_id=1, source_target_pairs={{0,1},{1,2},{2,3},{3,4},{4,5},{5,6},{6,7},{7,8},{8,9},{9,10},{10,1... | collective-permute-start | bytes 688136 | tf_op jit(solution)/shard_map/while/body/eval_jaxpr/ppermute | solution.py:22
  645.4 22.6 %collective-permute-start.3 = (bf16[42,8192]{1,0:T(8,128)(2,1)S(1)}, bf16[42,8192]{1,0:T(8,128)(2,1)S(1)}, u32[]{:S(2)}, u32[]{:S(2)}) collective-permute-start(bf16[42,8192]{1,0:T(8,128)(2,1)S(1)} %convert_element_type.159), channel_id=1, source_target_pairs={{0,448},{4,452},{8,456},{12,460},{16,464},{20,468},{24,472},{28,47... | collective-permute-start | bytes 2064392 | tf_op jit(solution)/shard_map/while/body/eval_jaxpr/ppermute | solution.py:12
  668.2 23.8 %collective-permute-start.4 = (bf16[14,8192]{1,0:T(8,128)(2,1)S(1)}, bf16[14,8192]{1,0:T(8,128)(2,1)S(1)}, u32[]{:S(2)}, u32[]{:S(2)}) collective-permute-start(bf16[14,8192]{1,0:T(8,128)(2,1)S(1)} %get-tuple-element.654), channel_id=1, source_target_pairs={{1,0},{2,1},{3,2},{4,3},{5,4},{6,5},{7,6},{8,7},{9,8},{10,9},{11,1... | collective-permute-start | bytes 688136 | tf_op jit(solution)/shard_map/while/body/eval_jaxpr/ppermute | solution.py:23
  684.3 13.1 %collective-permute-start.5 = (bf16[14,8192]{1,0:T(8,128)(2,1)S(1)}, bf16[14,8192]{1,0:T(8,128)(2,1)S(1)}, u32[]{:S(2)}, u32[]{:S(2)}) collective-permute-start(bf16[14,8192]{1,0:T(8,128)(2,1)S(1)} %get-tuple-element.655), channel_id=1, source_target_pairs={{0,1},{1,2},{2,3},{3,4},{4,5},{5,6},{6,7},{7,8},{8,9},{9,10},{10,1... | collective-permute-start | bytes 688136 | tf_op jit(solution)/shard_map/while/body/eval_jaxpr/ppermute | solution.py:22
  704.1 20.7 %collective-permute-start.3 = (bf16[42,8192]{1,0:T(8,128)(2,1)S(1)}, bf16[42,8192]{1,0:T(8,128)(2,1)S(1)}, u32[]{:S(2)}, u32[]{:S(2)}) collective-permute-start(bf16[42,8192]{1,0:T(8,128)(2,1)S(1)} %convert_element_type.159), channel_id=1, source_target_pairs={{0,448},{4,452},{8,456},{12,460},{16,464},{20,468},{24,472},{28,47... | collective-permute-start | bytes 2064392 | tf_op jit(solution)/shard_map/while/body/eval_jaxpr/ppermute | solution.py:12
  724.9 21.1 %collective-permute-start.4 = (bf16[14,8192]{1,0:T(8,128)(2,1)S(1)}, bf16[14,8192]{1,0:T(8,128)(2,1)S(1)}, u32[]{:S(2)}, u32[]{:S(2)}) collective-permute-start(bf16[14,8192]{1,0:T(8,128)(2,1)S(1)} %get-tuple-element.654), channel_id=1, source_target_pairs={{1,0},{2,1},{3,2},{4,3},{5,4},{6,5},{7,6},{8,7},{9,8},{10,9},{11,1... | collective-permute-start | bytes 688136 | tf_op jit(solution)/shard_map/while/body/eval_jaxpr/ppermute | solution.py:23
  742.2 13.1 %collective-permute-start.5 = (bf16[14,8192]{1,0:T(8,128)(2,1)S(1)}, bf16[14,8192]{1,0:T(8,128)(2,1)S(1)}, u32[]{:S(2)}, u32[]{:S(2)}) collective-permute-start(bf16[14,8192]{1,0:T(8,128)(2,1)S(1)} %get-tuple-element.655), channel_id=1, source_target_pairs={{0,1},{1,2},{2,3},{3,4},{4,5},{5,6},{6,7},{7,8},{8,9},{9,10},{10,1... | collective-permute-start | bytes 688136 | tf_op jit(solution)/shard_map/while/body/eval_jaxpr/ppermute | solution.py:22
  (57 other events, 481.0 us)
where the time goes:
time: 760 us; the launch traced here: 758 us
  waiting for transfers between devices  391 us (51%)
  starting transfers between devices  263 us (35%)
  local copies, waits for them, and re-layouts  42 us (6%)
  matrix products  29.7 us (4%)
  other arithmetic  29.4 us (4%)
    ppermute x16, waiting for transfers between devices, from_behind(): return lax.ppermute(value, axis, pairs)  221 us
    ppermute x16, starting transfers between devices, padded_2(): after = lax.ppermute(leading, axis, down)  175 us
    ppermute x16, waiting for transfers between devices, padded_2(): before = lax.ppermute(last, axis, up)  101 us
    ppermute x16, waiting for transfers between devices, padded_2(): after = lax.ppermute(leading, axis, down)  69 us
    ppermute x16, starting transfers between devices, from_behind(): return lax.ppermute(value, axis, pairs)  51.9 us
    ppermute x16, starting transfers between devices, padded_2(): before = lax.ppermute(last, axis, up)  35.5 us
    while x192, local copies, waits for them, and re-layouts  28.6 us
    scatter-add x8, other arithmetic, incoming_sum(): jax.ops.segment_sum(flat_terms, pattern.reshape(-1), num_segments=3 * slo...  20.3 us
  transfers between devices with their start and end apart: 48, of which 45 were waited for; matrix products, arithmetic and copies ran while one was open for 1% of the time, Pallas kernels for 0%

commit v1 on v0

v1 whole, which is shorter than its diff:
```python
import functools

import jax
import jax.numpy as jnp
from jax import lax
from jax.experimental import pallas as pl
from jax.experimental.pallas import tpu as pltpu
from jax.sharding import PartitionSpec as P

LEVELS = 8
RANKS = 64
SLOTS = 14
PAIRS = 7
LINKS = 3
ORDER = 64
COLS = 128
PART = 16
ROTATION = 96
W_ROWS = SLOTS * ORDER
W_ALL = W_ROWS + 16
AXES = ("lvl", "row")
BF16 = jnp.bfloat16
F32 = jnp.float32
VMEM = pltpu.VMEM


def place(rank, slot):
    plane, side = divmod(rank, 4)
    y = side if plane % 2 == 0 else 3 - side
    return (plane * 8 + slot) * 4 + y


def gather_pairs():
    pairs = []
    for device in range(LEVELS * RANKS):
        level, rank = divmod((device + ROTATION) % (LEVELS * RANKS), RANKS)
        pairs.append((device, place(rank, level)))
    return pairs


def neighbour_pairs(step):
    return [
        (place(rank, slot), place(rank + step, slot))
        for rank in range(RANKS)
        if 0 <= rank + step < RANKS
        for slot in range(LEVELS)
    ]


def group_list():
    return [[plane * 8 + slot for slot in range(8)] for plane in range(16)]


def left_lanes(shape):
    return lax.broadcasted_iota(jnp.int32, shape, len(shape) - 1) < ORDER


def call(kernel, outs, operands, in_specs, scratch=(), flops=0):
    return pl.pallas_call(
        kernel,
        out_shape=[jax.ShapeDtypeStruct(shape, dtype) for shape, dtype in outs],
        grid=(1,),
        in_specs=in_specs,
        out_specs=[
            pl.BlockSpec(shape, functools.partial(lambda n, i: (0,) * n, len(shape)))
            for shape, _ in outs
        ],
        scratch_shapes=list(scratch),
        compiler_params=pltpu.CompilerParams(vmem_limit_bytes=32 * 1024 * 1024),
    )(*operands)


def whole(array):
    return pl.BlockSpec(array.shape, lambda i: (0,) * array.ndim)


def at_level(level, rows, width):
    return pl.BlockSpec((1, rows, width), lambda i: (level, 0, 0))


def prepare_kernel(first_ref, rhs_ref, factor_ref, diag_ref, pattern_ref, w_ref, rhs_t_ref):
    first = first_ref[0] == 1
    for i in range(PAIRS):
        halves = []
        for n, side in ((i, 0), (i + PAIRS, 1)):
            blocks = [factor_ref[n, m] for m in range(LINKS)]
            diag = diag_ref[n]
            tail = [diag, blocks[2]] if side == 0 else [blocks[2], diag]
            w_ref[n * ORDER : (n + 1) * ORDER, :] = jnp.concatenate(blocks[:2] + tail, axis=1)
            rhs = rhs_ref[n]
            solved = jnp.dot(diag, rhs, preferred_element_type=F32).astype(BF16)
            halves.append(jnp.where(first, solved, rhs))
        both = jnp.concatenate(halves, axis=0).astype(F32)
        turned = both.T.astype(BF16)
        for j in range(COLS // PART):
            rhs_t_ref[j, i] = turned[j * PART : (j + 1) * PART, :]
    w_ref[W_ROWS:, :] = pattern_ref[...]


def finish_kernel(parts_ref, out_ref):
    for i in range(PAIRS):
        columns = jnp.concatenate([parts_ref[j, i] for j in range(COLS // PART)], axis=0)
        turned = columns.astype(F32).T.astype(BF16)
        out_ref[i] = turned[:ORDER]
        out_ref[i + PAIRS] = turned[ORDER:]


def put_window(window_ref, source_ref, base):
    for i in range(PAIRS):
        pair = source_ref[i].astype(F32)
        swapped = pltpu.roll(pair, ORDER, 1)
        left = left_lanes(pair.shape)
        window_ref[base + i] = jnp.where(left, pair, swapped).astype(BF16)
        window_ref[base + PAIRS + i] = jnp.where(left, swapped, pair).astype(BF16)


def diag_pair(w_ref, i):
    upper = w_ref[0, i * ORDER : (i + 1) * ORDER, 128:]
    j = i + PAIRS
    lower = w_ref[0, j * ORDER : (j + 1) * ORDER, 128:]
    left = left_lanes(upper.shape)
    zero = jnp.zeros_like(upper)
    return jnp.concatenate([jnp.where(left, upper, zero), jnp.where(left, zero, lower)], axis=0)


def picked_product(pattern_ref, w_ref, window_ref, level, n):
    p = [pattern_ref[level, LINKS * n + m] for m in range(LINKS)]
    a, b, c = (window_ref[index] for index in p)
    left = left_lanes(a.shape)
    zero = jnp.zeros_like(c)
    head = jnp.where(left, a, b)
    tail = jnp.where(left, zero, c) if n < PAIRS else jnp.where(left, c, zero)
    w = w_ref[0, n * ORDER : (n + 1) * ORDER, :]
    return lax.dot_general(
        jnp.concatenate([head, tail], axis=1), w, (((1,), (1,)), ((), ())), preferred_element_type=F32
    )


def forward_pair(pattern_ref, w_ref, window_ref, rhs_ref, level, i):
    coupled = jnp.concatenate(
        [picked_product(pattern_ref, w_ref, window_ref, level, n) for n in (i, i + PAIRS)], axis=1
    )
    reduced = (rhs_ref[0, i].astype(F32) - coupled).astype(BF16)
    return lax.dot_general(
        reduced, diag_pair(w_ref, i), (((1,), (1,)), ((), ())), preferred_element_type=F32
    ).astype(BF16)


def fill_window(window_ref, own_ref, below_ref, above_ref):
    put_window(window_ref, below_ref, 0)
    put_window(window_ref, own_ref, SLOTS)
    put_window(window_ref, above_ref, 2 * SLOTS)


def forward_kernel(level, pattern_ref, w_ref, rhs_ref, own_ref, below_ref, above_ref, out_ref, window_ref):
    fill_window(window_ref, own_ref, below_ref, above_ref)
    for i in range(PAIRS):
        out_ref[i] = forward_pair(pattern_ref, w_ref, window_ref, rhs_ref, level, i)


def spread(pattern_ref, w_ref, solved, level, sums_ref, total_ref):
    for q in range(LINKS * SLOTS):
        total_ref[q] = jnp.zeros(total_ref.shape[1:], F32)
    for i in range(PAIRS):
        j = i + PAIRS
        left = left_lanes(solved[i].shape)
        zero = jnp.zeros_like(solved[i])
        rows = jnp.concatenate(
            [jnp.where(left, solved[i], zero), jnp.where(left, zero, solved[i])], axis=0
        )
        w = jnp.concatenate(
            [w_ref[0, n * ORDER : (n + 1) * ORDER, :] for n in (i, j)], axis=0
        )
        products = jnp.dot(rows, w, preferred_element_type=F32)
        for n, product in ((i, products[:PART]), (j, products[PART:])):
            head, tail = product[:, :128], product[:, 128:]
            left = left_lanes(head.shape)
            zero = jnp.zeros_like(head)
            terms = (
                jnp.where(left, head, zero),
                jnp.where(left, zero, head),
                jnp.where(left, zero, tail) if n < PAIRS else jnp.where(left, tail, zero),
            )
            for m in range(LINKS):
                q = pattern_ref[level, LINKS * n + m]
                total_ref[q] += terms[m]
    for part in range(LINKS):
        for i in range(PAIRS):
            one = total_ref[part * SLOTS + i]
            two = total_ref[part * SLOTS + PAIRS + i]
            left = left_lanes(one.shape)
            one = one + pltpu.roll(one, ORDER, 1)
            two = two + pltpu.roll(two, ORDER, 1)
            sums_ref[part, i] = jnp.where(left, one, two).astype(BF16)


def backward_pair(w_ref, reduced, i):
    return jnp.dot(reduced, diag_pair(w_ref, i), preferred_element_type=F32).astype(BF16)


def turn_kernel(
    level, pattern_ref, w_ref, rhs_ref, own_ref, below_ref, above_ref,
    out_ref, back_ref, sums_ref, window_ref, total_ref,
):
    fill_window(window_ref, own_ref, below_ref, above_ref)
    solved = []
    for i in range(PAIRS):
        forward = forward_pair(pattern_ref, w_ref, window_ref, rhs_ref, level, i)
        out_ref[i] = forward
        back = backward_pair(w_ref, forward, i)
        back_ref[i] = back
        solved.append(back)
    spread(pattern_ref, w_ref, solved, level, sums_ref, total_ref)


def backward_solve(w_ref, forward_ref, own_ref, below_ref, above_ref, back_ref):
    solved = []
    for i in range(PAIRS):
        incoming = (
            own_ref[1, i].astype(F32) + below_ref[i].astype(F32) + above_ref[i].astype(F32)
        )
        reduced = (forward_ref[i].astype(F32) - incoming).astype(BF16)
        back = backward_pair(w_ref, reduced, i)
        back_ref[i] = back
        solved.append(back)
    return solved


def backward_kernel(
    level, pattern_ref, w_ref, forward_ref, own_ref, below_ref, above_ref, back_ref, sums_ref, total_ref
):
    solved = backward_solve(w_ref, forward_ref, own_ref, below_ref, above_ref, back_ref)
    spread(pattern_ref, w_ref, solved, level, sums_ref, total_ref)


def last_kernel(w_ref, forward_ref, own_ref, below_ref, above_ref, back_ref):
    backward_solve(w_ref, forward_ref, own_ref, below_ref, above_ref, back_ref)


def per_device(right_side, factor_blocks, diag_inverse, pattern):
    to_group = gather_pairs()
    to_native = [(b, a) for a, b in to_group]
    up, down = neighbour_pairs(1), neighbour_pairs(-1)
    groups = group_list()
    smem = pl.BlockSpec(memory_space=pltpu.SMEM)
    solved_shape = ((PAIRS, PART, 128), BF16)
    window = VMEM((LINKS * SLOTS, PART, 128), BF16)
    total = VMEM((LINKS * SLOTS, PART, 128), F32)

    device = lax.axis_index("lvl") * 4 + lax.axis_index("row")
    own_level = (device + ROTATION) % (LEVELS * RANKS) // RANKS
    first = (own_level == 0).astype(jnp.int32).reshape(1)
    entries = jnp.clip(pattern, 0, LINKS * SLOTS - 1).astype(BF16).reshape(1, LINKS * SLOTS)
    entries = jnp.pad(entries, ((0, 15), (0, 256 - LINKS * SLOTS)))

    factors, rhs = call(
        prepare_kernel,
        [((W_ALL, 256), BF16), ((COLS // PART, PAIRS, PART, 128), BF16)],
        (first, right_side, factor_blocks, diag_inverse, entries),
        [smem, whole(right_side), whole(factor_blocks), whole(diag_inverse), whole(entries)],
    )
    factors = lax.ppermute(factors, AXES, to_group)
    rhs = lax.ppermute(rhs, AXES, to_group)
    factors = lax.all_gather(factors, "lvl", axis_index_groups=groups)
    rhs = lax.all_to_all(rhs, "lvl", 0, 0, axis_index_groups=groups)
    patterns = factors[:, W_ROWS, : LINKS * SLOTS].astype(jnp.int32)

    def exchange(to_above, to_below):
        return lax.ppermute(to_above, AXES, up), lax.ppermute(to_below, AXES, down)

    small = pl.BlockSpec((PAIRS, PART, 128), lambda i: (0, 0, 0))
    sums_spec = pl.BlockSpec((LINKS, PAIRS, PART, 128), lambda i: (0, 0, 0, 0))
    sums_shape = ((LINKS, PAIRS, PART, 128), BF16)

    def rhs_spec(level):
        return pl.BlockSpec((1, PAIRS, PART, 128), lambda i: (level, 0, 0, 0))

    latest = rhs[0]
    forward = [latest]
    for level in range(1, LEVELS - 1):
        below, above = exchange(latest, latest)
        (latest,) = call(
            functools.partial(forward_kernel, level),
            [solved_shape],
            (patterns, factors, rhs, latest, below, above),
            [smem, at_level(level, W_ALL, 256), rhs_spec(level), small, small, small],
            [window],
        )
        forward.append(latest)
    below, above = exchange(latest, latest)
    level = LEVELS - 1
    latest, back, sums = call(
        functools.partial(turn_kernel, level),
        [solved_shape, solved_shape, sums_shape],
        (patterns, factors, rhs, latest, below, above),
        [smem, at_level(level, W_ALL, 256), rhs_spec(level), small, small, small],
        [window, total],
    )
    forward.append(latest)
    backward = [back]
    for level in range(LEVELS - 2, 0, -1):
        below, above = exchange(sums[2], sums[0])
        back, sums = call(
            functools.partial(backward_kernel, level),
            [solved_shape, sums_shape],
            (patterns, factors, forward[level], sums, below, above),
            [smem, at_level(level, W_ALL, 256), small, sums_spec, small, small],
            [total],
        )
        backward.append(back)
    below, above = exchange(sums[2], sums[0])
    (back,) = call(
        last_kernel,
        [solved_shape],
        (factors, forward[0], sums, below, above),
        [at_level(0, W_ALL, 256), small, sums_spec, small, small],
    )
    backward.append(back)

    def to_output(levels):
        parts = lax.all_to_all(jnp.stack(levels), "lvl", 0, 0, axis_index_groups=groups)
        parts = lax.ppermute(parts, AXES, to_native)
        (out,) = call(
            finish_kernel, [((SLOTS, ORDER, COLS), BF16)], (parts,), [whole(parts)]
        )
        return out

    return to_output(forward), to_output(backward[::-1])


def solution(mesh):
    return jax.shard_map(
        per_device,
        mesh=mesh,
        in_specs=(
            P(AXES, None, None),
            P(AXES, None, None, None),
            P(AXES, None, None),
            P(AXES, None),
        ),
        out_specs=(P(AXES, None, None), P(AXES, None, None)),
        check_vma=False,
    )
```

time: 760 us -> 341 us (0.45)
  the two profiles are of different devices: /device:TPU:384 before, /device:TPU:37 now
where the time goes in v1:
time: 341 us; the launch traced here: 339 us
  starting transfers between devices  141 us (41%)
  waiting for transfers between devices  123 us (36%)
  blocking collectives  22 us (6%)
  Pallas kernels  19.3 us (6%)
  local copies, waits for them, and re-layouts  17.9 us (5%)
  between operations  14.6 us (4%)
    ppermute x2, waiting for transfers between devices, to_output(): parts = lax.ppermute(parts, AXES, to_native)  53 us
    ppermute x14, starting transfers between devices, exchange(): lax.ppermute(to_above, AXES, up)  42.2 us
    ppermute x14, starting transfers between devices, exchange(): lax.ppermute(to_below, AXES, down)  32.6 us
    ppermute x1, waiting for transfers between devices, per_device(): factors = lax.ppermute(factors, AXES, to_group)  27.4 us
    all_to_all x2, starting transfers between devices, to_output(): lax.all_to_all(jnp.stack(levels), 'lvl', 0, 0, axis_index_groups=groups)  27.1 us
    ppermute x14, waiting for transfers between devices, exchange(): lax.ppermute(to_below, AXES, down)  25.5 us
    all_to_all x1, blocking collectives, per_device(): rhs = lax.all_to_all(rhs, 'lvl', 0, 0, axis_index_groups=groups)  22 us
    pallas_call x17, Pallas kernels, call(): pl.pallas_call(kernel, out_shape=[jax.ShapeDtypeStruct(shape, dtype) for...  19.3 us
  transfers between devices with their start and end apart: 35, of which 17 were waited for; matrix products, arithmetic and copies ran while one was open for 3% of the time, Pallas kernels for 0%

profile of v1, /device:TPU:37, one launch (start us, length us, event | category | flops | bytes accessed | tf_op | source)
XLA Modules:
  0.0 339.1 jit_solution(5098446483386032718)
XLA Ops:
  11.5 11.8 %collective-permute-start.1 = (bf16[912,256]{1,0:T(8,128)(2,1)S(1)}, bf16[912,256]{1,0:T(8,128)(2,1)S(1)}, u32[]{:S(2)}, u32[]{:S(2)}) collective-permute-start(bf16[912,256]{1,0:T(8,128)(2,1)S(1)} %get-tuple-element.20), channel_id=1, source_target_pairs={{0,260},{1,261},{2,262},{3,263},{4,295},{5,294},{6,293},{7,292},{8... | collective-permute-start | bytes 1400840 | tf_op jit(solution)/shard_map/ppermute | solution.py:262
  23.3 27.4 %collective-permute-done.1 = bf16[912,256]{1,0:T(8,128)(2,1)S(1)} collective-permute-done((bf16[912,256]{1,0:T(8,128)(2,1)S(1)}, bf16[912,256]{1,0:T(8,128)(2,1)S(1)}, u32[]{:S(2)}, u32[]{:S(2)}) %collective-permute-start.1) | collective-permute-done | bytes 466976 | tf_op jit(solution)/shard_map/ppermute | solution.py:262
  51.5 11.5 %collective-permute-start = (bf16[8,7,16,128]{3,2,1,0:T(8,128)(2,1)S(1)}, bf16[8,7,16,128]{3,2,1,0:T(8,128)(2,1)S(1)}, u32[]{:S(2)}, u32[]{:S(2)}) collective-permute-start(bf16[8,7,16,128]{3,2,1,0:T(8,128)(2,1)S(1)} %get-tuple-element.19), channel_id=1, source_target_pairs={{0,260},{1,261},{2,262},{3,263},{4,295},{5,294},{6,293},{7,292},{8... | collective-permute-start | bytes 688136 | tf_op jit(solution)/shard_map/ppermute | solution.py:263
  62.9 7.4 %collective-permute-done = bf16[8,7,16,128]{3,2,1,0:T(8,128)(2,1)S(1)} collective-permute-done((bf16[8,7,16,128]{3,2,1,0:T(8,128)(2,1)S(1)}, bf16[8,7,16,128]{3,2,1,0:T(8,128)(2,1)S(1)}, u32[]{:S(2)}, u32[]{:S(2)}) %collective-permute-start) | collective-permute-done | bytes 229408 | tf_op jit(solution)/shard_map/ppermute | solution.py:263
  70.4 22.0 %all_to_all.15.rhs_ref = bf16[8,7,16,128]{3,2,1,0:T(8,128)(2,1)S(1)} all-to-all(bf16[8,7,16,128]{3,2,1,0:T(8,128)(2,1)S(1)} %collective-permute-done), channel_id=1, replica_groups={{0,4,8,12,16,20,24,28},{32,36,40,44,48,52,56,60},{64,68,72,76,80,84,88,..., dimensions={0} | all-to-all | bytes 458752 | tf_op jit(solution)/shard_map/all_to_all | solution.py:265
  94.9 3.4 collective-permute-start.3
  98.3 9.2 %all-gather.3.cloned.1.call-done = bf16[7296,256]{1,0:T(8,128)(2,1)} async-done(((bf16[912,256]{1,0:T(8,128)(2,1)}), bf16[7296,256]{1,0:T(8,128)(2,1)}) %all-gather.3.cloned.1.call-update) | async-done | bytes 3735568 | tf_op jit(solution)/shard_map/all_gather | solution.py:264
  108.3 2.0 copy-done
  111.5 1.9 collective-permute-start.4
  113.4 3.4 collective-permute-start.5
  119.3 2.4 collective-permute-start.6
  121.6 2.9 collective-permute-start.7
  127.5 3.1 collective-permute-start.8
  130.6 2.2 collective-permute-start.9
  132.8 2.4 collective-permute-done.9.above_ref
  136.4 2.8 collective-permute-start.10
  139.3 2.5 collective-permute-start.11
  141.7 2.1 collective-permute-done.11.above_ref
  145.1 3.7 %collective-permute-start.12 = (bf16[7,16,128]{2,1,0:T(8,128)(2,1)S(1)}, bf16[7,16,128]{2,1,0:T(8,128)(2,1)S(1)}, u32[]{:S(2)}, u32[]{:S(2)}) collective-permute-start(bf16[7,16,128]{2,1,0:T(8,128)(2,1)S(1)} %shard_map.64.own_ref.forward_ref), channel_id=1, source_target_pairs={{0,1},{4,5},{8,9},{12,13},{16,17},{20,21},{24,25},{28,29},{1,2},{5... | collective-permute-start | bytes 86024 | tf_op jit(solution)/shard_map/ppermute | solution.py:269
  148.8 1.9 collective-permute-start.13
  150.7 3.9 %collective-permute-done.13.above_ref = bf16[7,16,128]{2,1,0:T(8,128)(2,1)S(1)} collective-permute-done((bf16[7,16,128]{2,1,0:T(8,128)(2,1)S(1)}, bf16[7,16,128]{2,1,0:T(8,128)(2,1)S(1)}, u32[]{:S(2)}, u32[]{:S(2)}) %collective-permute-start.13) | collective-permute-done | bytes 28704 | tf_op jit(solution)/shard_map/ppermute | solution.py:269
  155.8 3.4 collective-permute-start.14
  159.2 1.9 collective-permute-start.15
  161.1 2.7 collective-permute-done.15.above_ref
  163.8 2.9 shard_map.66
  166.8 3.3 collective-permute-start.17
  170.1 2.0 collective-permute-start.18
  172.7 2.0 collective-permute-done.18.above_ref
  175.9 3.4 collective-permute-start.19
  179.3 1.9 collective-permute-start.20
  181.8 2.1 collective-permute-done.20.above_ref
  185.1 3.8 %collective-permute-start.21 = (bf16[7,16,128]{2,1,0:T(8,128)(2,1)S(1)}, bf16[7,16,128]{2,1,0:T(8,128)(2,1)S(1)}, u32[]{:S(2)}, u32[]{:S(2)}) collective-permute-start(bf16[7,16,128]{2,1,0:T(8,128)(2,1)S(1)} %get-tuple-element.47), channel_id=1, source_target_pairs={{0,1},{4,5},{8,9},{12,13},{16,17},{20,21},{24,25},{28,29},{1,2},{5... | collective-permute-start | bytes 86024 | tf_op jit(solution)/shard_map/ppermute | solution.py:269
  191.4 2.1 collective-permute-done.22.above_ref
  194.6 2.5 collective-permute-start.23
  197.1 2.8 collective-permute-start.24
  203.0 3.4 %collective-permute-start.25 = (bf16[7,16,128]{2,1,0:T(8,128)(2,1)S(1)}, bf16[7,16,128]{2,1,0:T(8,128)(2,1)S(1)}, u32[]{:S(2)}, u32[]{:S(2)}) collective-permute-start(bf16[7,16,128]{2,1,0:T(8,128)(2,1)S(1)} %get-tuple-element.43), channel_id=1, source_target_pairs={{0,1},{4,5},{8,9},{12,13},{16,17},{20,21},{24,25},{28,29},{1,2},{5... | collective-permute-start | bytes 86024 | tf_op jit(solution)/shard_map/ppermute | solution.py:269
  209.0 2.1 collective-permute-done.26.above_ref
  212.2 3.2 collective-permute-start.27
  215.5 2.1 collective-permute-start.28
  218.2 1.9 collective-permute-done.28.above_ref
  221.3 3.4 collective-permute-start.29
  227.2 22.3 %all-to-all-start.1 = ((bf16[8,7,16,128]{3,2,1,0:T(8,128)(2,1)}), bf16[8,7,16,128]{3,2,1,0:T(8,128)(2,1)S(1)}, u32[]{:S(2)}, u32[]{:S(2)}) async-start(bf16[8,7,16,128]{3,2,1,0:T(8,128)(2,1)} %constant_dynamic-update-slice_fusion), calls=%async_computation.1 | async-start | bytes 458752 | tf_op jit(solution)/shard_map/all_to_all | solution.py:321
  249.5 2.0 copy-done.1
  256.6 4.8 %all-to-all-start.2 = ((bf16[8,7,16,128]{3,2,1,0:T(8,128)(2,1)}), bf16[8,7,16,128]{3,2,1,0:T(8,128)(2,1)S(1)}, u32[]{:S(2)}, u32[]{:S(2)}) async-start(bf16[8,7,16,128]{3,2,1,0:T(8,128)(2,1)} %constant_dynamic-update-slice_fusion.8), calls=%async_computation.2 | async-start | bytes 458752 | tf_op jit(solution)/shard_map/all_to_all | solution.py:321
  261.4 9.9 %collective-permute-start.16 = (bf16[8,7,16,128]{3,2,1,0:T(8,128)(2,1)S(1)}, bf16[8,7,16,128]{3,2,1,0:T(8,128)(2,1)S(1)}, u32[]{:S(2)}, u32[]{:S(2)}) collective-permute-start(bf16[8,7,16,128]{3,2,1,0:T(8,128)(2,1)S(1)} %all-to-all-done.1), channel_id=1, source_target_pairs={{260,0},{261,1},{262,2},{263,3},{295,4},{294,5},{293,6},{292,7},{3... | collective-permute-start | bytes 688136 | tf_op jit(solution)/shard_map/ppermute | solution.py:322
  271.4 6.2 %collective-permute-start.31 = (bf16[8,7,16,128]{3,2,1,0:T(8,128)(2,1)S(1)}, bf16[8,7,16,128]{3,2,1,0:T(8,128)(2,1)S(1)}, u32[]{:S(2)}, u32[]{:S(2)}) collective-permute-start(bf16[8,7,16,128]{3,2,1,0:T(8,128)(2,1)S(1)} %all-to-all-done.2), channel_id=1, source_target_pairs={{260,0},{261,1},{262,2},{263,3},{295,4},{294,5},{293,6},{292,7},{3... | collective-permute-start | bytes 688136 | tf_op jit(solution)/shard_map/ppermute | solution.py:322
  277.5 48.9 %collective-permute-done.16.parts_ref = bf16[8,7,16,128]{3,2,1,0:T(8,128)(2,1)S(1)} collective-permute-done((bf16[8,7,16,128]{3,2,1,0:T(8,128)(2,1)S(1)}, bf16[8,7,16,128]{3,2,1,0:T(8,128)(2,1)S(1)}, u32[]{:S(2)}, u32[]{:S(2)}) %collective-permute-start.16) | collective-permute-done | bytes 229408 | tf_op jit(solution)/shard_map/ppermute | solution.py:322
  327.3 4.1 %collective-permute-done.31.parts_ref = bf16[8,7,16,128]{3,2,1,0:T(8,128)(2,1)S(1)} collective-permute-done((bf16[8,7,16,128]{3,2,1,0:T(8,128)(2,1)S(1)}, bf16[8,7,16,128]{3,2,1,0:T(8,128)(2,1)S(1)}, u32[]{:S(2)}, u32[]{:S(2)}) %collective-permute-start.31) | collective-permute-done | bytes 229408 | tf_op jit(solution)/shard_map/ppermute | solution.py:322
  (81 shorter events, 43.6 us)
Async XLA Ops:
  7.2 100.3 %all-gather.3.cloned.1.call-start = ((), (), s32[]{:S(2)}) async-start(), calls=%async_computation.3 | async-start | bytes 4202496 | tf_op jit(solution)/shard_map/all_gather | solution.py:264
  8.2 1.1 copy-start.2
  9.3 0.9 copy-start.3
  10.2 0.9 copy-start.4
  11.5 39.2 %collective-permute-start.1 = (bf16[912,256]{1,0:T(8,128)(2,1)S(1)}, bf16[912,256]{1,0:T(8,128)(2,1)S(1)}, u32[]{:S(2)}, u32[]{:S(2)}) collective-permute-start(bf16[912,256]{1,0:T(8,128)(2,1)S(1)} %get-tuple-element.20), channel_id=1, source_target_pairs={{0,260},{1,261},{2,262},{3,263},{4,295},{5,294},{6,293},{7,292},{8... | collective-permute-start | bytes 1400840 | tf_op jit(solution)/shard_map/ppermute | solution.py:262
  50.6 0.8 copy-start.5
  51.5 18.9 %collective-permute-start = (bf16[8,7,16,128]{3,2,1,0:T(8,128)(2,1)S(1)}, bf16[8,7,16,128]{3,2,1,0:T(8,128)(2,1)S(1)}, u32[]{:S(2)}, u32[]{:S(2)}) collective-permute-start(bf16[8,7,16,128]{3,2,1,0:T(8,128)(2,1)S(1)} %get-tuple-element.19), channel_id=1, source_target_pairs={{0,260},{1,261},{2,262},{3,263},{4,295},{5,294},{6,293},{7,292},{8... | collective-permute-start | bytes 688136 | tf_op jit(solution)/shard_map/ppermute | solution.py:263
  93.0 15.2 %collective-permute-start.2 = (bf16[7,16,128]{2,1,0:T(8,128)(2,1)S(1)}, bf16[7,16,128]{2,1,0:T(8,128)(2,1)S(1)}, u32[]{:S(2)}, u32[]{:S(2)}) collective-permute-start(bf16[7,16,128]{2,1,0:T(8,128)(2,1)S(1)} %get-tuple-element.36.own_ref.forward_ref), channel_id=1, source_target_pairs={{0,1},{4,5},{8,9},{12,13},{16,17},{20,21},{24,25},{28,29},{1,2},{5... | collective-permute-start | bytes 86024 | tf_op jit(solution)/shard_map/ppermute | solution.py:269
  94.9 13.3 %collective-permute-start.3 = (bf16[7,16,128]{2,1,0:T(8,128)(2,1)S(1)}, bf16[7,16,128]{2,1,0:T(8,128)(2,1)S(1)}, u32[]{:S(2)}, u32[]{:S(2)}) collective-permute-start(bf16[7,16,128]{2,1,0:T(8,128)(2,1)S(1)} %get-tuple-element.36.own_ref.forward_ref), channel_id=1, source_target_pairs={{1,0},{5,4},{9,8},{13,12},{17,16},{21,20},{25,24},{29,28},{2,1},{6... | collective-permute-start | bytes 86024 | tf_op jit(solution)/shard_map/ppermute | solution.py:269
  108.2 2.1 copy-start
  111.5 5.3 %collective-permute-start.4 = (bf16[7,16,128]{2,1,0:T(8,128)(2,1)S(1)}, bf16[7,16,128]{2,1,0:T(8,128)(2,1)S(1)}, u32[]{:S(2)}, u32[]{:S(2)}) collective-permute-start(bf16[7,16,128]{2,1,0:T(8,128)(2,1)S(1)} %shard_map.60.own_ref.forward_ref), channel_id=1, source_target_pairs={{0,1},{4,5},{8,9},{12,13},{16,17},{20,21},{24,25},{28,29},{1,2},{5... | collective-permute-start | bytes 86024 | tf_op jit(solution)/shard_map/ppermute | solution.py:269
  113.4 4.6 %collective-permute-start.5 = (bf16[7,16,128]{2,1,0:T(8,128)(2,1)S(1)}, bf16[7,16,128]{2,1,0:T(8,128)(2,1)S(1)}, u32[]{:S(2)}, u32[]{:S(2)}) collective-permute-start(bf16[7,16,128]{2,1,0:T(8,128)(2,1)S(1)} %shard_map.60.own_ref.forward_ref), channel_id=1, source_target_pairs={{1,0},{5,4},{9,8},{13,12},{17,16},{21,20},{25,24},{29,28},{2,1},{6... | collective-permute-start | bytes 86024 | tf_op jit(solution)/shard_map/ppermute | solution.py:269
  119.3 5.3 %collective-permute-start.6 = (bf16[7,16,128]{2,1,0:T(8,128)(2,1)S(1)}, bf16[7,16,128]{2,1,0:T(8,128)(2,1)S(1)}, u32[]{:S(2)}, u32[]{:S(2)}) collective-permute-start(bf16[7,16,128]{2,1,0:T(8,128)(2,1)S(1)} %shard_map.61.own_ref.forward_ref), channel_id=1, source_target_pairs={{0,1},{4,5},{8,9},{12,13},{16,17},{20,21},{24,25},{28,29},{1,2},{5... | collective-permute-start | bytes 86024 | tf_op jit(solution)/shard_map/ppermute | solution.py:269
  121.6 4.6 %collective-permute-start.7 = (bf16[7,16,128]{2,1,0:T(8,128)(2,1)S(1)}, bf16[7,16,128]{2,1,0:T(8,128)(2,1)S(1)}, u32[]{:S(2)}, u32[]{:S(2)}) collective-permute-start(bf16[7,16,128]{2,1,0:T(8,128)(2,1)S(1)} %shard_map.61.own_ref.forward_ref), channel_id=1, source_target_pairs={{1,0},{5,4},{9,8},{13,12},{17,16},{21,20},{25,24},{29,28},{2,1},{6... | collective-permute-start | bytes 86024 | tf_op jit(solution)/shard_map/ppermute | solution.py:269
  127.5 5.3 %collective-permute-start.8 = (bf16[7,16,128]{2,1,0:T(8,128)(2,1)S(1)}, bf16[7,16,128]{2,1,0:T(8,128)(2,1)S(1)}, u32[]{:S(2)}, u32[]{:S(2)}) collective-permute-start(bf16[7,16,128]{2,1,0:T(8,128)(2,1)S(1)} %shard_map.62.own_ref.forward_ref), channel_id=1, source_target_pairs={{0,1},{4,5},{8,9},{12,13},{16,17},{20,21},{24,25},{28,29},{1,2},{5... | collective-permute-start | bytes 86024 | tf_op jit(solution)/shard_map/ppermute | solution.py:269
  130.6 4.6 %collective-permute-start.9 = (bf16[7,16,128]{2,1,0:T(8,128)(2,1)S(1)}, bf16[7,16,128]{2,1,0:T(8,128)(2,1)S(1)}, u32[]{:S(2)}, u32[]{:S(2)}) collective-permute-start(bf16[7,16,128]{2,1,0:T(8,128)(2,1)S(1)} %shard_map.62.own_ref.forward_ref), channel_id=1, source_target_pairs={{1,0},{5,4},{9,8},{13,12},{17,16},{21,20},{25,24},{29,28},{2,1},{6... | collective-permute-start | bytes 86024 | tf_op jit(solution)/shard_map/ppermute | solution.py:269
  136.4 5.3 %collective-permute-start.10 = (bf16[7,16,128]{2,1,0:T(8,128)(2,1)S(1)}, bf16[7,16,128]{2,1,0:T(8,128)(2,1)S(1)}, u32[]{:S(2)}, u32[]{:S(2)}) collective-permute-start(bf16[7,16,128]{2,1,0:T(8,128)(2,1)S(1)} %shard_map.63.own_ref.forward_ref), channel_id=1, source_target_pairs={{0,1},{4,5},{8,9},{12,13},{16,17},{20,21},{24,25},{28,29},{1,2},{5... | collective-permute-start | bytes 86024 | tf_op jit(solution)/shard_map/ppermute | solution.py:269
  139.3 4.6 %collective-permute-start.11 = (bf16[7,16,128]{2,1,0:T(8,128)(2,1)S(1)}, bf16[7,16,128]{2,1,0:T(8,128)(2,1)S(1)}, u32[]{:S(2)}, u32[]{:S(2)}) collective-permute-start(bf16[7,16,128]{2,1,0:T(8,128)(2,1)S(1)} %shard_map.63.own_ref.forward_ref), channel_id=1, source_target_pairs={{1,0},{5,4},{9,8},{13,12},{17,16},{21,20},{25,24},{29,28},{2,1},{6... | collective-permute-start | bytes 86024 | tf_op jit(solution)/shard_map/ppermute | solution.py:269
  145.1 5.6 %collective-permute-start.12 = (bf16[7,16,128]{2,1,0:T(8,128)(2,1)S(1)}, bf16[7,16,128]{2,1,0:T(8,128)(2,1)S(1)}, u32[]{:S(2)}, u32[]{:S(2)}) collective-permute-start(bf16[7,16,128]{2,1,0:T(8,128)(2,1)S(1)} %shard_map.64.own_ref.forward_ref), channel_id=1, source_target_pairs={{0,1},{4,5},{8,9},{12,13},{16,17},{20,21},{24,25},{28,29},{1,2},{5... | collective-permute-start | bytes 86024 | tf_op jit(solution)/shard_map/ppermute | solution.py:269
  148.8 5.8 %collective-permute-start.13 = (bf16[7,16,128]{2,1,0:T(8,128)(2,1)S(1)}, bf16[7,16,128]{2,1,0:T(8,128)(2,1)S(1)}, u32[]{:S(2)}, u32[]{:S(2)}) collective-permute-start(bf16[7,16,128]{2,1,0:T(8,128)(2,1)S(1)} %shard_map.64.own_ref.forward_ref), channel_id=1, source_target_pairs={{1,0},{5,4},{9,8},{13,12},{17,16},{21,20},{25,24},{29,28},{2,1},{6... | collective-permute-start | bytes 86024 | tf_op jit(solution)/shard_map/ppermute | solution.py:269
  155.8 5.3 %collective-permute-start.14 = (bf16[7,16,128]{2,1,0:T(8,128)(2,1)S(1)}, bf16[7,16,128]{2,1,0:T(8,128)(2,1)S(1)}, u32[]{:S(2)}, u32[]{:S(2)}) collective-permute-start(bf16[7,16,128]{2,1,0:T(8,128)(2,1)S(1)} %shard_map.65.own_ref.forward_ref), channel_id=1, source_target_pairs={{0,1},{4,5},{8,9},{12,13},{16,17},{20,21},{24,25},{28,29},{1,2},{5... | collective-permute-start | bytes 86024 | tf_op jit(solution)/shard_map/ppermute | solution.py:269
  159.2 4.6 %collective-permute-start.15 = (bf16[7,16,128]{2,1,0:T(8,128)(2,1)S(1)}, bf16[7,16,128]{2,1,0:T(8,128)(2,1)S(1)}, u32[]{:S(2)}, u32[]{:S(2)}) collective-permute-start(bf16[7,16,128]{2,1,0:T(8,128)(2,1)S(1)} %shard_map.65.own_ref.forward_ref), channel_id=1, source_target_pairs={{1,0},{5,4},{9,8},{13,12},{17,16},{21,20},{25,24},{29,28},{2,1},{6... | collective-permute-start | bytes 86024 | tf_op jit(solution)/shard_map/ppermute | solution.py:269
  166.8 5.9 %collective-permute-start.17 = (bf16[7,16,128]{2,1,0:T(8,128)(2,1)S(1)}, bf16[7,16,128]{2,1,0:T(8,128)(2,1)S(1)}, u32[]{:S(2)}, u32[]{:S(2)}) collective-permute-start(bf16[7,16,128]{2,1,0:T(8,128)(2,1)S(1)} %get-tuple-element.51), channel_id=1, source_target_pairs={{0,1},{4,5},{8,9},{12,13},{16,17},{20,21},{24,25},{28,29},{1,2},{5... | collective-permute-start | bytes 86024 | tf_op jit(solution)/shard_map/ppermute | solution.py:269
  170.1 4.6 %collective-permute-start.18 = (bf16[7,16,128]{2,1,0:T(8,128)(2,1)S(1)}, bf16[7,16,128]{2,1,0:T(8,128)(2,1)S(1)}, u32[]{:S(2)}, u32[]{:S(2)}) collective-permute-start(bf16[7,16,128]{2,1,0:T(8,128)(2,1)S(1)} %get-tuple-element.50), channel_id=1, source_target_pairs={{1,0},{5,4},{9,8},{13,12},{17,16},{21,20},{25,24},{29,28},{2,1},{6... | collective-permute-start | bytes 86024 | tf_op jit(solution)/shard_map/ppermute | solution.py:269
  175.9 5.9 %collective-permute-start.19 = (bf16[7,16,128]{2,1,0:T(8,128)(2,1)S(1)}, bf16[7,16,128]{2,1,0:T(8,128)(2,1)S(1)}, u32[]{:S(2)}, u32[]{:S(2)}) collective-permute-start(bf16[7,16,128]{2,1,0:T(8,128)(2,1)S(1)} %get-tuple-element.49), channel_id=1, source_target_pairs={{0,1},{4,5},{8,9},{12,13},{16,17},{20,21},{24,25},{28,29},{1,2},{5... | collective-permute-start | bytes 86024 | tf_op jit(solution)/shard_map/ppermute | solution.py:269
  179.3 4.6 %collective-permute-start.20 = (bf16[7,16,128]{2,1,0:T(8,128)(2,1)S(1)}, bf16[7,16,128]{2,1,0:T(8,128)(2,1)S(1)}, u32[]{:S(2)}, u32[]{:S(2)}) collective-permute-start(bf16[7,16,128]{2,1,0:T(8,128)(2,1)S(1)} %get-tuple-element.48), channel_id=1, source_target_pairs={{1,0},{5,4},{9,8},{13,12},{17,16},{21,20},{25,24},{29,28},{2,1},{6... | collective-permute-start | bytes 86024 | tf_op jit(solution)/shard_map/ppermute | solution.py:269
  185.1 6.3 %collective-permute-start.21 = (bf16[7,16,128]{2,1,0:T(8,128)(2,1)S(1)}, bf16[7,16,128]{2,1,0:T(8,128)(2,1)S(1)}, u32[]{:S(2)}, u32[]{:S(2)}) collective-permute-start(bf16[7,16,128]{2,1,0:T(8,128)(2,1)S(1)} %get-tuple-element.47), channel_id=1, source_target_pairs={{0,1},{4,5},{8,9},{12,13},{16,17},{20,21},{24,25},{28,29},{1,2},{5... | collective-permute-start | bytes 86024 | tf_op jit(solution)/shard_map/ppermute | solution.py:269
  188.8 4.6 %collective-permute-start.22 = (bf16[7,16,128]{2,1,0:T(8,128)(2,1)S(1)}, bf16[7,16,128]{2,1,0:T(8,128)(2,1)S(1)}, u32[]{:S(2)}, u32[]{:S(2)}) collective-permute-start(bf16[7,16,128]{2,1,0:T(8,128)(2,1)S(1)} %get-tuple-element.46), channel_id=1, source_target_pairs={{1,0},{5,4},{9,8},{13,12},{17,16},{21,20},{25,24},{29,28},{2,1},{6... | collective-permute-start | bytes 86024 | tf_op jit(solution)/shard_map/ppermute | solution.py:269
  194.6 5.9 %collective-permute-start.23 = (bf16[7,16,128]{2,1,0:T(8,128)(2,1)S(1)}, bf16[7,16,128]{2,1,0:T(8,128)(2,1)S(1)}, u32[]{:S(2)}, u32[]{:S(2)}) collective-permute-start(bf16[7,16,128]{2,1,0:T(8,128)(2,1)S(1)} %get-tuple-element.45), channel_id=1, source_target_pairs={{0,1},{4,5},{8,9},{12,13},{16,17},{20,21},{24,25},{28,29},{1,2},{5... | collective-permute-start | bytes 86024 | tf_op jit(solution)/shard_map/ppermute | solution.py:269
  197.1 4.7 %collective-permute-start.24 = (bf16[7,16,128]{2,1,0:T(8,128)(2,1)S(1)}, bf16[7,16,128]{2,1,0:T(8,128)(2,1)S(1)}, u32[]{:S(2)}, u32[]{:S(2)}) collective-permute-start(bf16[7,16,128]{2,1,0:T(8,128)(2,1)S(1)} %get-tuple-element.44), channel_id=1, source_target_pairs={{1,0},{5,4},{9,8},{13,12},{17,16},{21,20},{25,24},{29,28},{2,1},{6... | collective-permute-start | bytes 86024 | tf_op jit(solution)/shard_map/ppermute | solution.py:269
  203.0 6.0 %collective-permute-start.25 = (bf16[7,16,128]{2,1,0:T(8,128)(2,1)S(1)}, bf16[7,16,128]{2,1,0:T(8,128)(2,1)S(1)}, u32[]{:S(2)}, u32[]{:S(2)}) collective-permute-start(bf16[7,16,128]{2,1,0:T(8,128)(2,1)S(1)} %get-tuple-element.43), channel_id=1, source_target_pairs={{0,1},{4,5},{8,9},{12,13},{16,17},{20,21},{24,25},{28,29},{1,2},{5... | collective-permute-start | bytes 86024 | tf_op jit(solution)/shard_map/ppermute | solution.py:269
  206.4 4.6 %collective-permute-start.26 = (bf16[7,16,128]{2,1,0:T(8,128)(2,1)S(1)}, bf16[7,16,128]{2,1,0:T(8,128)(2,1)S(1)}, u32[]{:S(2)}, u32[]{:S(2)}) collective-permute-start(bf16[7,16,128]{2,1,0:T(8,128)(2,1)S(1)} %get-tuple-element.42), channel_id=1, source_target_pairs={{1,0},{5,4},{9,8},{13,12},{17,16},{21,20},{25,24},{29,28},{2,1},{6... | collective-permute-start | bytes 86024 | tf_op jit(solution)/shard_map/ppermute | solution.py:269
  212.2 5.9 %collective-permute-start.27 = (bf16[7,16,128]{2,1,0:T(8,128)(2,1)S(1)}, bf16[7,16,128]{2,1,0:T(8,128)(2,1)S(1)}, u32[]{:S(2)}, u32[]{:S(2)}) collective-permute-start(bf16[7,16,128]{2,1,0:T(8,128)(2,1)S(1)} %get-tuple-element.41), channel_id=1, source_target_pairs={{0,1},{4,5},{8,9},{12,13},{16,17},{20,21},{24,25},{28,29},{1,2},{5... | collective-permute-start | bytes 86024 | tf_op jit(solution)/shard_map/ppermute | solution.py:269
  215.5 4.6 %collective-permute-start.28 = (bf16[7,16,128]{2,1,0:T(8,128)(2,1)S(1)}, bf16[7,16,128]{2,1,0:T(8,128)(2,1)S(1)}, u32[]{:S(2)}, u32[]{:S(2)}) collective-permute-start(bf16[7,16,128]{2,1,0:T(8,128)(2,1)S(1)} %get-tuple-element.40), channel_id=1, source_target_pairs={{1,0},{5,4},{9,8},{13,12},{17,16},{21,20},{25,24},{29,28},{2,1},{6... | collective-permute-start | bytes 86024 | tf_op jit(solution)/shard_map/ppermute | solution.py:269
  221.3 28.2 %collective-permute-start.29 = (bf16[7,16,128]{2,1,0:T(8,128)(2,1)S(1)}, bf16[7,16,128]{2,1,0:T(8,128)(2,1)S(1)}, u32[]{:S(2)}, u32[]{:S(2)}) collective-permute-start(bf16[7,16,128]{2,1,0:T(8,128)(2,1)S(1)} %get-tuple-element.39), channel_id=1, source_target_pairs={{0,1},{4,5},{8,9},{12,13},{16,17},{20,21},{24,25},{28,29},{1,2},{5... | collective-permute-start | bytes 86024 | tf_op jit(solution)/shard_map/ppermute | solution.py:269
  224.7 24.8 %collective-permute-start.30 = (bf16[7,16,128]{2,1,0:T(8,128)(2,1)S(1)}, bf16[7,16,128]{2,1,0:T(8,128)(2,1)S(1)}, u32[]{:S(2)}, u32[]{:S(2)}) collective-permute-start(bf16[7,16,128]{2,1,0:T(8,128)(2,1)S(1)} %get-tuple-element.38), channel_id=1, source_target_pairs={{1,0},{5,4},{9,8},{13,12},{17,16},{21,20},{25,24},{29,28},{2,1},{6... | collective-permute-start | bytes 86024 | tf_op jit(solution)/shard_map/ppermute | solution.py:269
  227.2 29.4 %all-to-all-start.1 = ((bf16[8,7,16,128]{3,2,1,0:T(8,128)(2,1)}), bf16[8,7,16,128]{3,2,1,0:T(8,128)(2,1)S(1)}, u32[]{:S(2)}, u32[]{:S(2)}) async-start(bf16[8,7,16,128]{3,2,1,0:T(8,128)(2,1)} %constant_dynamic-update-slice_fusion), calls=%async_computation.1 | async-start | bytes 458752 | tf_op jit(solution)/shard_map/all_to_all | solution.py:321
  249.5 2.1 copy-start.1
  256.6 14.7 %all-to-all-start.2 = ((bf16[8,7,16,128]{3,2,1,0:T(8,128)(2,1)}), bf16[8,7,16,128]{3,2,1,0:T(8,128)(2,1)S(1)}, u32[]{:S(2)}, u32[]{:S(2)}) async-start(bf16[8,7,16,128]{3,2,1,0:T(8,128)(2,1)} %constant_dynamic-update-slice_fusion.8), calls=%async_computation.2 | async-start | bytes 458752 | tf_op jit(solution)/shard_map/all_to_all | solution.py:321
  261.4 65.1 %collective-permute-start.16 = (bf16[8,7,16,128]{3,2,1,0:T(8,128)(2,1)S(1)}, bf16[8,7,16,128]{3,2,1,0:T(8,128)(2,1)S(1)}, u32[]{:S(2)}, u32[]{:S(2)}) collective-permute-start(bf16[8,7,16,128]{3,2,1,0:T(8,128)(2,1)S(1)} %all-to-all-done.1), channel_id=1, source_target_pairs={{260,0},{261,1},{262,2},{263,3},{295,4},{294,5},{293,6},{292,7},{3... | collective-permute-start | bytes 688136 | tf_op jit(solution)/shard_map/ppermute | solution.py:322
  271.4 60.0 %collective-permute-start.31 = (bf16[8,7,16,128]{3,2,1,0:T(8,128)(2,1)S(1)}, bf16[8,7,16,128]{3,2,1,0:T(8,128)(2,1)S(1)}, u32[]{:S(2)}, u32[]{:S(2)}) collective-permute-start(bf16[8,7,16,128]{3,2,1,0:T(8,128)(2,1)S(1)} %all-to-all-done.2), channel_id=1, source_target_pairs={{260,0},{261,1},{262,2},{263,3},{295,4},{294,5},{293,6},{292,7},{3... | collective-permute-start | bytes 688136 | tf_op jit(solution)/shard_map/ppermute | solution.py:322
Sparse Core Ops, SparseCore 0:
  51.6 55.8 all-gather.2

commit v2 on v0

v2 whole, which is shorter than its diff:
```python
import functools

import jax
import jax.numpy as jnp
from jax import lax
from jax.experimental import pallas as pl
from jax.experimental.pallas import tpu as pltpu
from jax.sharding import PartitionSpec as P

LEVELS = 8
RANKS = 64
SLOTS = 14
PAIRS = 7
LINKS = 3
ORDER = 64
COLS = 128
PART = 16
WINDOW = LINKS * SLOTS
ROTATION = 96
PLANES = 16
ROWS = PAIRS * ORDER
BLOCK = ROWS + 16
SHARD = LINKS * BLOCK
PIECE = PAIRS * 16
WIDE = 2 * LINKS * ORDER
CHUNK = LEVELS // 2
AXES = ("lvl", "row")
BF16 = jnp.bfloat16
F32 = jnp.float32
VMEM = pltpu.VMEM

PLANE_OF = [(band + 14) % PLANES for band in range(PLANES)]


def slot_of(band, turn):
    return (turn - band) % 4 * 2 + turn // 4


def turn_of_slot(slot, shift):
    return (slot // 2 + shift) % 4 + slot % 2 * 4


def place_slot(rank, slot):
    band, side = divmod(rank, 4)
    y = side if band % 2 == 0 else 3 - side
    return (PLANE_OF[band] * 8 + slot) * 4 + y


def place(rank, turn):
    return place_slot(rank, slot_of(rank // 4, turn))


def native(level, rank):
    return (level * RANKS + rank - ROTATION) % (LEVELS * RANKS)


def level_pairs():
    return [
        (native(level, rank), place(rank, level))
        for level in range(LEVELS)
        for rank in range(RANKS)
    ]


def neighbour_pairs(step):
    return [
        (place_slot(rank, slot), place_slot(rank + step, slot))
        for rank in range(RANKS)
        if 0 <= rank + step < RANKS
        for slot in range(COLS // PART)
    ]


def group_list():
    return [
        [PLANE_OF[band] * 8 + slot_of(band, turn) for turn in range(LEVELS)] for band in range(PLANES)
    ]


def left_lanes(shape):
    return lax.broadcasted_iota(jnp.int32, shape, len(shape) - 1) < ORDER


def call(kernel, outs, operands, scratch=(), scalars=0):
    return pl.pallas_call(
        kernel,
        out_shape=[jax.ShapeDtypeStruct(shape, dtype) for shape, dtype in outs],
        in_specs=[
            pl.BlockSpec(memory_space=pltpu.SMEM if n < scalars else VMEM) for n in range(len(operands))
        ],
        out_specs=[pl.BlockSpec(memory_space=VMEM) for _ in outs],
        scratch_shapes=list(scratch),
        compiler_params=pltpu.CompilerParams(vmem_limit_bytes=16 * 1024 * 1024),
    )(*operands)


def put_block(ref, row, values):
    for part in range(LINKS):
        start = part * BLOCK + row
        ref[start : start + values.shape[0], :] = values[:, part * 128 : (part + 1) * 128]


def prepare_kernel(shift_ref, pattern_ref, rhs_ref, factor_ref, diag_ref, out_ref):
    lane = lax.broadcasted_iota(jnp.int32, (16, WIDE), 1)
    entries = jnp.zeros((16, WIDE), jnp.int32)
    for n in range(SLOTS):
        for m in range(LINKS):
            entry = jnp.clip(pattern_ref[n, m], 0, WINDOW - 1)
            entries = jnp.where(lane == LINKS * n + m, entry, entries)
    entries = entries.astype(F32).astype(BF16)
    for i in range(PAIRS):
        couplings, sides = [], []
        for n in (i, i + PAIRS):
            diag = diag_ref[n]
            factor = jnp.concatenate([factor_ref[n, m] for m in range(LINKS)], axis=1)
            couplings.append(jnp.dot(diag, factor, preferred_element_type=F32))
            sides.append(jnp.dot(diag, rhs_ref[n], preferred_element_type=F32))
        both = jnp.concatenate(couplings, axis=1).astype(BF16)
        put_block(out_ref, i * ORDER, both)
        turned = jnp.concatenate(sides, axis=0).T.astype(BF16)
        for j in range(COLS // PART):
            row = SHARD + turn_of_slot(j, shift_ref[0]) * PIECE + i * PART
            out_ref[pl.ds(pl.multiple_of(row, 16), PART), :] = turned[j * PART : (j + 1) * PART, :]
    put_block(out_ref, ROWS, entries)


def finish_kernel(shift_ref, parts_ref, diag_ref, forward_ref, backward_ref):
    for i in range(PAIRS):
        for kind in range(2):
            columns = jnp.concatenate(
                [parts_ref[turn_of_slot(j, shift_ref[0]), kind, i] for j in range(COLS // PART)], axis=0
            )
            turned = columns.astype(F32).T.astype(BF16)
            for n, rows in ((i, turned[:ORDER]), (i + PAIRS, turned[ORDER:])):
                if kind == 0:
                    forward_ref[n] = rows
                else:
                    backward_ref[n] = lax.dot_general(
                        diag_ref[n], rows, (((0,), (0,)), ((), ())), preferred_element_type=F32
                    ).astype(BF16)


def put_window(window_ref, source_ref, base):
    for i in range(PAIRS):
        pair = source_ref[i].astype(F32)
        swapped = pltpu.roll(pair, ORDER, 1)
        left = left_lanes(pair.shape)
        window_ref[base + i] = jnp.where(left, pair, swapped).astype(BF16)
        window_ref[base + PAIRS + i] = jnp.where(left, swapped, pair).astype(BF16)


def level_weights(level, state_ref, own_ref, other_ref):
    mine = state_ref[1] == level // 4
    index = shard_index(state_ref, level)

    def weights(i):
        parts = []
        for part in range(LINKS):
            rows = pl.ds(part * BLOCK + i * ORDER, ORDER)
            parts.append(jnp.where(mine, own_ref[index, rows, :], other_ref[index, rows, :]))
        return jnp.concatenate(parts, axis=1)

    return weights


def shard_index(state_ref, level):
    return (state_ref[0] + LEVELS - level) & 3


def forward_pair(pattern_ref, level, index, weights, window_ref, rhs_ref, i):
    w = weights(i)
    sums = []
    for n in (i, i + PAIRS):
        a, b, c = (window_ref[pattern_ref[index, LINKS * n + m]] for m in range(LINKS))
        left = left_lanes(a.shape)
        zero = jnp.zeros_like(a)
        if n < PAIRS:
            picked, lanes = (jnp.where(left, a, b), jnp.where(left, c, zero)), slice(0, 256)
        else:
            picked, lanes = (jnp.where(left, zero, a), jnp.where(left, b, c)), slice(128, 384)
        sums.append(
            lax.dot_general(
                jnp.concatenate(picked, axis=1),
                w[:, lanes],
                (((1,), (1,)), ((), ())),
                preferred_element_type=F32,
            )
        )
    return (rhs_ref[level, i].astype(F32) - jnp.concatenate(sums, axis=1)).astype(BF16)


def fill_window(window_ref, own_ref, below_ref, above_ref):
    put_window(window_ref, below_ref, 0)
    put_window(window_ref, own_ref, SLOTS)
    put_window(window_ref, above_ref, 2 * SLOTS)


def level_kernel(level, step, state_ref, pattern_ref, own_ref, other_ref, *refs):
    weights = level_weights(level, state_ref, own_ref, other_ref)
    index = shard_index(state_ref, level) + 4 * (state_ref[1] != level // 4).astype(jnp.int32)
    step(pattern_ref, level, index, weights, *refs)


def forward_step(
    pattern_ref, level, index, weights, rhs_ref, own_ref, below_ref, above_ref, out_ref, window_ref
):
    fill_window(window_ref, own_ref, below_ref, above_ref)
    for i in range(PAIRS):
        out_ref[i] = forward_pair(pattern_ref, level, index, weights, window_ref, rhs_ref, i)


def spread(pattern_ref, index, weights, reduced, sums_ref, total_ref):
    for q in range(WINDOW):
        total_ref[q] = jnp.zeros(total_ref.shape[1:], F32)
    for i in range(PAIRS):
        pair = reduced[i].astype(F32)
        rows = jnp.concatenate([pair, pltpu.roll(pair, ORDER, 1)], axis=0)[:, :ORDER].astype(BF16)
        products = jnp.dot(rows, weights(i), preferred_element_type=F32)
        for n, product in ((i, products[:PART, :256]), (i + PAIRS, products[PART:, 128:])):
            head, tail = product[:, :128], product[:, 128:]
            left = left_lanes(head.shape)
            zero = jnp.zeros_like(head)
            if n < PAIRS:
                terms = (jnp.where(left, head, zero), jnp.where(left, zero, head), jnp.where(left, tail, zero))
            else:
                terms = (jnp.where(left, zero, head), jnp.where(left, tail, zero), jnp.where(left, zero, tail))
            for m in range(LINKS):
                total_ref[pattern_ref[index, LINKS * n + m]] += terms[m]
    for part in range(LINKS):
        for i in range(PAIRS):
            one = total_ref[part * SLOTS + i]
            two = total_ref[part * SLOTS + PAIRS + i]
            left = left_lanes(one.shape)
            one = one + pltpu.roll(one, ORDER, 1)
            two = two + pltpu.roll(two, ORDER, 1)
            sums_ref[part, i] = jnp.where(left, one, two).astype(BF16)


def turn_step(
    pattern_ref, level, index, weights, rhs_ref, own_ref, below_ref, above_ref,
    out_ref, sums_ref, window_ref, total_ref,
):
    fill_window(window_ref, own_ref, below_ref, above_ref)
    solved = []
    for i in range(PAIRS):
        solved.append(forward_pair(pattern_ref, level, index, weights, window_ref, rhs_ref, i))
        out_ref[i] = solved[i]
    spread(pattern_ref, index, weights, solved, sums_ref, total_ref)


def reduce(forward_ref, own_ref, below_ref, above_ref, out_ref):
    reduced = []
    for i in range(PAIRS):
        incoming = own_ref[1, i].astype(F32) + below_ref[i].astype(F32) + above_ref[i].astype(F32)
        reduced.append((forward_ref[i].astype(F32) - incoming).astype(BF16))
        out_ref[i] = reduced[i]
    return reduced


def backward_step(
    pattern_ref, level, index, weights, forward_ref, own_ref, below_ref, above_ref, out_ref, sums_ref, total_ref
):
    reduced = reduce(forward_ref, own_ref, below_ref, above_ref, out_ref)
    spread(pattern_ref, index, weights, reduced, sums_ref, total_ref)


def last_kernel(sums_ref, below_ref, above_ref, *refs):
    forward, reduced, packed_ref = refs[:LEVELS], refs[LEVELS:-1], refs[-1]
    for level in range(LEVELS):
        packed_ref[level, 0] = forward[level][...]
        if level > 0:
            packed_ref[level, 1] = reduced[level - 1][...]
    reduce(forward[0], sums_ref, below_ref, above_ref, packed_ref.at[0, 1])


def per_device(right_side, factor_blocks, diag_inverse, pattern):
    up, down = neighbour_pairs(1), neighbour_pairs(-1)
    to_group = level_pairs()
    to_native = [(b, a) for a, b in to_group]
    groups = group_list()
    solved_shape = ((PAIRS, PART, 128), BF16)
    sums_shape = ((LINKS, PAIRS, PART, 128), BF16)
    window = VMEM((WINDOW, PART, 128), BF16)
    total = VMEM((WINDOW, PART, 128), F32)

    def exchange(to_above, to_below):
        return lax.ppermute(to_above, AXES, up), lax.ppermute(to_below, AXES, down)

    lvl = lax.axis_index("lvl")
    plane, x, core = lvl // 8, lvl % 8 // 2, lvl % 2
    band = (plane - PLANE_OF[0]) % PLANES
    state = jnp.stack([(x + band) % 4, core]).astype(jnp.int32)
    shift = ((x * 2 + core) % 4).astype(jnp.int32).reshape(1)

    (prepared,) = call(
        prepare_kernel,
        [((SHARD + COLS // PART * PIECE, 128), BF16)],
        (shift, pattern, right_side, factor_blocks, diag_inverse),
        scalars=2,
    )
    prepared = lax.ppermute(prepared, AXES, to_group)
    weights, rhs = prepared[:SHARD], prepared[SHARD:].reshape(LEVELS, PAIRS, PART, 128)

    def along_x(steps):
        pairs = [(i, i // 8 * 8 + (i % 8 + 2 * steps) % 8) for i in range(128)]
        return lax.ppermute(weights, "lvl", pairs)

    gathered = (along_x(1), along_x(2), along_x(3))
    rhs = lax.all_to_all(rhs, "lvl", 0, 0, axis_index_groups=groups)
    latest = rhs[0]
    near = exchange(latest, latest)
    *gathered, below, above = lax.optimization_barrier((*gathered, *near))
    near = (below, above)
    own = jnp.stack([weights, *gathered])
    other = lax.ppermute(own, "lvl", [(i, i ^ 1) for i in range(128)])
    patterns = jnp.concatenate([own[:, ROWS, :WINDOW], other[:, ROWS, :WINDOW]]).astype(jnp.int32)

    def level_call(level, step, arrays, outs, scratch):
        kernel = functools.partial(level_kernel, level, step)
        return call(kernel, outs, (state, patterns, own, other) + arrays, scratch, scalars=2)

    forward = [latest]
    for level in range(1, LEVELS):
        below, above = near if level == 1 else exchange(latest, latest)
        last = level == LEVELS - 1
        latest, *rest = level_call(
            level,
            turn_step if last else forward_step,
            (rhs, latest, below, above),
            [solved_shape, sums_shape] if last else [solved_shape],
            [window, total] if last else [window],
        )
        forward.append(latest)
    (sums,) = rest

    reduced = [latest]
    for level in range(LEVELS - 2, 0, -1):
        below, above = exchange(sums[2], sums[0])
        latest, sums = level_call(
            level,
            backward_step,
            (forward[level], sums, below, above),
            [solved_shape, sums_shape],
            [total],
        )
        reduced.append(latest)
    below, above = exchange(sums[2], sums[0])
    (packed,) = call(
        last_kernel,
        [((LEVELS, 2, PAIRS, PART, 128), BF16)],
        (sums, below, above, *forward, *reduced[::-1]),
    )

    parts = lax.all_to_all(packed, "lvl", 0, 0, axis_index_groups=groups)
    parts = lax.ppermute(parts, AXES, to_native)
    out_shape = ((SLOTS, ORDER, COLS), BF16)
    return call(finish_kernel, [out_shape] * 2, (shift, parts, diag_inverse), scalars=1)


def solution(mesh):
    return jax.shard_map(
        per_device,
        mesh=mesh,
        in_specs=(
            P(AXES, None, None),
            P(AXES, None, None, None),
            P(AXES, None, None),
            P(AXES, None),
        ),
        out_specs=(P(AXES, None, None), P(AXES, None, None)),
        check_vma=False,
    )
```

time: 760 us -> 277 us (0.36)
  the two profiles are of different devices: /device:TPU:384 before, /device:TPU:97 now
where the time goes in v2:
time: 277 us; the launch traced here: 275 us
  starting transfers between devices  145 us (52%)
  waiting for transfers between devices  82.9 us (30%)
  blocking collectives  25.4 us (9%)
  Pallas kernels  16.2 us (6%)
  local copies, waits for them, and re-layouts  4.57 us (2%)
    ppermute x14, starting transfers between devices, exchange(): lax.ppermute(to_above, AXES, up)  68.9 us
    ppermute x1, waiting for transfers between devices, per_device(): parts = lax.ppermute(parts, AXES, to_native)  32.2 us
    ppermute x1, waiting for transfers between devices, per_device(): prepared = lax.ppermute(prepared, AXES, to_group)  30.3 us
    ppermute x14, starting transfers between devices, exchange(): lax.ppermute(to_below, AXES, down)  27.1 us
    all_to_all x1, blocking collectives, per_device(): parts = lax.all_to_all(packed, 'lvl', 0, 0, axis_index_groups=groups)  25.4 us
    pallas_call x16, Pallas kernels, call(): pl.pallas_call(kernel, out_shape=[jax.ShapeDtypeStruct(shape, dtype) for...  16.2 us
    all_to_all x1, starting transfers between devices, per_device(): rhs = lax.all_to_all(rhs, 'lvl', 0, 0, axis_index_groups=groups)  15.8 us
    ppermute x1, starting transfers between devices, per_device(): prepared = lax.ppermute(prepared, AXES, to_group)  15.2 us
  transfers between devices with their start and end apart: 35, of which 18 were waited for; matrix products, arithmetic and copies ran while one was open for 0% of the time, Pallas kernels for 0%

profile of v2, /device:TPU:97, one launch (start us, length us, event | category | flops | bytes accessed | tf_op | source)
XLA Modules:
  0.0 275.4 jit_solution(2896231825820237075)
XLA Ops:
  4.4 1.2 shard_map.59
  5.6 15.2 %collective-permute-start = (bf16[2288,128]{1,0:T(8,128)(2,1)S(1)}, bf16[2288,128]{1,0:T(8,128)(2,1)S(1)}, u32[]{:S(2)}, u32[]{:S(2)}) collective-permute-start(bf16[2288,128]{1,0:T(8,128)(2,1)S(1)} %shard_map.59), channel_id=1, source_target_pairs={{416,448},{417,449},{418,450},{419,451},{420,507},{421,506},{422,5... | collective-permute-start | bytes 1757192 | tf_op jit(solution)/shard_map/ppermute | solution.py:301
  20.9 30.3 %collective-permute-done = bf16[2288,128]{1,0:T(8,128)(2,1)S(1)} collective-permute-done((bf16[2288,128]{1,0:T(8,128)(2,1)S(1)}, bf16[2288,128]{1,0:T(8,128)(2,1)S(1)}, u32[]{:S(2)}, u32[]{:S(2)}) %collective-permute-start) | collective-permute-done | bytes 585760 | tf_op jit(solution)/shard_map/ppermute | solution.py:301
  51.9 15.8 %all-to-all-start = ((bf16[8,7,16,128]{3,2,1,0:T(8,128)(2,1)}), bf16[8,7,16,128]{3,2,1,0:T(8,128)(2,1)S(1)}, u32[]{:S(2)}, u32[]{:S(2)}) async-start(bf16[8,7,16,128]{3,2,1,0:T(8,128)(2,1)} %bitcast.4), calls=%async_computation | async-start | bytes 458752 | tf_op jit(solution)/shard_map/all_to_all | solution.py:309
  67.7 3.1 %collective-permute-start.2 = (bf16[1392,128]{1,0:T(8,128)(2,1)S(1)}, bf16[1392,128]{1,0:T(8,128)(2,1)S(1)}, u32[]{:S(2)}, u32[]{:S(2)}) collective-permute-start(bf16[1392,128]{1,0:T(8,128)(2,1)S(1)} %get-tuple-element.41), channel_id=1, source_target_pairs={{0,16},{4,20},{8,24},{12,28},{16,0},{20,4},{24,8},{28,12},{32,48},... | collective-permute-start | bytes 1069064 | tf_op jit(solution)/shard_map/ppermute | solution.py:306
  70.9 2.1 collective-permute-start.1
  72.9 4.4 %collective-permute-start.3 = (bf16[1392,128]{1,0:T(8,128)(2,1)S(1)}, bf16[1392,128]{1,0:T(8,128)(2,1)S(1)}, u32[]{:S(2)}, u32[]{:S(2)}) collective-permute-start(bf16[1392,128]{1,0:T(8,128)(2,1)S(1)} %get-tuple-element.41), channel_id=1, source_target_pairs={{0,24},{4,28},{8,0},{12,4},{16,8},{20,12},{24,16},{28,20},{32,56},... | collective-permute-start | bytes 1069064 | tf_op jit(solution)/shard_map/ppermute | solution.py:306
  77.4 1.9 collective-permute-start.5
  79.3 4.6 %collective-permute-start.4 = (bf16[7,16,128]{2,1,0:T(8,128)(2,1)S(1)}, bf16[7,16,128]{2,1,0:T(8,128)(2,1)S(1)}, u32[]{:S(2)}, u32[]{:S(2)}) collective-permute-start(bf16[7,16,128]{2,1,0:T(8,128)(2,1)S(1)} %slice_bitcast_fusion.refs_1_.refs_0_), channel_id=1, source_target_pairs={{448,449},{452,453},{456,457},{460,461},{464,465},{468,469},{472,4... | collective-permute-start | bytes 86024 | tf_op jit(solution)/shard_map/ppermute | solution.py:287
  84.9 4.2 %collective-permute-done.1 = bf16[1392,128]{1,0:T(8,128)(2,1)S(1)} collective-permute-done((bf16[1392,128]{1,0:T(8,128)(2,1)S(1)}, bf16[1392,128]{1,0:T(8,128)(2,1)S(1)}, u32[]{:S(2)}, u32[]{:S(2)}) %collective-permute-start.1) | collective-permute-done | bytes 356384 | tf_op jit(solution)/shard_map/ppermute | solution.py:306
  89.2 2.4 collective-permute-start.6
  91.8 2.7 collective-permute-done.6.other_ref
  95.4 1.9 collective-permute-start.8
  97.4 5.6 %collective-permute-start.7 = (bf16[7,16,128]{2,1,0:T(8,128)(2,1)S(1)}, bf16[7,16,128]{2,1,0:T(8,128)(2,1)S(1)}, u32[]{:S(2)}, u32[]{:S(2)}) collective-permute-start(bf16[7,16,128]{2,1,0:T(8,128)(2,1)S(1)} %shard_map.60.refs_1_.refs_0_), channel_id=1, source_target_pairs={{448,449},{452,453},{456,457},{460,461},{464,465},{468,469},{472,4... | collective-permute-start | bytes 86024 | tf_op jit(solution)/shard_map/ppermute | solution.py:287
  105.0 1.9 collective-permute-start.10
  106.9 4.9 %collective-permute-start.9 = (bf16[7,16,128]{2,1,0:T(8,128)(2,1)S(1)}, bf16[7,16,128]{2,1,0:T(8,128)(2,1)S(1)}, u32[]{:S(2)}, u32[]{:S(2)}) collective-permute-start(bf16[7,16,128]{2,1,0:T(8,128)(2,1)S(1)} %shard_map.61.refs_1_.refs_0_.refs_2_), channel_id=1, source_target_pairs={{448,449},{452,453},{456,457},{460,461},{464,465},{468,469},{472,4... | collective-permute-start | bytes 86024 | tf_op jit(solution)/shard_map/ppermute | solution.py:287
  113.7 1.9 collective-permute-start.12
  115.6 4.9 %collective-permute-start.11 = (bf16[7,16,128]{2,1,0:T(8,128)(2,1)S(1)}, bf16[7,16,128]{2,1,0:T(8,128)(2,1)S(1)}, u32[]{:S(2)}, u32[]{:S(2)}) collective-permute-start(bf16[7,16,128]{2,1,0:T(8,128)(2,1)S(1)} %shard_map.62.refs_1_.refs_0_.refs_3_), channel_id=1, source_target_pairs={{448,449},{452,453},{456,457},{460,461},{464,465},{468,469},{472,4... | collective-permute-start | bytes 86024 | tf_op jit(solution)/shard_map/ppermute | solution.py:287
  122.4 1.9 collective-permute-start.14
  124.4 4.9 %collective-permute-start.13 = (bf16[7,16,128]{2,1,0:T(8,128)(2,1)S(1)}, bf16[7,16,128]{2,1,0:T(8,128)(2,1)S(1)}, u32[]{:S(2)}, u32[]{:S(2)}) collective-permute-start(bf16[7,16,128]{2,1,0:T(8,128)(2,1)S(1)} %shard_map.63.refs_1_.refs_0_.refs_4_), channel_id=1, source_target_pairs={{448,449},{452,453},{456,457},{460,461},{464,465},{468,469},{472,4... | collective-permute-start | bytes 86024 | tf_op jit(solution)/shard_map/ppermute | solution.py:287
  131.2 1.9 collective-permute-start.16
  133.1 4.9 %collective-permute-start.15 = (bf16[7,16,128]{2,1,0:T(8,128)(2,1)S(1)}, bf16[7,16,128]{2,1,0:T(8,128)(2,1)S(1)}, u32[]{:S(2)}, u32[]{:S(2)}) collective-permute-start(bf16[7,16,128]{2,1,0:T(8,128)(2,1)S(1)} %shard_map.64.refs_1_.refs_0_.refs_5_), channel_id=1, source_target_pairs={{448,449},{452,453},{456,457},{460,461},{464,465},{468,469},{472,4... | collective-permute-start | bytes 86024 | tf_op jit(solution)/shard_map/ppermute | solution.py:287
  139.9 1.9 collective-permute-start.18
  141.8 4.9 %collective-permute-start.17 = (bf16[7,16,128]{2,1,0:T(8,128)(2,1)S(1)}, bf16[7,16,128]{2,1,0:T(8,128)(2,1)S(1)}, u32[]{:S(2)}, u32[]{:S(2)}) collective-permute-start(bf16[7,16,128]{2,1,0:T(8,128)(2,1)S(1)} %shard_map.65.refs_1_.refs_0_.refs_6_), channel_id=1, source_target_pairs={{448,449},{452,453},{456,457},{460,461},{464,465},{468,469},{472,4... | collective-permute-start | bytes 86024 | tf_op jit(solution)/shard_map/ppermute | solution.py:287
  147.7 1.5 shard_map.66
  149.1 1.9 collective-permute-start.20
  151.1 4.9 %collective-permute-start.19 = (bf16[7,16,128]{2,1,0:T(8,128)(2,1)S(1)}, bf16[7,16,128]{2,1,0:T(8,128)(2,1)S(1)}, u32[]{:S(2)}, u32[]{:S(2)}) collective-permute-start(bf16[7,16,128]{2,1,0:T(8,128)(2,1)S(1)} %get-tuple-element.55), channel_id=1, source_target_pairs={{448,449},{452,453},{456,457},{460,461},{464,465},{468,469},{472,4... | collective-permute-start | bytes 86024 | tf_op jit(solution)/shard_map/ppermute | solution.py:287
  156.9 1.1 shard_map.67
  158.0 1.9 collective-permute-start.22
  160.0 4.9 %collective-permute-start.21 = (bf16[7,16,128]{2,1,0:T(8,128)(2,1)S(1)}, bf16[7,16,128]{2,1,0:T(8,128)(2,1)S(1)}, u32[]{:S(2)}, u32[]{:S(2)}) collective-permute-start(bf16[7,16,128]{2,1,0:T(8,128)(2,1)S(1)} %get-tuple-element.53), channel_id=1, source_target_pairs={{448,449},{452,453},{456,457},{460,461},{464,465},{468,469},{472,4... | collective-permute-start | bytes 86024 | tf_op jit(solution)/shard_map/ppermute | solution.py:287
  165.8 1.1 shard_map.68
  166.9 1.9 collective-permute-start.24
  168.8 4.9 %collective-permute-start.23 = (bf16[7,16,128]{2,1,0:T(8,128)(2,1)S(1)}, bf16[7,16,128]{2,1,0:T(8,128)(2,1)S(1)}, u32[]{:S(2)}, u32[]{:S(2)}) collective-permute-start(bf16[7,16,128]{2,1,0:T(8,128)(2,1)S(1)} %get-tuple-element.51), channel_id=1, source_target_pairs={{448,449},{452,453},{456,457},{460,461},{464,465},{468,469},{472,4... | collective-permute-start | bytes 86024 | tf_op jit(solution)/shard_map/ppermute | solution.py:287
  174.8 1.1 shard_map.69
  175.9 1.9 collective-permute-start.26
  177.8 5.3 %collective-permute-start.25 = (bf16[7,16,128]{2,1,0:T(8,128)(2,1)S(1)}, bf16[7,16,128]{2,1,0:T(8,128)(2,1)S(1)}, u32[]{:S(2)}, u32[]{:S(2)}) collective-permute-start(bf16[7,16,128]{2,1,0:T(8,128)(2,1)S(1)} %get-tuple-element.49), channel_id=1, source_target_pairs={{448,449},{452,453},{456,457},{460,461},{464,465},{468,469},{472,4... | collective-permute-start | bytes 86024 | tf_op jit(solution)/shard_map/ppermute | solution.py:287
  185.3 1.9 collective-permute-start.28
  187.2 4.9 %collective-permute-start.27 = (bf16[7,16,128]{2,1,0:T(8,128)(2,1)S(1)}, bf16[7,16,128]{2,1,0:T(8,128)(2,1)S(1)}, u32[]{:S(2)}, u32[]{:S(2)}) collective-permute-start(bf16[7,16,128]{2,1,0:T(8,128)(2,1)S(1)} %get-tuple-element.47), channel_id=1, source_target_pairs={{448,449},{452,453},{456,457},{460,461},{464,465},{468,469},{472,4... | collective-permute-start | bytes 86024 | tf_op jit(solution)/shard_map/ppermute | solution.py:287
  193.0 1.1 shard_map.71
  194.1 1.9 collective-permute-start.30
  196.1 4.9 %collective-permute-start.29 = (bf16[7,16,128]{2,1,0:T(8,128)(2,1)S(1)}, bf16[7,16,128]{2,1,0:T(8,128)(2,1)S(1)}, u32[]{:S(2)}, u32[]{:S(2)}) collective-permute-start(bf16[7,16,128]{2,1,0:T(8,128)(2,1)S(1)} %get-tuple-element.45), channel_id=1, source_target_pairs={{448,449},{452,453},{456,457},{460,461},{464,465},{468,469},{472,4... | collective-permute-start | bytes 86024 | tf_op jit(solution)/shard_map/ppermute | solution.py:287
  201.9 1.1 shard_map.72
  203.0 2.1 collective-permute-start.32
  205.1 4.9 %collective-permute-start.31 = (bf16[7,16,128]{2,1,0:T(8,128)(2,1)S(1)}, bf16[7,16,128]{2,1,0:T(8,128)(2,1)S(1)}, u32[]{:S(2)}, u32[]{:S(2)}) collective-permute-start(bf16[7,16,128]{2,1,0:T(8,128)(2,1)S(1)} %get-tuple-element.43), channel_id=1, source_target_pairs={{448,449},{452,453},{456,457},{460,461},{464,465},{468,469},{472,4... | collective-permute-start | bytes 86024 | tf_op jit(solution)/shard_map/ppermute | solution.py:287
  211.0 25.4 %all_to_all.10 = bf16[8,2,7,16,128]{4,3,2,1,0:T(8,128)(2,1)S(1)} all-to-all(bf16[8,2,7,16,128]{4,3,2,1,0:T(8,128)(2,1)S(1)} %shard_map.73), channel_id=1, replica_groups={{448,456,464,472,452,460,468,476},{504,480,488,496,508,484,492,500},{16..., dimensions={0} | all-to-all | bytes 917504 | tf_op jit(solution)/shard_map/all_to_all | solution.py:354
  236.3 5.8 %collective-permute-start.33 = (bf16[8,2,7,16,128]{4,3,2,1,0:T(8,128)(2,1)S(1)}, bf16[8,2,7,16,128]{4,3,2,1,0:T(8,128)(2,1)S(1)}, u32[]{:S(2)}, u32[]{:S(2)}) collective-permute-start(bf16[8,2,7,16,128]{4,3,2,1,0:T(8,128)(2,1)S(1)} %all_to_all.10), channel_id=1, source_target_pairs={{448,416},{449,417},{450,418},{451,419},{507,420},{506,421},{505,4... | collective-permute-start | bytes 1376264 | tf_op jit(solution)/shard_map/ppermute | solution.py:355
  242.1 32.2 %collective-permute-done.33.parts_ref = bf16[8,2,7,16,128]{4,3,2,1,0:T(8,128)(2,1)S(1)} collective-permute-done((bf16[8,2,7,16,128]{4,3,2,1,0:T(8,128)(2,1)S(1)}, bf16[8,2,7,16,128]{4,3,2,1,0:T(8,128)(2,1)S(1)}, u32[]{:S(2)}, u32[]{:S(2)}) %collective-permute-start.33) | collective-permute-done | bytes 458784 | tf_op jit(solution)/shard_map/ppermute | solution.py:355
  274.3 1.1 shard_map.74
  (65 shorter events, 25.3 us)
Async XLA Ops:
  1.5 0.9 copy-start
  2.4 1.1 copy-start.2
  3.5 0.9 copy-start.3
  5.6 45.5 %collective-permute-start = (bf16[2288,128]{1,0:T(8,128)(2,1)S(1)}, bf16[2288,128]{1,0:T(8,128)(2,1)S(1)}, u32[]{:S(2)}, u32[]{:S(2)}) collective-permute-start(bf16[2288,128]{1,0:T(8,128)(2,1)S(1)} %shard_map.59), channel_id=1, source_target_pairs={{416,448},{417,449},{418,450},{419,451},{420,507},{421,506},{422,5... | collective-permute-start | bytes 1757192 | tf_op jit(solution)/shard_map/ppermute | solution.py:301
  51.9 25.5 %all-to-all-start = ((bf16[8,7,16,128]{3,2,1,0:T(8,128)(2,1)}), bf16[8,7,16,128]{3,2,1,0:T(8,128)(2,1)S(1)}, u32[]{:S(2)}, u32[]{:S(2)}) async-start(bf16[8,7,16,128]{3,2,1,0:T(8,128)(2,1)} %bitcast.4), calls=%async_computation | async-start | bytes 458752 | tf_op jit(solution)/shard_map/all_to_all | solution.py:309
  67.7 17.1 %collective-permute-start.2 = (bf16[1392,128]{1,0:T(8,128)(2,1)S(1)}, bf16[1392,128]{1,0:T(8,128)(2,1)S(1)}, u32[]{:S(2)}, u32[]{:S(2)}) collective-permute-start(bf16[1392,128]{1,0:T(8,128)(2,1)S(1)} %get-tuple-element.41), channel_id=1, source_target_pairs={{0,16},{4,20},{8,24},{12,28},{16,0},{20,4},{24,8},{28,12},{32,48},... | collective-permute-start | bytes 1069064 | tf_op jit(solution)/shard_map/ppermute | solution.py:306
  70.9 18.2 %collective-permute-start.1 = (bf16[1392,128]{1,0:T(8,128)(2,1)S(1)}, bf16[1392,128]{1,0:T(8,128)(2,1)S(1)}, u32[]{:S(2)}, u32[]{:S(2)}) collective-permute-start(bf16[1392,128]{1,0:T(8,128)(2,1)S(1)} %get-tuple-element.41), channel_id=1, source_target_pairs={{0,8},{4,12},{8,16},{12,20},{16,24},{20,28},{24,0},{28,4},{32,40},... | collective-permute-start | bytes 1069064 | tf_op jit(solution)/shard_map/ppermute | solution.py:306
  72.9 16.1 %collective-permute-start.3 = (bf16[1392,128]{1,0:T(8,128)(2,1)S(1)}, bf16[1392,128]{1,0:T(8,128)(2,1)S(1)}, u32[]{:S(2)}, u32[]{:S(2)}) collective-permute-start(bf16[1392,128]{1,0:T(8,128)(2,1)S(1)} %get-tuple-element.41), channel_id=1, source_target_pairs={{0,24},{4,28},{8,0},{12,4},{16,8},{20,12},{24,16},{28,20},{32,56},... | collective-permute-start | bytes 1069064 | tf_op jit(solution)/shard_map/ppermute | solution.py:306
  77.4 6.5 %collective-permute-start.5 = (bf16[7,16,128]{2,1,0:T(8,128)(2,1)S(1)}, bf16[7,16,128]{2,1,0:T(8,128)(2,1)S(1)}, u32[]{:S(2)}, u32[]{:S(2)}) collective-permute-start(bf16[7,16,128]{2,1,0:T(8,128)(2,1)S(1)} %slice_bitcast_fusion.refs_1_.refs_0_), channel_id=1, source_target_pairs={{449,448},{453,452},{457,456},{461,460},{465,464},{469,468},{473,4... | collective-permute-start | bytes 86024 | tf_op jit(solution)/shard_map/ppermute | solution.py:287
  79.3 5.5 %collective-permute-start.4 = (bf16[7,16,128]{2,1,0:T(8,128)(2,1)S(1)}, bf16[7,16,128]{2,1,0:T(8,128)(2,1)S(1)}, u32[]{:S(2)}, u32[]{:S(2)}) collective-permute-start(bf16[7,16,128]{2,1,0:T(8,128)(2,1)S(1)} %slice_bitcast_fusion.refs_1_.refs_0_), channel_id=1, source_target_pairs={{448,449},{452,453},{456,457},{460,461},{464,465},{468,469},{472,4... | collective-permute-start | bytes 86024 | tf_op jit(solution)/shard_map/ppermute | solution.py:287
  89.2 5.2 %collective-permute-start.6 = (bf16[4,1392,128]{2,1,0:T(8,128)(2,1)S(1)}, bf16[4,1392,128]{2,1,0:T(8,128)(2,1)S(1)}, u32[]{:S(2)}, u32[]{:S(2)}) collective-permute-start(bf16[4,1392,128]{2,1,0:T(8,128)(2,1)S(1)} %pad_maximum_fusion.own_ref), channel_id=1, source_target_pairs={{0,4},{4,0},{8,12},{12,8},{16,20},{20,16},{24,28},{28,24},{32,36},... | collective-permute-start | bytes 4276232 | tf_op jit(solution)/shard_map/ppermute | solution.py:315
  95.4 7.6 %collective-permute-start.8 = (bf16[7,16,128]{2,1,0:T(8,128)(2,1)S(1)}, bf16[7,16,128]{2,1,0:T(8,128)(2,1)S(1)}, u32[]{:S(2)}, u32[]{:S(2)}) collective-permute-start(bf16[7,16,128]{2,1,0:T(8,128)(2,1)S(1)} %shard_map.60.refs_1_.refs_0_), channel_id=1, source_target_pairs={{449,448},{453,452},{457,456},{461,460},{465,464},{469,468},{473,4... | collective-permute-start | bytes 86024 | tf_op jit(solution)/shard_map/ppermute | solution.py:287
  97.4 6.6 %collective-permute-start.7 = (bf16[7,16,128]{2,1,0:T(8,128)(2,1)S(1)}, bf16[7,16,128]{2,1,0:T(8,128)(2,1)S(1)}, u32[]{:S(2)}, u32[]{:S(2)}) collective-permute-start(bf16[7,16,128]{2,1,0:T(8,128)(2,1)S(1)} %shard_map.60.refs_1_.refs_0_), channel_id=1, source_target_pairs={{448,449},{452,453},{456,457},{460,461},{464,465},{468,469},{472,4... | collective-permute-start | bytes 86024 | tf_op jit(solution)/shard_map/ppermute | solution.py:287
  105.0 6.8 %collective-permute-start.10 = (bf16[7,16,128]{2,1,0:T(8,128)(2,1)S(1)}, bf16[7,16,128]{2,1,0:T(8,128)(2,1)S(1)}, u32[]{:S(2)}, u32[]{:S(2)}) collective-permute-start(bf16[7,16,128]{2,1,0:T(8,128)(2,1)S(1)} %shard_map.61.refs_1_.refs_0_.refs_2_), channel_id=1, source_target_pairs={{449,448},{453,452},{457,456},{461,460},{465,464},{469,468},{473,4... | collective-permute-start | bytes 86024 | tf_op jit(solution)/shard_map/ppermute | solution.py:287
  106.9 5.8 %collective-permute-start.9 = (bf16[7,16,128]{2,1,0:T(8,128)(2,1)S(1)}, bf16[7,16,128]{2,1,0:T(8,128)(2,1)S(1)}, u32[]{:S(2)}, u32[]{:S(2)}) collective-permute-start(bf16[7,16,128]{2,1,0:T(8,128)(2,1)S(1)} %shard_map.61.refs_1_.refs_0_.refs_2_), channel_id=1, source_target_pairs={{448,449},{452,453},{456,457},{460,461},{464,465},{468,469},{472,4... | collective-permute-start | bytes 86024 | tf_op jit(solution)/shard_map/ppermute | solution.py:287
  113.7 6.8 %collective-permute-start.12 = (bf16[7,16,128]{2,1,0:T(8,128)(2,1)S(1)}, bf16[7,16,128]{2,1,0:T(8,128)(2,1)S(1)}, u32[]{:S(2)}, u32[]{:S(2)}) collective-permute-start(bf16[7,16,128]{2,1,0:T(8,128)(2,1)S(1)} %shard_map.62.refs_1_.refs_0_.refs_3_), channel_id=1, source_target_pairs={{449,448},{453,452},{457,456},{461,460},{465,464},{469,468},{473,4... | collective-permute-start | bytes 86024 | tf_op jit(solution)/shard_map/ppermute | solution.py:287
  115.6 5.8 %collective-permute-start.11 = (bf16[7,16,128]{2,1,0:T(8,128)(2,1)S(1)}, bf16[7,16,128]{2,1,0:T(8,128)(2,1)S(1)}, u32[]{:S(2)}, u32[]{:S(2)}) collective-permute-start(bf16[7,16,128]{2,1,0:T(8,128)(2,1)S(1)} %shard_map.62.refs_1_.refs_0_.refs_3_), channel_id=1, source_target_pairs={{448,449},{452,453},{456,457},{460,461},{464,465},{468,469},{472,4... | collective-permute-start | bytes 86024 | tf_op jit(solution)/shard_map/ppermute | solution.py:287
  122.4 6.8 %collective-permute-start.14 = (bf16[7,16,128]{2,1,0:T(8,128)(2,1)S(1)}, bf16[7,16,128]{2,1,0:T(8,128)(2,1)S(1)}, u32[]{:S(2)}, u32[]{:S(2)}) collective-permute-start(bf16[7,16,128]{2,1,0:T(8,128)(2,1)S(1)} %shard_map.63.refs_1_.refs_0_.refs_4_), channel_id=1, source_target_pairs={{449,448},{453,452},{457,456},{461,460},{465,464},{469,468},{473,4... | collective-permute-start | bytes 86024 | tf_op jit(solution)/shard_map/ppermute | solution.py:287
  124.4 5.8 %collective-permute-start.13 = (bf16[7,16,128]{2,1,0:T(8,128)(2,1)S(1)}, bf16[7,16,128]{2,1,0:T(8,128)(2,1)S(1)}, u32[]{:S(2)}, u32[]{:S(2)}) collective-permute-start(bf16[7,16,128]{2,1,0:T(8,128)(2,1)S(1)} %shard_map.63.refs_1_.refs_0_.refs_4_), channel_id=1, source_target_pairs={{448,449},{452,453},{456,457},{460,461},{464,465},{468,469},{472,4... | collective-permute-start | bytes 86024 | tf_op jit(solution)/shard_map/ppermute | solution.py:287
  131.2 6.8 %collective-permute-start.16 = (bf16[7,16,128]{2,1,0:T(8,128)(2,1)S(1)}, bf16[7,16,128]{2,1,0:T(8,128)(2,1)S(1)}, u32[]{:S(2)}, u32[]{:S(2)}) collective-permute-start(bf16[7,16,128]{2,1,0:T(8,128)(2,1)S(1)} %shard_map.64.refs_1_.refs_0_.refs_5_), channel_id=1, source_target_pairs={{449,448},{453,452},{457,456},{461,460},{465,464},{469,468},{473,4... | collective-permute-start | bytes 86024 | tf_op jit(solution)/shard_map/ppermute | solution.py:287
  133.1 5.8 %collective-permute-start.15 = (bf16[7,16,128]{2,1,0:T(8,128)(2,1)S(1)}, bf16[7,16,128]{2,1,0:T(8,128)(2,1)S(1)}, u32[]{:S(2)}, u32[]{:S(2)}) collective-permute-start(bf16[7,16,128]{2,1,0:T(8,128)(2,1)S(1)} %shard_map.64.refs_1_.refs_0_.refs_5_), channel_id=1, source_target_pairs={{448,449},{452,453},{456,457},{460,461},{464,465},{468,469},{472,4... | collective-permute-start | bytes 86024 | tf_op jit(solution)/shard_map/ppermute | solution.py:287
  139.9 6.8 %collective-permute-start.18 = (bf16[7,16,128]{2,1,0:T(8,128)(2,1)S(1)}, bf16[7,16,128]{2,1,0:T(8,128)(2,1)S(1)}, u32[]{:S(2)}, u32[]{:S(2)}) collective-permute-start(bf16[7,16,128]{2,1,0:T(8,128)(2,1)S(1)} %shard_map.65.refs_1_.refs_0_.refs_6_), channel_id=1, source_target_pairs={{449,448},{453,452},{457,456},{461,460},{465,464},{469,468},{473,4... | collective-permute-start | bytes 86024 | tf_op jit(solution)/shard_map/ppermute | solution.py:287
  141.8 5.8 %collective-permute-start.17 = (bf16[7,16,128]{2,1,0:T(8,128)(2,1)S(1)}, bf16[7,16,128]{2,1,0:T(8,128)(2,1)S(1)}, u32[]{:S(2)}, u32[]{:S(2)}) collective-permute-start(bf16[7,16,128]{2,1,0:T(8,128)(2,1)S(1)} %shard_map.65.refs_1_.refs_0_.refs_6_), channel_id=1, source_target_pairs={{448,449},{452,453},{456,457},{460,461},{464,465},{468,469},{472,4... | collective-permute-start | bytes 86024 | tf_op jit(solution)/shard_map/ppermute | solution.py:287
  149.1 6.8 %collective-permute-start.20 = (bf16[7,16,128]{2,1,0:T(8,128)(2,1)S(1)}, bf16[7,16,128]{2,1,0:T(8,128)(2,1)S(1)}, u32[]{:S(2)}, u32[]{:S(2)}) collective-permute-start(bf16[7,16,128]{2,1,0:T(8,128)(2,1)S(1)} %get-tuple-element.54), channel_id=1, source_target_pairs={{449,448},{453,452},{457,456},{461,460},{465,464},{469,468},{473,4... | collective-permute-start | bytes 86024 | tf_op jit(solution)/shard_map/ppermute | solution.py:287
  151.1 5.8 %collective-permute-start.19 = (bf16[7,16,128]{2,1,0:T(8,128)(2,1)S(1)}, bf16[7,16,128]{2,1,0:T(8,128)(2,1)S(1)}, u32[]{:S(2)}, u32[]{:S(2)}) collective-permute-start(bf16[7,16,128]{2,1,0:T(8,128)(2,1)S(1)} %get-tuple-element.55), channel_id=1, source_target_pairs={{448,449},{452,453},{456,457},{460,461},{464,465},{468,469},{472,4... | collective-permute-start | bytes 86024 | tf_op jit(solution)/shard_map/ppermute | solution.py:287
  158.0 6.8 %collective-permute-start.22 = (bf16[7,16,128]{2,1,0:T(8,128)(2,1)S(1)}, bf16[7,16,128]{2,1,0:T(8,128)(2,1)S(1)}, u32[]{:S(2)}, u32[]{:S(2)}) collective-permute-start(bf16[7,16,128]{2,1,0:T(8,128)(2,1)S(1)} %get-tuple-element.52), channel_id=1, source_target_pairs={{449,448},{453,452},{457,456},{461,460},{465,464},{469,468},{473,4... | collective-permute-start | bytes 86024 | tf_op jit(solution)/shard_map/ppermute | solution.py:287
  160.0 5.8 %collective-permute-start.21 = (bf16[7,16,128]{2,1,0:T(8,128)(2,1)S(1)}, bf16[7,16,128]{2,1,0:T(8,128)(2,1)S(1)}, u32[]{:S(2)}, u32[]{:S(2)}) collective-permute-start(bf16[7,16,128]{2,1,0:T(8,128)(2,1)S(1)} %get-tuple-element.53), channel_id=1, source_target_pairs={{448,449},{452,453},{456,457},{460,461},{464,465},{468,469},{472,4... | collective-permute-start | bytes 86024 | tf_op jit(solution)/shard_map/ppermute | solution.py:287
  166.9 6.8 %collective-permute-start.24 = (bf16[7,16,128]{2,1,0:T(8,128)(2,1)S(1)}, bf16[7,16,128]{2,1,0:T(8,128)(2,1)S(1)}, u32[]{:S(2)}, u32[]{:S(2)}) collective-permute-start(bf16[7,16,128]{2,1,0:T(8,128)(2,1)S(1)} %get-tuple-element.50), channel_id=1, source_target_pairs={{449,448},{453,452},{457,456},{461,460},{465,464},{469,468},{473,4... | collective-permute-start | bytes 86024 | tf_op jit(solution)/shard_map/ppermute | solution.py:287
  168.8 6.0 %collective-permute-start.23 = (bf16[7,16,128]{2,1,0:T(8,128)(2,1)S(1)}, bf16[7,16,128]{2,1,0:T(8,128)(2,1)S(1)}, u32[]{:S(2)}, u32[]{:S(2)}) collective-permute-start(bf16[7,16,128]{2,1,0:T(8,128)(2,1)S(1)} %get-tuple-element.51), channel_id=1, source_target_pairs={{448,449},{452,453},{456,457},{460,461},{464,465},{468,469},{472,4... | collective-permute-start | bytes 86024 | tf_op jit(solution)/shard_map/ppermute | solution.py:287
  175.9 7.3 %collective-permute-start.26 = (bf16[7,16,128]{2,1,0:T(8,128)(2,1)S(1)}, bf16[7,16,128]{2,1,0:T(8,128)(2,1)S(1)}, u32[]{:S(2)}, u32[]{:S(2)}) collective-permute-start(bf16[7,16,128]{2,1,0:T(8,128)(2,1)S(1)} %get-tuple-element.48), channel_id=1, source_target_pairs={{449,448},{453,452},{457,456},{461,460},{465,464},{469,468},{473,4... | collective-permute-start | bytes 86024 | tf_op jit(solution)/shard_map/ppermute | solution.py:287
  177.8 6.3 %collective-permute-start.25 = (bf16[7,16,128]{2,1,0:T(8,128)(2,1)S(1)}, bf16[7,16,128]{2,1,0:T(8,128)(2,1)S(1)}, u32[]{:S(2)}, u32[]{:S(2)}) collective-permute-start(bf16[7,16,128]{2,1,0:T(8,128)(2,1)S(1)} %get-tuple-element.49), channel_id=1, source_target_pairs={{448,449},{452,453},{456,457},{460,461},{464,465},{468,469},{472,4... | collective-permute-start | bytes 86024 | tf_op jit(solution)/shard_map/ppermute | solution.py:287
  185.3 6.8 %collective-permute-start.28 = (bf16[7,16,128]{2,1,0:T(8,128)(2,1)S(1)}, bf16[7,16,128]{2,1,0:T(8,128)(2,1)S(1)}, u32[]{:S(2)}, u32[]{:S(2)}) collective-permute-start(bf16[7,16,128]{2,1,0:T(8,128)(2,1)S(1)} %get-tuple-element.46), channel_id=1, source_target_pairs={{449,448},{453,452},{457,456},{461,460},{465,464},{469,468},{473,4... | collective-permute-start | bytes 86024 | tf_op jit(solution)/shard_map/ppermute | solution.py:287
  187.2 5.8 %collective-permute-start.27 = (bf16[7,16,128]{2,1,0:T(8,128)(2,1)S(1)}, bf16[7,16,128]{2,1,0:T(8,128)(2,1)S(1)}, u32[]{:S(2)}, u32[]{:S(2)}) collective-permute-start(bf16[7,16,128]{2,1,0:T(8,128)(2,1)S(1)} %get-tuple-element.47), channel_id=1, source_target_pairs={{448,449},{452,453},{456,457},{460,461},{464,465},{468,469},{472,4... | collective-permute-start | bytes 86024 | tf_op jit(solution)/shard_map/ppermute | solution.py:287
  194.1 6.8 %collective-permute-start.30 = (bf16[7,16,128]{2,1,0:T(8,128)(2,1)S(1)}, bf16[7,16,128]{2,1,0:T(8,128)(2,1)S(1)}, u32[]{:S(2)}, u32[]{:S(2)}) collective-permute-start(bf16[7,16,128]{2,1,0:T(8,128)(2,1)S(1)} %get-tuple-element.44), channel_id=1, source_target_pairs={{449,448},{453,452},{457,456},{461,460},{465,464},{469,468},{473,4... | collective-permute-start | bytes 86024 | tf_op jit(solution)/shard_map/ppermute | solution.py:287
  196.1 5.8 %collective-permute-start.29 = (bf16[7,16,128]{2,1,0:T(8,128)(2,1)S(1)}, bf16[7,16,128]{2,1,0:T(8,128)(2,1)S(1)}, u32[]{:S(2)}, u32[]{:S(2)}) collective-permute-start(bf16[7,16,128]{2,1,0:T(8,128)(2,1)S(1)} %get-tuple-element.45), channel_id=1, source_target_pairs={{448,449},{452,453},{456,457},{460,461},{464,465},{468,469},{472,4... | collective-permute-start | bytes 86024 | tf_op jit(solution)/shard_map/ppermute | solution.py:287
  203.0 71.3 %copy-start.1 = (bf16[14,64,64]{2,1,0:T(8,128)(2,1)S(1)}, bf16[14,64,64]{2,1,0:T(8,128)(2,1)}, u32[]{:S(2)}) copy-start(bf16[14,64,64]{2,1,0:T(8,128)(2,1)} %diag_ref.3) | copy-start | bytes 344068
  203.0 6.9 %collective-permute-start.32 = (bf16[7,16,128]{2,1,0:T(8,128)(2,1)S(1)}, bf16[7,16,128]{2,1,0:T(8,128)(2,1)S(1)}, u32[]{:S(2)}, u32[]{:S(2)}) collective-permute-start(bf16[7,16,128]{2,1,0:T(8,128)(2,1)S(1)} %get-tuple-element.42), channel_id=1, source_target_pairs={{449,448},{453,452},{457,456},{461,460},{465,464},{469,468},{473,4... | collective-permute-start | bytes 86024 | tf_op jit(solution)/shard_map/ppermute | solution.py:287
  205.1 5.8 %collective-permute-start.31 = (bf16[7,16,128]{2,1,0:T(8,128)(2,1)S(1)}, bf16[7,16,128]{2,1,0:T(8,128)(2,1)S(1)}, u32[]{:S(2)}, u32[]{:S(2)}) collective-permute-start(bf16[7,16,128]{2,1,0:T(8,128)(2,1)S(1)} %get-tuple-element.43), channel_id=1, source_target_pairs={{448,449},{452,453},{456,457},{460,461},{464,465},{468,469},{472,4... | collective-permute-start | bytes 86024 | tf_op jit(solution)/shard_map/ppermute | solution.py:287
  236.3 38.0 %collective-permute-start.33 = (bf16[8,2,7,16,128]{4,3,2,1,0:T(8,128)(2,1)S(1)}, bf16[8,2,7,16,128]{4,3,2,1,0:T(8,128)(2,1)S(1)}, u32[]{:S(2)}, u32[]{:S(2)}) collective-permute-start(bf16[8,2,7,16,128]{4,3,2,1,0:T(8,128)(2,1)S(1)} %all_to_all.10), channel_id=1, source_target_pairs={{448,416},{449,417},{450,418},{451,419},{507,420},{506,421},{505,4... | collective-permute-start | bytes 1376264 | tf_op jit(solution)/shard_map/ppermute | solution.py:355

commit v3 on v2

--- a/solution.py
+++ b/solution.py
@@ -15,6 +15,7 @@
 ORDER = 64
 COLS = 128
 PART = 16
+BOTH = 2 * PART
 WINDOW = LINKS * SLOTS
 ROTATION = 96
 PLANES = 16
@@ -33,11 +34,11 @@
 
 
 def slot_of(band, turn):
-    return (turn - band) % 4 * 2 + turn // 4
+    return (turn - band) % 4 * 2 + 1 - turn // 4
 
 
 def turn_of_slot(slot, shift):
-    return (slot // 2 + shift) % 4 + slot % 2 * 4
+    return (slot // 2 + shift) % 4 + (1 - slot % 2) * 4
 
 
 def place_slot(rank, slot):
@@ -54,10 +55,10 @@
     return (level * RANKS + rank - ROTATION) % (LEVELS * RANKS)
 
 
-def level_pairs():
+def level_pairs(first=0):
     return [
         (native(level, rank), place(rank, level))
-        for level in range(LEVELS)
+        for level in range(first, LEVELS)
         for rank in range(RANKS)
     ]
 
@@ -67,7 +68,7 @@
         (place_slot(rank, slot), place_slot(rank + step, slot))
         for rank in range(RANKS)
         if 0 <= rank + step < RANKS
-        for slot in range(COLS // PART)
+        for slot in range(1, COLS // PART, 2)
     ]
 
 
@@ -81,7 +82,7 @@
     return lax.broadcasted_iota(jnp.int32, shape, len(shape) - 1) < ORDER
 
 
-def call(kernel, outs, operands, scratch=(), scalars=0):
+def call(kernel, outs, operands, scratch=(), scalars=0, cost=None):
     return pl.pallas_call(
         kernel,
         out_shape=[jax.ShapeDtypeStruct(shape, dtype) for shape, dtype in outs],
@@ -91,6 +92,7 @@
         out_specs=[pl.BlockSpec(memory_space=VMEM) for _ in outs],
         scratch_shapes=list(scratch),
         compiler_params=pltpu.CompilerParams(vmem_limit_bytes=16 * 1024 * 1024),
+        cost_estimate=cost,
     )(*operands)
 
 
@@ -100,14 +102,26 @@
         ref[start : start + values.shape[0], :] = values[:, part * 128 : (part + 1) * 128]
 
 
-def prepare_kernel(shift_ref, pattern_ref, rhs_ref, factor_ref, diag_ref, out_ref):
+def prepare_kernel(
+    shift_ref, pattern_ref, rhs_hbm, factor_hbm, diag_hbm, out_ref, rhs_t_ref, rhs_ref, factor_ref, diag_ref, sems
+):
+    arrays = ((diag_hbm, diag_ref), (rhs_hbm, rhs_ref), (factor_hbm, factor_ref))
+    copies = []
+    for half in range(2):
+        rows = pl.ds(half * PAIRS, PAIRS)
+        for n, (source, target) in enumerate(arrays):
+            copies.append(pltpu.make_async_copy(source.at[rows], target.at[rows], sems.at[half * 3 + n]))
+    for copy in copies:
+        copy.start()
     lane = lax.broadcasted_iota(jnp.int32, (16, WIDE), 1)
     entries = jnp.zeros((16, WIDE), jnp.int32)
     for n in range(SLOTS):
         for m in range(LINKS):
-            entry = jnp.clip(pattern_ref[n, m], 0, WINDOW - 1)
+            entry = jnp.clip(pattern_ref[m, n], 0, WINDOW - 1)
             entries = jnp.where(lane == LINKS * n + m, entry, entries)
     entries = entries.astype(F32).astype(BF16)
+    for copy in copies:
+        copy.wait()
     for i in range(PAIRS):
         couplings, sides = [], []
         for n in (i, i + PAIRS):
@@ -119,8 +133,7 @@
         put_block(out_ref, i * ORDER, both)
         turned = jnp.concatenate(sides, axis=0).T.astype(BF16)
         for j in range(COLS // PART):
-            row = SHARD + turn_of_slot(j, shift_ref[0]) * PIECE + i * PART
-            out_ref[pl.ds(pl.multiple_of(row, 16), PART), :] = turned[j * PART : (j + 1) * PART, :]
+            rhs_t_ref[turn_of_slot(j, shift_ref[0]), i] = turned[j * PART : (j + 1) * PART, :]
     put_block(out_ref, ROWS, entries)
 
 
@@ -140,6 +153,10 @@
                     ).astype(BF16)
 
 
+def copy_kernel(source_ref, out_ref):
+    out_ref[...] = source_ref[...]
+
+
 def put_window(window_ref, source_ref, base):
     for i in range(PAIRS):
         pair = source_ref[i].astype(F32)
@@ -149,29 +166,20 @@
         window_ref[base + PAIRS + i] = jnp.where(left, swapped, pair).astype(BF16)
 
 
-def level_weights(level, state_ref, own_ref, other_ref):
-    mine = state_ref[1] == level // 4
-    index = shard_index(state_ref, level)
-
+def level_weights(index, shards_ref):
     def weights(i):
-        parts = []
-        for part in range(LINKS):
-            rows = pl.ds(part * BLOCK + i * ORDER, ORDER)
-            parts.append(jnp.where(mine, own_ref[index, rows, :], other_ref[index, rows, :]))
-        return jnp.concatenate(parts, axis=1)
+        return jnp.concatenate(
+            [shards_ref[index, pl.ds(part * BLOCK + i * ORDER, ORDER), :] for part in range(LINKS)], axis=1
+        )
 
     return weights
 
 
-def shard_index(state_ref, level):
-    return (state_ref[0] + LEVELS - level) & 3
-
-
-def forward_pair(pattern_ref, level, index, weights, window_ref, rhs_ref, i):
+def forward_pair(pattern, level, weights, window_ref, rhs_ref, i):
     w = weights(i)
     sums = []
     for n in (i, i + PAIRS):
-        a, b, c = (window_ref[pattern_ref[index, LINKS * n + m]] for m in range(LINKS))
+        a, b, c = (window_ref[pattern(n, m)] for m in range(LINKS))
         left = left_lanes(a.shape)
         zero = jnp.zeros_like(a)
         if n < PAIRS:
@@ -195,28 +203,28 @@
     put_window(window_ref, above_ref, 2 * SLOTS)
 
 
-def level_kernel(level, step, state_ref, pattern_ref, own_ref, other_ref, *refs):
-    weights = level_weights(level, state_ref, own_ref, other_ref)
-    index = shard_index(state_ref, level) + 4 * (state_ref[1] != level // 4).astype(jnp.int32)
-    step(pattern_ref, level, index, weights, *refs)
+def level_kernel(level, step, table_ref, shards_ref, *refs):
+    index = (table_ref[0, 0] + LEVELS - level) & 3
+    row = table_ref[pl.ds(index, 1), :]
+    step(lambda n, m: row[0, 1 + LINKS * n + m], level, level_weights(index, shards_ref), *refs)
 
 
 def forward_step(
-    pattern_ref, level, index, weights, rhs_ref, own_ref, below_ref, above_ref, out_ref, window_ref
+    pattern, level, weights, rhs_ref, own_ref, below_ref, above_ref, out_ref, window_ref
 ):
     fill_window(window_ref, own_ref, below_ref, above_ref)
     for i in range(PAIRS):
-        out_ref[i] = forward_pair(pattern_ref, level, index, weights, window_ref, rhs_ref, i)
-
-
-def spread(pattern_ref, index, weights, reduced, sums_ref, total_ref):
+        out_ref[i] = forward_pair(pattern, level, weights, window_ref, rhs_ref, i)
+
+
+def spread(pattern, weights, reduced, sums_ref, total_ref):
     for q in range(WINDOW):
         total_ref[q] = jnp.zeros(total_ref.shape[1:], F32)
     for i in range(PAIRS):
         pair = reduced[i].astype(F32)
         rows = jnp.concatenate([pair, pltpu.roll(pair, ORDER, 1)], axis=0)[:, :ORDER].astype(BF16)
         products = jnp.dot(rows, weights(i), preferred_element_type=F32)
-        for n, product in ((i, products[:PART, :256]), (i + PAIRS, products[PART:, 128:])):
+        for n, product in ((i, products[:BOTH, :256]), (i + PAIRS, products[BOTH:, 128:])):
             head, tail = product[:, :128], product[:, 128:]
             left = left_lanes(head.shape)
             zero = jnp.zeros_like(head)
@@ -225,7 +233,7 @@
             else:
                 terms = (jnp.where(left, zero, head), jnp.where(left, tail, zero), jnp.where(left, zero, tail))
             for m in range(LINKS):
-                total_ref[pattern_ref[index, LINKS * n + m]] += terms[m]
+                total_ref[pattern(n, m)] += terms[m]
     for part in range(LINKS):
         for i in range(PAIRS):
             one = total_ref[part * SLOTS + i]
@@ -237,15 +245,15 @@
 
 
 def turn_step(
-    pattern_ref, level, index, weights, rhs_ref, own_ref, below_ref, above_ref,
+    pattern, level, weights, rhs_ref, own_ref, below_ref, above_ref,
     out_ref, sums_ref, window_ref, total_ref,
 ):
     fill_window(window_ref, own_ref, below_ref, above_ref)
     solved = []
     for i in range(PAIRS):
-        solved.append(forward_pair(pattern_ref, level, index, weights, window_ref, rhs_ref, i))
+        solved.append(forward_pair(pattern, level, weights, window_ref, rhs_ref, i))
         out_ref[i] = solved[i]
-    spread(pattern_ref, index, weights, solved, sums_ref, total_ref)
+    spread(pattern, weights, solved, sums_ref, total_ref)
 
 
 def reduce(forward_ref, own_ref, below_ref, above_ref, out_ref):
@@ -258,19 +266,21 @@
 
 
 def backward_step(
-    pattern_ref, level, index, weights, forward_ref, own_ref, below_ref, above_ref, out_ref, sums_ref, total_ref
+    pattern, level, weights, forward_ref, own_ref, below_ref, above_ref, out_ref, sums_ref, total_ref
 ):
     reduced = reduce(forward_ref, own_ref, below_ref, above_ref, out_ref)
-    spread(pattern_ref, index, weights, reduced, sums_ref, total_ref)
+    spread(pattern, weights, reduced, sums_ref, total_ref)
 
 
 def last_kernel(sums_ref, below_ref, above_ref, *refs):
-    forward, reduced, packed_ref = refs[:LEVELS], refs[LEVELS:-1], refs[-1]
-    for level in range(LEVELS):
-        packed_ref[level, 0] = forward[level][...]
-        if level > 0:
-            packed_ref[level, 1] = reduced[level - 1][...]
-    reduce(forward[0], sums_ref, below_ref, above_ref, packed_ref.at[0, 1])
+    forward, reduced, last_ref = refs[:LEVELS], refs[LEVELS:-3], refs[-1]
+    reduce(forward[0], sums_ref, below_ref, above_ref, last_ref)
+    for core in range(2):
+        columns = pl.ds(core * PART, PART)
+        for level in range(LEVELS):
+            refs[core - 3][level, 0] = forward[level][:, columns, :]
+            back_ref = reduced[level - 1] if level else last_ref
+            refs[core - 3][level, 1] = back_ref[:, columns, :]
 
 
 def per_device(right_side, factor_blocks, diag_inverse, pattern):
@@ -278,10 +288,10 @@
     to_group = level_pairs()
     to_native = [(b, a) for a, b in to_group]
     groups = group_list()
-    solved_shape = ((PAIRS, PART, 128), BF16)
-    sums_shape = ((LINKS, PAIRS, PART, 128), BF16)
-    window = VMEM((WINDOW, PART, 128), BF16)
-    total = VMEM((WINDOW, PART, 128), F32)
+    solved_shape = ((PAIRS, BOTH, 128), BF16)
+    sums_shape = ((LINKS, PAIRS, BOTH, 128), BF16)
+    window = VMEM((WINDOW, BOTH, 128), BF16)
+    total = VMEM((WINDOW, BOTH, 128), F32)
 
     def exchange(to_above, to_below):
         return lax.ppermute(to_above, AXES, up), lax.ppermute(to_below, AXES, down)
@@ -289,35 +299,55 @@
     lvl = lax.axis_index("lvl")
     plane, x, core = lvl // 8, lvl % 8 // 2, lvl % 2
     band = (plane - PLANE_OF[0]) % PLANES
-    state = jnp.stack([(x + band) % 4, core]).astype(jnp.int32)
+    state = ((x + band) % 4).astype(jnp.int32).reshape(1)
     shift = ((x * 2 + core) % 4).astype(jnp.int32).reshape(1)
 
-    (prepared,) = call(
+    stored = (right_side, factor_blocks, diag_inverse)
+    weights, rhs = pl.pallas_call(
         prepare_kernel,
-        [((SHARD + COLS // PART * PIECE, 128), BF16)],
-        (shift, pattern, right_side, factor_blocks, diag_inverse),
-        scalars=2,
-    )
-    prepared = lax.ppermute(prepared, AXES, to_group)
-    weights, rhs = prepared[:SHARD], prepared[SHARD:].reshape(LEVELS, PAIRS, PART, 128)
-
-    def along_x(steps):
-        pairs = [(i, i // 8 * 8 + (i % 8 + 2 * steps) % 8) for i in range(128)]
-        return lax.ppermute(weights, "lvl", pairs)
-
-    gathered = (along_x(1), along_x(2), along_x(3))
+        out_shape=[
+            jax.ShapeDtypeStruct((SHARD, 128), BF16),
+            jax.ShapeDtypeStruct((LEVELS, PAIRS, PART, 128), BF16),
+        ],
+        in_specs=[pl.BlockSpec(memory_space=pltpu.SMEM)] * 2 + [pl.BlockSpec(memory_space=pltpu.HBM)] * 3,
+        out_specs=[pl.BlockSpec(memory_space=VMEM)] * 2,
+        scratch_shapes=[VMEM(array.shape, BF16) for array in stored] + [pltpu.SemaphoreType.DMA((6,))],
+        compiler_params=pltpu.CompilerParams(vmem_limit_bytes=16 * 1024 * 1024),
+    )(shift, pattern.T, *stored)
+    rhs = lax.ppermute(rhs, AXES, to_group)
+    weights = lax.ppermute(weights, AXES, level_pairs(1))
+    cost = pl.CostEstimate(flops=50 * 10**9, bytes_accessed=SHARD * 512, transcendentals=0)
+    (weights,) = call(copy_kernel, [((SHARD, 128), BF16)], (weights,), cost=cost)
+
+    def along_x(value, core):
+        def moved(steps):
+            pairs = [(i, i // 8 * 8 + (i % 8 + 2 * steps) % 8) for i in range(core, 128, 2)]
+            return lax.ppermute(value, "lvl", pairs)
+
+        return moved(1), moved(2), moved(3)
+
+    to_first = [(i + 1, i) for i in range(0, 128, 2)]
+    to_second = [(i, i + 1) for i in range(0, 128, 2)]
+    low = along_x(weights, 1)
     rhs = lax.all_to_all(rhs, "lvl", 0, 0, axis_index_groups=groups)
+    rhs = jnp.concatenate([lax.ppermute(rhs, "lvl", to_second), rhs], axis=2)
     latest = rhs[0]
     near = exchange(latest, latest)
-    *gathered, below, above = lax.optimization_barrier((*gathered, *near))
+    *low, below, above = lax.optimization_barrier((*low, *near))
     near = (below, above)
-    own = jnp.stack([weights, *gathered])
-    other = lax.ppermute(own, "lvl", [(i, i ^ 1) for i in range(128)])
-    patterns = jnp.concatenate([own[:, ROWS, :WINDOW], other[:, ROWS, :WINDOW]]).astype(jnp.int32)
+    low = jnp.stack([weights, *low])
+    def gather_high(solved):
+        ready = lax.ppermute(solved, "lvl", to_first).reshape(PAIRS * BOTH, 128)
+        shards = jnp.concatenate([weights, ready])
+        return lax.ppermute(jnp.stack([shards, *along_x(shards, 0)]), "lvl", to_second)
 
     def level_call(level, step, arrays, outs, scratch):
         kernel = functools.partial(level_kernel, level, step)
-        return call(kernel, outs, (state, patterns, own, other) + arrays, scratch, scalars=2)
+        shards = high if level >= CHUNK else low
+        patterns = shards[:, ROWS, :WINDOW].astype(jnp.int32)
+        table = jnp.concatenate([jnp.broadcast_to(state, (4, 1)), patterns], axis=1)
+        cost = pl.CostEstimate(flops=20 * 10**9, bytes_accessed=SHARD * 512, transcendentals=0)
+        return call(kernel, outs, (table, shards) + arrays, scratch, cost=cost)
 
     forward = [latest]
     for level in range(1, LEVELS):
@@ -331,6 +361,8 @@
             [window, total] if last else [window],
         )
         forward.append(latest)
+        if level == 1:
+            high = gather_high(latest)
     (sums,) = rest
 
     reduced = [latest]
@@ -345,11 +377,11 @@
         )
         reduced.append(latest)
     below, above = exchange(sums[2], sums[0])
-    (packed,) = call(
-        last_kernel,
-        [((LEVELS, 2, PAIRS, PART, 128), BF16)],
-        (sums, below, above, *forward, *reduced[::-1]),
+    packed_shape = ((LEVELS, 2, PAIRS, PART, 128), BF16)
+    for_first, for_second = call(
+        last_kernel, [packed_shape] * 2, (sums, below, above, *forward, *reduced[::-1]), [VMEM(*solved_shape)]
     )
+    packed = jnp.where(core == 1, for_second, lax.ppermute(for_first, "lvl", to_first))
 
     parts = lax.all_to_all(packed, "lvl", 0, 0, axis_index_groups=groups)
     parts = lax.ppermute(parts, AXES, to_native)

time: 277 us -> 250 us (0.903)
  the two profiles are of different devices: /device:TPU:97 before, /device:TPU:135 now
where the time goes in v3:
time: 250 us; the launch traced here: 249 us
  starting transfers between devices  137 us (55%)
  waiting for transfers between devices  47.4 us (19%)
  blocking collectives  47.4 us (19%)
  Pallas kernels  10.8 us (4%)
  local copies, waits for them, and re-layouts  3.96 us (2%)
    ppermute x14, starting transfers between devices, exchange(): lax.ppermute(to_below, AXES, down)  68.1 us
    all_to_all x1, blocking collectives, per_device(): rhs = lax.all_to_all(rhs, 'lvl', 0, 0, axis_index_groups=groups)  35.1 us
    ppermute x1, waiting for transfers between devices, per_device(): parts = lax.ppermute(parts, AXES, to_native)  31 us
    ppermute x14, starting transfers between devices, exchange(): lax.ppermute(to_above, AXES, up)  26.9 us
    ppermute x1, starting transfers between devices, per_device(): rhs = lax.ppermute(rhs, AXES, to_group)  12.6 us
    all_to_all x1, blocking collectives, per_device(): parts = lax.all_to_all(packed, 'lvl', 0, 0, axis_index_groups=groups)  12.3 us
    ppermute x14, waiting for transfers between devices, exchange(): lax.ppermute(to_below, AXES, down)  12.2 us
    ppermute x1, starting transfers between devices, per_device(): parts = lax.ppermute(parts, AXES, to_native)  10.1 us
  transfers between devices with their start and end apart: 41, of which 14 were waited for; matrix products, arithmetic and copies ran while one was open for 0% of the time, Pallas kernels for 0%

profile of v3, /device:TPU:135, one launch (start us, length us, event | category | flops | bytes accessed | tf_op | source)
XLA Modules:
  0.0 248.9 jit_solution(14782669739814090326)
XLA Ops:
  4.4 2.1 shard_map.59
  6.4 12.6 %collective-permute-start.4 = (bf16[8,7,16,128]{3,2,1,0:T(8,128)(2,1)S(1)}, bf16[8,7,16,128]{3,2,1,0:T(8,128)(2,1)S(1)}, u32[]{:S(2)}, u32[]{:S(2)}) collective-permute-start(bf16[8,7,16,128]{3,2,1,0:T(8,128)(2,1)S(1)} %get-tuple-element.26), channel_id=1, source_target_pairs={{416,452},{417,453},{418,454},{419,455},{420,511},{421,510},{422,5... | collective-permute-start | bytes 688136 | tf_op jit(solution)/shard_map/ppermute | solution.py:317
  19.0 5.0 %collective-permute-start = (bf16[1392,128]{1,0:T(8,128)(2,1)S(1)}, bf16[1392,128]{1,0:T(8,128)(2,1)S(1)}, u32[]{:S(2)}, u32[]{:S(2)}) collective-permute-start(bf16[1392,128]{1,0:T(8,128)(2,1)S(1)} %get-tuple-element.25), channel_id=1, source_target_pairs={{480,460},{481,461},{482,462},{483,463},{484,487},{485,486},{486,4... | collective-permute-start | bytes 1069064 | tf_op jit(solution)/shard_map/ppermute | solution.py:318
  24.0 35.1 %all_to_all.10 = bf16[8,7,16,128]{3,2,1,0:T(8,128)(2,1)S(1)} all-to-all(bf16[8,7,16,128]{3,2,1,0:T(8,128)(2,1)S(1)} %collective-permute-done.4), channel_id=1, replica_groups={{452,460,468,476,448,456,464,472},{508,484,492,500,504,480,488,496},{20..., dimensions={0} | all-to-all | bytes 458752 | tf_op jit(solution)/shard_map/all_to_all | solution.py:332
  59.1 1.3 collective-permute-start.5
  60.4 2.1 collective-permute-start.1
  62.5 3.4 %collective-permute-start.2 = (bf16[1392,128]{1,0:T(8,128)(2,1)S(1)}, bf16[1392,128]{1,0:T(8,128)(2,1)S(1)}, u32[]{:S(2)}, u32[]{:S(2)}) collective-permute-start(bf16[1392,128]{1,0:T(8,128)(2,1)S(1)} %shard_map.60), channel_id=1, source_target_pairs={{4,20},{12,28},{20,4},{28,12},{36,52},{44,60},{52,36},{60,44},{68,... | collective-permute-start | bytes 1069064 | tf_op jit(solution)/shard_map/ppermute | solution.py:325
  65.9 2.0 collective-permute-start.3
  68.0 1.9 collective-permute-start.6
  69.9 4.6 %collective-permute-start.7 = (bf16[7,32,128]{2,1,0:T(8,128)(2,1)S(1)}, bf16[7,32,128]{2,1,0:T(8,128)(2,1)S(1)}, u32[]{:S(2)}, u32[]{:S(2)}) collective-permute-start(bf16[7,32,128]{2,1,0:T(8,128)(2,1)S(1)} %slice_bitcast_fusion.refs_1_.refs_0_), channel_id=1, source_target_pairs={{453,452},{461,460},{469,468},{477,476},{454,453},{462,461},{470,4... | collective-permute-start | bytes 172040 | tf_op jit(solution)/shard_map/ppermute | solution.py:297
  74.6 1.3 collective-permute-done.3
  76.7 1.3 collective-permute-start.12
  78.0 1.9 collective-permute-start.8
  79.9 4.9 %collective-permute-start.9 = (bf16[7,32,128]{2,1,0:T(8,128)(2,1)S(1)}, bf16[7,32,128]{2,1,0:T(8,128)(2,1)S(1)}, u32[]{:S(2)}, u32[]{:S(2)}) collective-permute-start(bf16[7,32,128]{2,1,0:T(8,128)(2,1)S(1)} %shard_map.61.refs_1_.refs_0_), channel_id=1, source_target_pairs={{453,452},{461,460},{469,468},{477,476},{454,453},{462,461},{470,4... | collective-permute-start | bytes 172040 | tf_op jit(solution)/shard_map/ppermute | solution.py:297
  87.5 1.9 collective-permute-start.10
  89.4 4.6 %collective-permute-start.11 = (bf16[7,32,128]{2,1,0:T(8,128)(2,1)S(1)}, bf16[7,32,128]{2,1,0:T(8,128)(2,1)S(1)}, u32[]{:S(2)}, u32[]{:S(2)}) collective-permute-start(bf16[7,32,128]{2,1,0:T(8,128)(2,1)S(1)} %shard_map.62.refs_1_.refs_0_.refs_2_), channel_id=1, source_target_pairs={{453,452},{461,460},{469,468},{477,476},{454,453},{462,461},{470,4... | collective-permute-start | bytes 172040 | tf_op jit(solution)/shard_map/ppermute | solution.py:297
  94.2 1.3 collective-permute-start.16
  96.0 1.9 collective-permute-start.17
  98.0 4.9 %collective-permute-start.18 = (bf16[7,32,128]{2,1,0:T(8,128)(2,1)S(1)}, bf16[7,32,128]{2,1,0:T(8,128)(2,1)S(1)}, u32[]{:S(2)}, u32[]{:S(2)}) collective-permute-start(bf16[7,32,128]{2,1,0:T(8,128)(2,1)S(1)} %shard_map.63.refs_1_.refs_0_.refs_3_), channel_id=1, source_target_pairs={{453,452},{461,460},{469,468},{477,476},{454,453},{462,461},{470,4... | collective-permute-start | bytes 172040 | tf_op jit(solution)/shard_map/ppermute | solution.py:297
  102.8 1.4 collective-permute-done.16.shards_ref
  104.8 1.9 collective-permute-start.19
  106.7 4.9 %collective-permute-start.20 = (bf16[7,32,128]{2,1,0:T(8,128)(2,1)S(1)}, bf16[7,32,128]{2,1,0:T(8,128)(2,1)S(1)}, u32[]{:S(2)}, u32[]{:S(2)}) collective-permute-start(bf16[7,32,128]{2,1,0:T(8,128)(2,1)S(1)} %shard_map.64.refs_1_.refs_0_.refs_4_), channel_id=1, source_target_pairs={{453,452},{461,460},{469,468},{477,476},{454,453},{462,461},{470,4... | collective-permute-start | bytes 172040 | tf_op jit(solution)/shard_map/ppermute | solution.py:297
  111.6 1.2 collective-permute-done.20.refs_3_
  113.3 1.9 collective-permute-start.21
  115.3 4.9 %collective-permute-start.22 = (bf16[7,32,128]{2,1,0:T(8,128)(2,1)S(1)}, bf16[7,32,128]{2,1,0:T(8,128)(2,1)S(1)}, u32[]{:S(2)}, u32[]{:S(2)}) collective-permute-start(bf16[7,32,128]{2,1,0:T(8,128)(2,1)S(1)} %shard_map.65.refs_1_.refs_0_.refs_5_), channel_id=1, source_target_pairs={{453,452},{461,460},{469,468},{477,476},{454,453},{462,461},{470,4... | collective-permute-start | bytes 172040 | tf_op jit(solution)/shard_map/ppermute | solution.py:297
  121.9 1.9 collective-permute-start.23
  123.8 4.9 %collective-permute-start.24 = (bf16[7,32,128]{2,1,0:T(8,128)(2,1)S(1)}, bf16[7,32,128]{2,1,0:T(8,128)(2,1)S(1)}, u32[]{:S(2)}, u32[]{:S(2)}) collective-permute-start(bf16[7,32,128]{2,1,0:T(8,128)(2,1)S(1)} %shard_map.66.refs_1_.refs_0_.refs_6_), channel_id=1, source_target_pairs={{453,452},{461,460},{469,468},{477,476},{454,453},{462,461},{470,4... | collective-permute-start | bytes 172040 | tf_op jit(solution)/shard_map/ppermute | solution.py:297
  128.7 1.2 collective-permute-done.24.refs_3_
  131.0 1.9 collective-permute-start.25
  133.0 4.9 %collective-permute-start.26 = (bf16[7,32,128]{2,1,0:T(8,128)(2,1)S(1)}, bf16[7,32,128]{2,1,0:T(8,128)(2,1)S(1)}, u32[]{:S(2)}, u32[]{:S(2)}) collective-permute-start(bf16[7,32,128]{2,1,0:T(8,128)(2,1)S(1)} %get-tuple-element.62), channel_id=1, source_target_pairs={{453,452},{461,460},{469,468},{477,476},{454,453},{462,461},{470,4... | collective-permute-start | bytes 172040 | tf_op jit(solution)/shard_map/ppermute | solution.py:297
  137.9 1.2 collective-permute-done.26.refs_3_
  139.7 1.9 collective-permute-start.27
  141.7 4.9 %collective-permute-start.28 = (bf16[7,32,128]{2,1,0:T(8,128)(2,1)S(1)}, bf16[7,32,128]{2,1,0:T(8,128)(2,1)S(1)}, u32[]{:S(2)}, u32[]{:S(2)}) collective-permute-start(bf16[7,32,128]{2,1,0:T(8,128)(2,1)S(1)} %get-tuple-element.60), channel_id=1, source_target_pairs={{453,452},{461,460},{469,468},{477,476},{454,453},{462,461},{470,4... | collective-permute-start | bytes 172040 | tf_op jit(solution)/shard_map/ppermute | solution.py:297
  148.4 1.9 collective-permute-start.29
  150.4 4.9 %collective-permute-start.30 = (bf16[7,32,128]{2,1,0:T(8,128)(2,1)S(1)}, bf16[7,32,128]{2,1,0:T(8,128)(2,1)S(1)}, u32[]{:S(2)}, u32[]{:S(2)}) collective-permute-start(bf16[7,32,128]{2,1,0:T(8,128)(2,1)S(1)} %get-tuple-element.58), channel_id=1, source_target_pairs={{453,452},{461,460},{469,468},{477,476},{454,453},{462,461},{470,4... | collective-permute-start | bytes 172040 | tf_op jit(solution)/shard_map/ppermute | solution.py:297
  157.1 1.9 collective-permute-start.31
  159.1 4.9 %collective-permute-start.32 = (bf16[7,32,128]{2,1,0:T(8,128)(2,1)S(1)}, bf16[7,32,128]{2,1,0:T(8,128)(2,1)S(1)}, u32[]{:S(2)}, u32[]{:S(2)}) collective-permute-start(bf16[7,32,128]{2,1,0:T(8,128)(2,1)S(1)} %get-tuple-element.56), channel_id=1, source_target_pairs={{453,452},{461,460},{469,468},{477,476},{454,453},{462,461},{470,4... | collective-permute-start | bytes 172040 | tf_op jit(solution)/shard_map/ppermute | solution.py:297
  165.8 1.9 collective-permute-start.33
  167.8 5.0 %collective-permute-start.34 = (bf16[7,32,128]{2,1,0:T(8,128)(2,1)S(1)}, bf16[7,32,128]{2,1,0:T(8,128)(2,1)S(1)}, u32[]{:S(2)}, u32[]{:S(2)}) collective-permute-start(bf16[7,32,128]{2,1,0:T(8,128)(2,1)S(1)} %get-tuple-element.54), channel_id=1, source_target_pairs={{453,452},{461,460},{469,468},{477,476},{454,453},{462,461},{470,4... | collective-permute-start | bytes 172040 | tf_op jit(solution)/shard_map/ppermute | solution.py:297
  174.7 1.9 collective-permute-start.35
  176.6 5.0 %collective-permute-start.36 = (bf16[7,32,128]{2,1,0:T(8,128)(2,1)S(1)}, bf16[7,32,128]{2,1,0:T(8,128)(2,1)S(1)}, u32[]{:S(2)}, u32[]{:S(2)}) collective-permute-start(bf16[7,32,128]{2,1,0:T(8,128)(2,1)S(1)} %get-tuple-element.52), channel_id=1, source_target_pairs={{453,452},{461,460},{469,468},{477,476},{454,453},{462,461},{470,4... | collective-permute-start | bytes 172040 | tf_op jit(solution)/shard_map/ppermute | solution.py:297
  183.5 1.9 collective-permute-start.37
  185.4 4.9 %collective-permute-start.38 = (bf16[7,32,128]{2,1,0:T(8,128)(2,1)S(1)}, bf16[7,32,128]{2,1,0:T(8,128)(2,1)S(1)}, u32[]{:S(2)}, u32[]{:S(2)}) collective-permute-start(bf16[7,32,128]{2,1,0:T(8,128)(2,1)S(1)} %get-tuple-element.50), channel_id=1, source_target_pairs={{453,452},{461,460},{469,468},{477,476},{454,453},{462,461},{470,4... | collective-permute-start | bytes 172040 | tf_op jit(solution)/shard_map/ppermute | solution.py:297
  191.7 1.3 collective-permute-start.39
  193.0 1.4 collective-permute-done.39
  194.5 12.3 %all_to_all.11 = bf16[8,2,7,16,128]{4,3,2,1,0:T(8,128)(2,1)S(1)} all-to-all(bf16[8,2,7,16,128]{4,3,2,1,0:T(8,128)(2,1)S(1)} %broadcast_select_fusion), channel_id=1, replica_groups={{452,460,468,476,448,456,464,472},{508,484,492,500,504,480,488,496},{20..., dimensions={0} | all-to-all | bytes 917504 | tf_op jit(solution)/shard_map/all_to_all | solution.py:386
  206.7 10.1 %collective-permute-start.40 = (bf16[8,2,7,16,128]{4,3,2,1,0:T(8,128)(2,1)S(1)}, bf16[8,2,7,16,128]{4,3,2,1,0:T(8,128)(2,1)S(1)}, u32[]{:S(2)}, u32[]{:S(2)}) collective-permute-start(bf16[8,2,7,16,128]{4,3,2,1,0:T(8,128)(2,1)S(1)} %all_to_all.11), channel_id=1, source_target_pairs={{452,416},{453,417},{454,418},{455,419},{511,420},{510,421},{509,4... | collective-permute-start | bytes 1376264 | tf_op jit(solution)/shard_map/ppermute | solution.py:387
  216.8 31.0 %collective-permute-done.40.parts_ref = bf16[8,2,7,16,128]{4,3,2,1,0:T(8,128)(2,1)S(1)} collective-permute-done((bf16[8,2,7,16,128]{4,3,2,1,0:T(8,128)(2,1)S(1)}, bf16[8,2,7,16,128]{4,3,2,1,0:T(8,128)(2,1)S(1)}, u32[]{:S(2)}, u32[]{:S(2)}) %collective-permute-start.40) | collective-permute-done | bytes 458784 | tf_op jit(solution)/shard_map/ppermute | solution.py:387
  (89 shorter events, 23.9 us)
Async XLA Ops:
  0.7 0.9 copy-start
  1.6 1.1 copy-start.2
  6.4 17.5 %collective-permute-start.4 = (bf16[8,7,16,128]{3,2,1,0:T(8,128)(2,1)S(1)}, bf16[8,7,16,128]{3,2,1,0:T(8,128)(2,1)S(1)}, u32[]{:S(2)}, u32[]{:S(2)}) collective-permute-start(bf16[8,7,16,128]{3,2,1,0:T(8,128)(2,1)S(1)} %get-tuple-element.26), channel_id=1, source_target_pairs={{416,452},{417,453},{418,454},{419,455},{420,511},{421,510},{422,5... | collective-permute-start | bytes 688136 | tf_op jit(solution)/shard_map/ppermute | solution.py:317
  19.0 41.4 %collective-permute-start = (bf16[1392,128]{1,0:T(8,128)(2,1)S(1)}, bf16[1392,128]{1,0:T(8,128)(2,1)S(1)}, u32[]{:S(2)}, u32[]{:S(2)}) collective-permute-start(bf16[1392,128]{1,0:T(8,128)(2,1)S(1)} %get-tuple-element.25), channel_id=1, source_target_pairs={{480,460},{481,461},{482,462},{483,463},{484,487},{485,486},{486,4... | collective-permute-start | bytes 1069064 | tf_op jit(solution)/shard_map/ppermute | solution.py:318
  59.1 8.8 %collective-permute-start.5 = (bf16[8,7,16,128]{3,2,1,0:T(8,128)(2,1)S(1)}, bf16[8,7,16,128]{3,2,1,0:T(8,128)(2,1)S(1)}, u32[]{:S(2)}, u32[]{:S(2)}) collective-permute-start(bf16[8,7,16,128]{3,2,1,0:T(8,128)(2,1)S(1)} %all_to_all.10), channel_id=1, source_target_pairs={{0,4},{8,12},{16,20},{24,28},{32,36},{40,44},{48,52},{56,60},{64,6... | collective-permute-start | bytes 688136 | tf_op jit(solution)/shard_map/ppermute | solution.py:333
  60.4 14.1 %collective-permute-start.1 = (bf16[1392,128]{1,0:T(8,128)(2,1)S(1)}, bf16[1392,128]{1,0:T(8,128)(2,1)S(1)}, u32[]{:S(2)}, u32[]{:S(2)}) collective-permute-start(bf16[1392,128]{1,0:T(8,128)(2,1)S(1)} %shard_map.60), channel_id=1, source_target_pairs={{4,12},{12,20},{20,28},{28,4},{36,44},{44,52},{52,60},{60,36},{68,... | collective-permute-start | bytes 1069064 | tf_op jit(solution)/shard_map/ppermute | solution.py:325
  62.5 12.1 %collective-permute-start.2 = (bf16[1392,128]{1,0:T(8,128)(2,1)S(1)}, bf16[1392,128]{1,0:T(8,128)(2,1)S(1)}, u32[]{:S(2)}, u32[]{:S(2)}) collective-permute-start(bf16[1392,128]{1,0:T(8,128)(2,1)S(1)} %shard_map.60), channel_id=1, source_target_pairs={{4,20},{12,28},{20,4},{28,12},{36,52},{44,60},{52,36},{60,44},{68,... | collective-permute-start | bytes 1069064 | tf_op jit(solution)/shard_map/ppermute | solution.py:325
  65.9 10.0 %collective-permute-start.3 = (bf16[1392,128]{1,0:T(8,128)(2,1)S(1)}, bf16[1392,128]{1,0:T(8,128)(2,1)S(1)}, u32[]{:S(2)}, u32[]{:S(2)}) collective-permute-start(bf16[1392,128]{1,0:T(8,128)(2,1)S(1)} %shard_map.60), channel_id=1, source_target_pairs={{4,28},{12,4},{20,12},{28,20},{36,60},{44,36},{52,44},{60,52},{68,... | collective-permute-start | bytes 1069064 | tf_op jit(solution)/shard_map/ppermute | solution.py:325
  68.0 8.7 %copy-start.3 = (bf16[7,32,128]{2,1,0:T(8,128)(2,1)}, bf16[7,32,128]{2,1,0:T(8,128)(2,1)S(1)}, u32[]{:S(2)}) copy-start(bf16[7,32,128]{2,1,0:T(8,128)(2,1)S(1)} %slice_bitcast_fusion.refs_1_.refs_0_) | copy-start | bytes 172036
  68.0 7.9 %collective-permute-start.6 = (bf16[7,32,128]{2,1,0:T(8,128)(2,1)S(1)}, bf16[7,32,128]{2,1,0:T(8,128)(2,1)S(1)}, u32[]{:S(2)}, u32[]{:S(2)}) collective-permute-start(bf16[7,32,128]{2,1,0:T(8,128)(2,1)S(1)} %slice_bitcast_fusion.refs_1_.refs_0_), channel_id=1, source_target_pairs={{452,453},{460,461},{468,469},{476,477},{453,454},{461,462},{469,4... | collective-permute-start | bytes 172040 | tf_op jit(solution)/shard_map/ppermute | solution.py:297
  69.9 6.0 %collective-permute-start.7 = (bf16[7,32,128]{2,1,0:T(8,128)(2,1)S(1)}, bf16[7,32,128]{2,1,0:T(8,128)(2,1)S(1)}, u32[]{:S(2)}, u32[]{:S(2)}) collective-permute-start(bf16[7,32,128]{2,1,0:T(8,128)(2,1)S(1)} %slice_bitcast_fusion.refs_1_.refs_0_), channel_id=1, source_target_pairs={{453,452},{461,460},{469,468},{477,476},{454,453},{462,461},{470,4... | collective-permute-start | bytes 172040 | tf_op jit(solution)/shard_map/ppermute | solution.py:297
  76.7 10.8 %copy-start.6 = (bf16[7,32,128]{2,1,0:T(8,128)(2,1)}, bf16[7,32,128]{2,1,0:T(8,128)(2,1)S(1)}, u32[]{:S(2)}) copy-start(bf16[7,32,128]{2,1,0:T(8,128)(2,1)S(1)} %shard_map.61.refs_1_.refs_0_) | copy-start | bytes 172036
  76.7 8.1 %collective-permute-start.12 = (bf16[7,32,128]{2,1,0:T(8,128)(2,1)S(1)}, bf16[7,32,128]{2,1,0:T(8,128)(2,1)S(1)}, u32[]{:S(2)}, u32[]{:S(2)}) collective-permute-start(bf16[7,32,128]{2,1,0:T(8,128)(2,1)S(1)} %shard_map.61.refs_1_.refs_0_), channel_id=1, source_target_pairs={{4,0},{12,8},{20,16},{28,24},{36,32},{44,40},{52,48},{60,56},{68,6... | collective-permute-start | bytes 172040 | tf_op jit(solution)/shard_map/ppermute | solution.py:340
  78.0 9.0 %collective-permute-start.8 = (bf16[7,32,128]{2,1,0:T(8,128)(2,1)S(1)}, bf16[7,32,128]{2,1,0:T(8,128)(2,1)S(1)}, u32[]{:S(2)}, u32[]{:S(2)}) collective-permute-start(bf16[7,32,128]{2,1,0:T(8,128)(2,1)S(1)} %shard_map.61.refs_1_.refs_0_), channel_id=1, source_target_pairs={{452,453},{460,461},{468,469},{476,477},{453,454},{461,462},{469,4... | collective-permute-start | bytes 172040 | tf_op jit(solution)/shard_map/ppermute | solution.py:297
  79.9 7.1 %collective-permute-start.9 = (bf16[7,32,128]{2,1,0:T(8,128)(2,1)S(1)}, bf16[7,32,128]{2,1,0:T(8,128)(2,1)S(1)}, u32[]{:S(2)}, u32[]{:S(2)}) collective-permute-start(bf16[7,32,128]{2,1,0:T(8,128)(2,1)S(1)} %shard_map.61.refs_1_.refs_0_), channel_id=1, source_target_pairs={{453,452},{461,460},{469,468},{477,476},{454,453},{462,461},{470,4... | collective-permute-start | bytes 172040 | tf_op jit(solution)/shard_map/ppermute | solution.py:297
  84.9 9.1 %collective-permute-start.13 = (bf16[1616,128]{1,0:T(8,128)(2,1)S(1)}, bf16[1616,128]{1,0:T(8,128)(2,1)S(1)}, u32[]{:S(2)}, u32[]{:S(2)}) collective-permute-start(bf16[1616,128]{1,0:T(8,128)(2,1)S(1)} %get-tuple-element.49), channel_id=1, source_target_pairs={{0,8},{8,16},{16,24},{24,0},{32,40},{40,48},{48,56},{56,32},{64,72... | collective-permute-start | bytes 1241096 | tf_op jit(solution)/shard_map/ppermute | solution.py:325
  85.6 8.4 %collective-permute-start.14 = (bf16[1616,128]{1,0:T(8,128)(2,1)S(1)}, bf16[1616,128]{1,0:T(8,128)(2,1)S(1)}, u32[]{:S(2)}, u32[]{:S(2)}) collective-permute-start(bf16[1616,128]{1,0:T(8,128)(2,1)S(1)} %get-tuple-element.49), channel_id=1, source_target_pairs={{0,16},{8,24},{16,0},{24,8},{32,48},{40,56},{48,32},{56,40},{64,80... | collective-permute-start | bytes 1241096 | tf_op jit(solution)/shard_map/ppermute | solution.py:325
  86.3 7.7 %collective-permute-start.15 = (bf16[1616,128]{1,0:T(8,128)(2,1)S(1)}, bf16[1616,128]{1,0:T(8,128)(2,1)S(1)}, u32[]{:S(2)}, u32[]{:S(2)}) collective-permute-start(bf16[1616,128]{1,0:T(8,128)(2,1)S(1)} %get-tuple-element.49), channel_id=1, source_target_pairs={{0,24},{8,0},{16,8},{24,16},{32,56},{40,32},{48,40},{56,48},{64,88... | collective-permute-start | bytes 1241096 | tf_op jit(solution)/shard_map/ppermute | solution.py:325
  87.5 8.1 %collective-permute-start.10 = (bf16[7,32,128]{2,1,0:T(8,128)(2,1)S(1)}, bf16[7,32,128]{2,1,0:T(8,128)(2,1)S(1)}, u32[]{:S(2)}, u32[]{:S(2)}) collective-permute-start(bf16[7,32,128]{2,1,0:T(8,128)(2,1)S(1)} %shard_map.62.refs_1_.refs_0_.refs_2_), channel_id=1, source_target_pairs={{452,453},{460,461},{468,469},{476,477},{453,454},{461,462},{469,4... | collective-permute-start | bytes 172040 | tf_op jit(solution)/shard_map/ppermute | solution.py:297
  89.4 6.1 %collective-permute-start.11 = (bf16[7,32,128]{2,1,0:T(8,128)(2,1)S(1)}, bf16[7,32,128]{2,1,0:T(8,128)(2,1)S(1)}, u32[]{:S(2)}, u32[]{:S(2)}) collective-permute-start(bf16[7,32,128]{2,1,0:T(8,128)(2,1)S(1)} %shard_map.62.refs_1_.refs_0_.refs_2_), channel_id=1, source_target_pairs={{453,452},{461,460},{469,468},{477,476},{454,453},{462,461},{470,4... | collective-permute-start | bytes 172040 | tf_op jit(solution)/shard_map/ppermute | solution.py:297
  94.2 10.0 %collective-permute-start.16 = (bf16[4,1616,128]{2,1,0:T(8,128)(2,1)S(1)}, bf16[4,1616,128]{2,1,0:T(8,128)(2,1)S(1)}, u32[]{:S(2)}, u32[]{:S(2)}) collective-permute-start(bf16[4,1616,128]{2,1,0:T(8,128)(2,1)S(1)} %pad_maximum_fusion), channel_id=1, source_target_pairs={{0,4},{8,12},{16,20},{24,28},{32,36},{40,44},{48,52},{56,60},{64,6... | collective-permute-start | bytes 4964360 | tf_op jit(solution)/shard_map/ppermute | solution.py:342
  96.0 8.3 %collective-permute-start.17 = (bf16[7,32,128]{2,1,0:T(8,128)(2,1)S(1)}, bf16[7,32,128]{2,1,0:T(8,128)(2,1)S(1)}, u32[]{:S(2)}, u32[]{:S(2)}) collective-permute-start(bf16[7,32,128]{2,1,0:T(8,128)(2,1)S(1)} %shard_map.63.refs_1_.refs_0_.refs_3_), channel_id=1, source_target_pairs={{452,453},{460,461},{468,469},{476,477},{453,454},{461,462},{469,4... | collective-permute-start | bytes 172040 | tf_op jit(solution)/shard_map/ppermute | solution.py:297
  98.0 6.4 %collective-permute-start.18 = (bf16[7,32,128]{2,1,0:T(8,128)(2,1)S(1)}, bf16[7,32,128]{2,1,0:T(8,128)(2,1)S(1)}, u32[]{:S(2)}, u32[]{:S(2)}) collective-permute-start(bf16[7,32,128]{2,1,0:T(8,128)(2,1)S(1)} %shard_map.63.refs_1_.refs_0_.refs_3_), channel_id=1, source_target_pairs={{453,452},{461,460},{469,468},{477,476},{454,453},{462,461},{470,4... | collective-permute-start | bytes 172040 | tf_op jit(solution)/shard_map/ppermute | solution.py:297
  104.8 6.8 %collective-permute-start.19 = (bf16[7,32,128]{2,1,0:T(8,128)(2,1)S(1)}, bf16[7,32,128]{2,1,0:T(8,128)(2,1)S(1)}, u32[]{:S(2)}, u32[]{:S(2)}) collective-permute-start(bf16[7,32,128]{2,1,0:T(8,128)(2,1)S(1)} %shard_map.64.refs_1_.refs_0_.refs_4_), channel_id=1, source_target_pairs={{452,453},{460,461},{468,469},{476,477},{453,454},{461,462},{469,4... | collective-permute-start | bytes 172040 | tf_op jit(solution)/shard_map/ppermute | solution.py:297
  106.7 6.1 %collective-permute-start.20 = (bf16[7,32,128]{2,1,0:T(8,128)(2,1)S(1)}, bf16[7,32,128]{2,1,0:T(8,128)(2,1)S(1)}, u32[]{:S(2)}, u32[]{:S(2)}) collective-permute-start(bf16[7,32,128]{2,1,0:T(8,128)(2,1)S(1)} %shard_map.64.refs_1_.refs_0_.refs_4_), channel_id=1, source_target_pairs={{453,452},{461,460},{469,468},{477,476},{454,453},{462,461},{470,4... | collective-permute-start | bytes 172040 | tf_op jit(solution)/shard_map/ppermute | solution.py:297
  113.3 6.8 %collective-permute-start.21 = (bf16[7,32,128]{2,1,0:T(8,128)(2,1)S(1)}, bf16[7,32,128]{2,1,0:T(8,128)(2,1)S(1)}, u32[]{:S(2)}, u32[]{:S(2)}) collective-permute-start(bf16[7,32,128]{2,1,0:T(8,128)(2,1)S(1)} %shard_map.65.refs_1_.refs_0_.refs_5_), channel_id=1, source_target_pairs={{452,453},{460,461},{468,469},{476,477},{453,454},{461,462},{469,4... | collective-permute-start | bytes 172040 | tf_op jit(solution)/shard_map/ppermute | solution.py:297
  115.3 6.1 %collective-permute-start.22 = (bf16[7,32,128]{2,1,0:T(8,128)(2,1)S(1)}, bf16[7,32,128]{2,1,0:T(8,128)(2,1)S(1)}, u32[]{:S(2)}, u32[]{:S(2)}) collective-permute-start(bf16[7,32,128]{2,1,0:T(8,128)(2,1)S(1)} %shard_map.65.refs_1_.refs_0_.refs_5_), channel_id=1, source_target_pairs={{453,452},{461,460},{469,468},{477,476},{454,453},{462,461},{470,4... | collective-permute-start | bytes 172040 | tf_op jit(solution)/shard_map/ppermute | solution.py:297
  121.9 6.8 %collective-permute-start.23 = (bf16[7,32,128]{2,1,0:T(8,128)(2,1)S(1)}, bf16[7,32,128]{2,1,0:T(8,128)(2,1)S(1)}, u32[]{:S(2)}, u32[]{:S(2)}) collective-permute-start(bf16[7,32,128]{2,1,0:T(8,128)(2,1)S(1)} %shard_map.66.refs_1_.refs_0_.refs_6_), channel_id=1, source_target_pairs={{452,453},{460,461},{468,469},{476,477},{453,454},{461,462},{469,4... | collective-permute-start | bytes 172040 | tf_op jit(solution)/shard_map/ppermute | solution.py:297
  123.8 6.1 %collective-permute-start.24 = (bf16[7,32,128]{2,1,0:T(8,128)(2,1)S(1)}, bf16[7,32,128]{2,1,0:T(8,128)(2,1)S(1)}, u32[]{:S(2)}, u32[]{:S(2)}) collective-permute-start(bf16[7,32,128]{2,1,0:T(8,128)(2,1)S(1)} %shard_map.66.refs_1_.refs_0_.refs_6_), channel_id=1, source_target_pairs={{453,452},{461,460},{469,468},{477,476},{454,453},{462,461},{470,4... | collective-permute-start | bytes 172040 | tf_op jit(solution)/shard_map/ppermute | solution.py:297
  131.0 6.8 %collective-permute-start.25 = (bf16[7,32,128]{2,1,0:T(8,128)(2,1)S(1)}, bf16[7,32,128]{2,1,0:T(8,128)(2,1)S(1)}, u32[]{:S(2)}, u32[]{:S(2)}) collective-permute-start(bf16[7,32,128]{2,1,0:T(8,128)(2,1)S(1)} %get-tuple-element.63), channel_id=1, source_target_pairs={{452,453},{460,461},{468,469},{476,477},{453,454},{461,462},{469,4... | collective-permute-start | bytes 172040 | tf_op jit(solution)/shard_map/ppermute | solution.py:297
  133.0 6.1 %collective-permute-start.26 = (bf16[7,32,128]{2,1,0:T(8,128)(2,1)S(1)}, bf16[7,32,128]{2,1,0:T(8,128)(2,1)S(1)}, u32[]{:S(2)}, u32[]{:S(2)}) collective-permute-start(bf16[7,32,128]{2,1,0:T(8,128)(2,1)S(1)} %get-tuple-element.62), channel_id=1, source_target_pairs={{453,452},{461,460},{469,468},{477,476},{454,453},{462,461},{470,4... | collective-permute-start | bytes 172040 | tf_op jit(solution)/shard_map/ppermute | solution.py:297
  139.7 6.8 %collective-permute-start.27 = (bf16[7,32,128]{2,1,0:T(8,128)(2,1)S(1)}, bf16[7,32,128]{2,1,0:T(8,128)(2,1)S(1)}, u32[]{:S(2)}, u32[]{:S(2)}) collective-permute-start(bf16[7,32,128]{2,1,0:T(8,128)(2,1)S(1)} %get-tuple-element.61), channel_id=1, source_target_pairs={{452,453},{460,461},{468,469},{476,477},{453,454},{461,462},{469,4... | collective-permute-start | bytes 172040 | tf_op jit(solution)/shard_map/ppermute | solution.py:297
  141.7 6.1 %collective-permute-start.28 = (bf16[7,32,128]{2,1,0:T(8,128)(2,1)S(1)}, bf16[7,32,128]{2,1,0:T(8,128)(2,1)S(1)}, u32[]{:S(2)}, u32[]{:S(2)}) collective-permute-start(bf16[7,32,128]{2,1,0:T(8,128)(2,1)S(1)} %get-tuple-element.60), channel_id=1, source_target_pairs={{453,452},{461,460},{469,468},{477,476},{454,453},{462,461},{470,4... | collective-permute-start | bytes 172040 | tf_op jit(solution)/shard_map/ppermute | solution.py:297
  148.4 6.8 %collective-permute-start.29 = (bf16[7,32,128]{2,1,0:T(8,128)(2,1)S(1)}, bf16[7,32,128]{2,1,0:T(8,128)(2,1)S(1)}, u32[]{:S(2)}, u32[]{:S(2)}) collective-permute-start(bf16[7,32,128]{2,1,0:T(8,128)(2,1)S(1)} %get-tuple-element.59), channel_id=1, source_target_pairs={{452,453},{460,461},{468,469},{476,477},{453,454},{461,462},{469,4... | collective-permute-start | bytes 172040 | tf_op jit(solution)/shard_map/ppermute | solution.py:297
  150.4 6.1 %collective-permute-start.30 = (bf16[7,32,128]{2,1,0:T(8,128)(2,1)S(1)}, bf16[7,32,128]{2,1,0:T(8,128)(2,1)S(1)}, u32[]{:S(2)}, u32[]{:S(2)}) collective-permute-start(bf16[7,32,128]{2,1,0:T(8,128)(2,1)S(1)} %get-tuple-element.58), channel_id=1, source_target_pairs={{453,452},{461,460},{469,468},{477,476},{454,453},{462,461},{470,4... | collective-permute-start | bytes 172040 | tf_op jit(solution)/shard_map/ppermute | solution.py:297
  157.1 6.8 %collective-permute-start.31 = (bf16[7,32,128]{2,1,0:T(8,128)(2,1)S(1)}, bf16[7,32,128]{2,1,0:T(8,128)(2,1)S(1)}, u32[]{:S(2)}, u32[]{:S(2)}) collective-permute-start(bf16[7,32,128]{2,1,0:T(8,128)(2,1)S(1)} %get-tuple-element.57), channel_id=1, source_target_pairs={{452,453},{460,461},{468,469},{476,477},{453,454},{461,462},{469,4... | collective-permute-start | bytes 172040 | tf_op jit(solution)/shard_map/ppermute | solution.py:297
  159.1 6.1 %collective-permute-start.32 = (bf16[7,32,128]{2,1,0:T(8,128)(2,1)S(1)}, bf16[7,32,128]{2,1,0:T(8,128)(2,1)S(1)}, u32[]{:S(2)}, u32[]{:S(2)}) collective-permute-start(bf16[7,32,128]{2,1,0:T(8,128)(2,1)S(1)} %get-tuple-element.56), channel_id=1, source_target_pairs={{453,452},{461,460},{469,468},{477,476},{454,453},{462,461},{470,4... | collective-permute-start | bytes 172040 | tf_op jit(solution)/shard_map/ppermute | solution.py:297
  165.8 7.0 %collective-permute-start.33 = (bf16[7,32,128]{2,1,0:T(8,128)(2,1)S(1)}, bf16[7,32,128]{2,1,0:T(8,128)(2,1)S(1)}, u32[]{:S(2)}, u32[]{:S(2)}) collective-permute-start(bf16[7,32,128]{2,1,0:T(8,128)(2,1)S(1)} %get-tuple-element.55), channel_id=1, source_target_pairs={{452,453},{460,461},{468,469},{476,477},{453,454},{461,462},{469,4... | collective-permute-start | bytes 172040 | tf_op jit(solution)/shard_map/ppermute | solution.py:297
  167.8 15.1 %copy-start.7 = (bf16[7,32,128]{2,1,0:T(8,128)(2,1)S(1)}, bf16[7,32,128]{2,1,0:T(8,128)(2,1)}, u32[]{:S(2)}) copy-start(bf16[7,32,128]{2,1,0:T(8,128)(2,1)} %copy-done.6) | copy-start | bytes 172036
  167.8 6.3 %collective-permute-start.34 = (bf16[7,32,128]{2,1,0:T(8,128)(2,1)S(1)}, bf16[7,32,128]{2,1,0:T(8,128)(2,1)S(1)}, u32[]{:S(2)}, u32[]{:S(2)}) collective-permute-start(bf16[7,32,128]{2,1,0:T(8,128)(2,1)S(1)} %get-tuple-element.54), channel_id=1, source_target_pairs={{453,452},{461,460},{469,468},{477,476},{454,453},{462,461},{470,4... | collective-permute-start | bytes 172040 | tf_op jit(solution)/shard_map/ppermute | solution.py:297
  174.7 7.0 %collective-permute-start.35 = (bf16[7,32,128]{2,1,0:T(8,128)(2,1)S(1)}, bf16[7,32,128]{2,1,0:T(8,128)(2,1)S(1)}, u32[]{:S(2)}, u32[]{:S(2)}) collective-permute-start(bf16[7,32,128]{2,1,0:T(8,128)(2,1)S(1)} %get-tuple-element.53), channel_id=1, source_target_pairs={{452,453},{460,461},{468,469},{476,477},{453,454},{461,462},{469,4... | collective-permute-start | bytes 172040 | tf_op jit(solution)/shard_map/ppermute | solution.py:297
  176.6 15.0 %copy-start.4 = (bf16[7,32,128]{2,1,0:T(8,128)(2,1)S(1)}, bf16[7,32,128]{2,1,0:T(8,128)(2,1)}, u32[]{:S(2)}) copy-start(bf16[7,32,128]{2,1,0:T(8,128)(2,1)} %copy-done.3) | copy-start | bytes 172036
  176.6 6.3 %collective-permute-start.36 = (bf16[7,32,128]{2,1,0:T(8,128)(2,1)S(1)}, bf16[7,32,128]{2,1,0:T(8,128)(2,1)S(1)}, u32[]{:S(2)}, u32[]{:S(2)}) collective-permute-start(bf16[7,32,128]{2,1,0:T(8,128)(2,1)S(1)} %get-tuple-element.52), channel_id=1, source_target_pairs={{453,452},{461,460},{469,468},{477,476},{454,453},{462,461},{470,4... | collective-permute-start | bytes 172040 | tf_op jit(solution)/shard_map/ppermute | solution.py:297
  183.5 6.8 %collective-permute-start.37 = (bf16[7,32,128]{2,1,0:T(8,128)(2,1)S(1)}, bf16[7,32,128]{2,1,0:T(8,128)(2,1)S(1)}, u32[]{:S(2)}, u32[]{:S(2)}) collective-permute-start(bf16[7,32,128]{2,1,0:T(8,128)(2,1)S(1)} %get-tuple-element.51), channel_id=1, source_target_pairs={{452,453},{460,461},{468,469},{476,477},{453,454},{461,462},{469,4... | collective-permute-start | bytes 172040 | tf_op jit(solution)/shard_map/ppermute | solution.py:297
  185.4 6.1 %collective-permute-start.38 = (bf16[7,32,128]{2,1,0:T(8,128)(2,1)S(1)}, bf16[7,32,128]{2,1,0:T(8,128)(2,1)S(1)}, u32[]{:S(2)}, u32[]{:S(2)}) collective-permute-start(bf16[7,32,128]{2,1,0:T(8,128)(2,1)S(1)} %get-tuple-element.50), channel_id=1, source_target_pairs={{453,452},{461,460},{469,468},{477,476},{454,453},{462,461},{470,4... | collective-permute-start | bytes 172040 | tf_op jit(solution)/shard_map/ppermute | solution.py:297
  191.6 56.2 %copy-start.1 = (bf16[14,64,64]{2,1,0:T(8,128)(2,1)S(1)}, bf16[14,64,64]{2,1,0:T(8,128)(2,1)}, u32[]{:S(2)}) copy-start(bf16[14,64,64]{2,1,0:T(8,128)(2,1)} %diag_ref.1) | copy-start | bytes 344068
  191.7 2.7 %collective-permute-start.39 = (bf16[8,2,7,16,128]{4,3,2,1,0:T(8,128)(2,1)S(1)}, bf16[8,2,7,16,128]{4,3,2,1,0:T(8,128)(2,1)S(1)}, u32[]{:S(2)}, u32[]{:S(2)}) collective-permute-start(bf16[8,2,7,16,128]{4,3,2,1,0:T(8,128)(2,1)S(1)} %get-tuple-element.47), channel_id=1, source_target_pairs={{4,0},{12,8},{20,16},{28,24},{36,32},{44,40},{52,48},{60,56},{68,6... | collective-permute-start | bytes 1376264 | tf_op jit(solution)/shard_map/ppermute | solution.py:384
  206.7 41.1 %collective-permute-start.40 = (bf16[8,2,7,16,128]{4,3,2,1,0:T(8,128)(2,1)S(1)}, bf16[8,2,7,16,128]{4,3,2,1,0:T(8,128)(2,1)S(1)}, u32[]{:S(2)}, u32[]{:S(2)}) collective-permute-start(bf16[8,2,7,16,128]{4,3,2,1,0:T(8,128)(2,1)S(1)} %all_to_all.11), channel_id=1, source_target_pairs={{452,416},{453,417},{454,418},{455,419},{511,420},{510,421},{509,4... | collective-permute-start | bytes 1376264 | tf_op jit(solution)/shard_map/ppermute | solution.py:387
  (2 other events, 1.6 us)

commit v4 on v3

--- a/solution.py
+++ b/solution.py
@@ -102,46 +102,39 @@
         ref[start : start + values.shape[0], :] = values[:, part * 128 : (part + 1) * 128]
 
 
-def prepare_kernel(
-    shift_ref, pattern_ref, rhs_hbm, factor_hbm, diag_hbm, out_ref, rhs_t_ref, rhs_ref, factor_ref, diag_ref, sems
-):
-    arrays = ((diag_hbm, diag_ref), (rhs_hbm, rhs_ref), (factor_hbm, factor_ref))
-    copies = []
-    for half in range(2):
-        rows = pl.ds(half * PAIRS, PAIRS)
-        for n, (source, target) in enumerate(arrays):
-            copies.append(pltpu.make_async_copy(source.at[rows], target.at[rows], sems.at[half * 3 + n]))
-    for copy in copies:
-        copy.start()
+def prepare_rhs_kernel(shift_ref, rhs_ref, diag_ref, out_ref):
+    shift = shift_ref[0, 0]
+    for i in range(PAIRS):
+        sides = [
+            jnp.dot(diag_ref[n], rhs_ref[n], preferred_element_type=F32) for n in (i, i + PAIRS)
+        ]
+        turned = jnp.concatenate(sides, axis=0).T.astype(BF16)
+        for j in range(COLS // PART):
+            out_ref[turn_of_slot(j, shift), i] = turned[j * PART : (j + 1) * PART, :]
+
+
+def prepare_weights_kernel(pattern_ref, factor_ref, diag_ref, out_ref):
+    patterns = pattern_ref[...]
     lane = lax.broadcasted_iota(jnp.int32, (16, WIDE), 1)
     entries = jnp.zeros((16, WIDE), jnp.int32)
     for n in range(SLOTS):
         for m in range(LINKS):
-            entry = jnp.clip(pattern_ref[m, n], 0, WINDOW - 1)
+            entry = jnp.clip(patterns[m, n], 0, WINDOW - 1)
             entries = jnp.where(lane == LINKS * n + m, entry, entries)
-    entries = entries.astype(F32).astype(BF16)
-    for copy in copies:
-        copy.wait()
-    for i in range(PAIRS):
-        couplings, sides = [], []
+    put_block(out_ref, ROWS, entries.astype(F32).astype(BF16))
+    for i in range(PAIRS):
+        couplings = []
         for n in (i, i + PAIRS):
-            diag = diag_ref[n]
             factor = jnp.concatenate([factor_ref[n, m] for m in range(LINKS)], axis=1)
-            couplings.append(jnp.dot(diag, factor, preferred_element_type=F32))
-            sides.append(jnp.dot(diag, rhs_ref[n], preferred_element_type=F32))
-        both = jnp.concatenate(couplings, axis=1).astype(BF16)
-        put_block(out_ref, i * ORDER, both)
-        turned = jnp.concatenate(sides, axis=0).T.astype(BF16)
-        for j in range(COLS // PART):
-            rhs_t_ref[turn_of_slot(j, shift_ref[0]), i] = turned[j * PART : (j + 1) * PART, :]
-    put_block(out_ref, ROWS, entries)
+            couplings.append(jnp.dot(diag_ref[n], factor, preferred_element_type=F32))
+        put_block(out_ref, i * ORDER, jnp.concatenate(couplings, axis=1).astype(BF16))
 
 
 def finish_kernel(shift_ref, parts_ref, diag_ref, forward_ref, backward_ref):
     for i in range(PAIRS):
         for kind in range(2):
             columns = jnp.concatenate(
-                [parts_ref[turn_of_slot(j, shift_ref[0]), kind, i] for j in range(COLS // PART)], axis=0
+                [parts_ref[turn_of_slot(j, shift_ref[0, 0]), kind, i] for j in range(COLS // PART)], axis=0
             )
             turned = columns.astype(F32).T.astype(BF16)
             for n, rows in ((i, turned[:ORDER]), (i + PAIRS, turned[ORDER:])):
@@ -300,20 +293,14 @@
     plane, x, core = lvl // 8, lvl % 8 // 2, lvl % 2
     band = (plane - PLANE_OF[0]) % PLANES
     state = ((x + band) % 4).astype(jnp.int32).reshape(1)
-    shift = ((x * 2 + core) % 4).astype(jnp.int32).reshape(1)
-
-    stored = (right_side, factor_blocks, diag_inverse)
-    weights, rhs = pl.pallas_call(
-        prepare_kernel,
-        out_shape=[
-            jax.ShapeDtypeStruct((SHARD, 128), BF16),
-            jax.ShapeDtypeStruct((LEVELS, PAIRS, PART, 128), BF16),
-        ],
-        in_specs=[pl.BlockSpec(memory_space=pltpu.SMEM)] * 2 + [pl.BlockSpec(memory_space=pltpu.HBM)] * 3,
-        out_specs=[pl.BlockSpec(memory_space=VMEM)] * 2,
-        scratch_shapes=[VMEM(array.shape, BF16) for array in stored] + [pltpu.SemaphoreType.DMA((6,))],
-        compiler_params=pltpu.CompilerParams(vmem_limit_bytes=16 * 1024 * 1024),
-    )(shift, pattern.T, *stored)
+    shift = ((x * 2 + core) % 4).astype(jnp.int32).reshape(1, 1)
+
+    (rhs,) = call(
+        prepare_rhs_kernel, [((LEVELS, PAIRS, PART, 128), BF16)], (shift, right_side, diag_inverse)
+    )
+    (weights,) = call(
+        prepare_weights_kernel, [((SHARD, 128), BF16)], (pattern.T, factor_blocks, diag_inverse)
+    )
     rhs = lax.ppermute(rhs, AXES, to_group)
     weights = lax.ppermute(weights, AXES, level_pairs(1))
     cost = pl.CostEstimate(flops=50 * 10**9, bytes_accessed=SHARD * 512, transcendentals=0)
@@ -386,7 +373,7 @@
     parts = lax.all_to_all(packed, "lvl", 0, 0, axis_index_groups=groups)
     parts = lax.ppermute(parts, AXES, to_native)
     out_shape = ((SLOTS, ORDER, COLS), BF16)
-    return call(finish_kernel, [out_shape] * 2, (shift, parts, diag_inverse), scalars=1)
+    return call(finish_kernel, [out_shape] * 2, (shift, parts, diag_inverse))
 
 
 def solution(mesh):

time: 250 us -> 247 us (0.988)
  blocking collectives: 47.4 us -> 44.3 us
    all_to_all x1, blocking collectives: 35.1 us -> 32 us  [per_device(): rhs = lax.all_to_all(rhs, 'lvl', 0, 0, axis_index_groups=groups)]
    pallas_call x16 -> x18, Pallas kernels: 8.76 us -> 9.55 us  [call(): pl.pallas_call(kernel, out_shape=[jax.ShapeDtypeStruct(shape, dtype) for...]
  transfers between devices with their start and end apart: 41 -> 41, of which waited for: 14 -> 14; matrix products, arithmetic and copies ran while one was open for 0% -> 0% of each run, Pallas kernels for 0% -> 1%
where the time goes in v4:
time: 247 us; the launch traced here: 245 us
  starting transfers between devices  136 us (55%)
  waiting for transfers between devices  48.8 us (20%)
  blocking collectives  44.3 us (18%)
  Pallas kernels  9.55 us (4%)
  local copies, waits for them, and re-layouts  4.89 us (2%)
    ppermute x14, starting transfers between devices, exchange(): lax.ppermute(to_below, AXES, down)  68 us
    ppermute x1, waiting for transfers between devices, per_device(): parts = lax.ppermute(parts, AXES, to_native)  32.3 us
    all_to_all x1, blocking collectives, per_device(): rhs = lax.all_to_all(rhs, 'lvl', 0, 0, axis_index_groups=groups)  32 us
    ppermute x14, starting transfers between devices, exchange(): lax.ppermute(to_above, AXES, up)  26.9 us
    ppermute x1, starting transfers between devices, per_device(): rhs = lax.ppermute(rhs, AXES, to_group)  12.6 us
    all_to_all x1, blocking collectives, per_device(): parts = lax.all_to_all(packed, 'lvl', 0, 0, axis_index_groups=groups)  12.3 us
    ppermute x14, waiting for transfers between devices, exchange(): lax.ppermute(to_below, AXES, down)  12.2 us
    pallas_call x18, Pallas kernels, call(): pl.pallas_call(kernel, out_shape=[jax.ShapeDtypeStruct(shape, dtype) for...  9.55 us
  transfers between devices with their start and end apart: 41, of which 14 were waited for; matrix products, arithmetic and copies ran while one was open for 0% of the time, Pallas kernels for 1%

profile of v4, /device:TPU:135, one launch (start us, length us, event | category | flops | bytes accessed | tf_op | source)
XLA Modules:
  0.0 245.3 jit_solution(4227566925072815330)
XLA Ops:
  2.9 12.6 %collective-permute-start.4 = (bf16[8,7,16,128]{3,2,1,0:T(8,128)(2,1)S(1)}, bf16[8,7,16,128]{3,2,1,0:T(8,128)(2,1)S(1)}, u32[]{:S(2)}, u32[]{:S(2)}) collective-permute-start(bf16[8,7,16,128]{3,2,1,0:T(8,128)(2,1)S(1)} %shard_map.61), channel_id=1, source_target_pairs={{416,452},{417,453},{418,454},{419,455},{420,511},{421,510},{422,5... | collective-permute-start | bytes 688136 | tf_op jit(solution)/shard_map/ppermute | solution.py:304
  18.6 5.0 %collective-permute-start = (bf16[1392,128]{1,0:T(8,128)(2,1)S(1)}, bf16[1392,128]{1,0:T(8,128)(2,1)S(1)}, u32[]{:S(2)}, u32[]{:S(2)}) collective-permute-start(bf16[1392,128]{1,0:T(8,128)(2,1)S(1)} %shard_map.59), channel_id=1, source_target_pairs={{480,460},{481,461},{482,462},{483,463},{484,487},{485,486},{486,4... | collective-permute-start | bytes 1069064 | tf_op jit(solution)/shard_map/ppermute | solution.py:305
  23.6 32.0 %all_to_all.10 = bf16[8,7,16,128]{3,2,1,0:T(8,128)(2,1)S(1)} all-to-all(bf16[8,7,16,128]{3,2,1,0:T(8,128)(2,1)S(1)} %collective-permute-done.4), channel_id=1, replica_groups={{452,460,468,476,448,456,464,472},{508,484,492,500,504,480,488,496},{20..., dimensions={0} | all-to-all | bytes 458752 | tf_op jit(solution)/shard_map/all_to_all | solution.py:319
  55.6 1.3 collective-permute-start.5
  56.9 2.1 collective-permute-start.1
  59.0 3.4 %collective-permute-start.2 = (bf16[1392,128]{1,0:T(8,128)(2,1)S(1)}, bf16[1392,128]{1,0:T(8,128)(2,1)S(1)}, u32[]{:S(2)}, u32[]{:S(2)}) collective-permute-start(bf16[1392,128]{1,0:T(8,128)(2,1)S(1)} %shard_map.60), channel_id=1, source_target_pairs={{4,20},{12,28},{20,4},{28,12},{36,52},{44,60},{52,36},{60,44},{68,... | collective-permute-start | bytes 1069064 | tf_op jit(solution)/shard_map/ppermute | solution.py:312
  62.5 2.0 collective-permute-start.3
  64.5 1.9 collective-permute-start.6
  66.4 4.6 %collective-permute-start.7 = (bf16[7,32,128]{2,1,0:T(8,128)(2,1)S(1)}, bf16[7,32,128]{2,1,0:T(8,128)(2,1)S(1)}, u32[]{:S(2)}, u32[]{:S(2)}) collective-permute-start(bf16[7,32,128]{2,1,0:T(8,128)(2,1)S(1)} %slice_bitcast_fusion.refs_1_.refs_0_), channel_id=1, source_target_pairs={{453,452},{461,460},{469,468},{477,476},{454,453},{462,461},{470,4... | collective-permute-start | bytes 172040 | tf_op jit(solution)/shard_map/ppermute | solution.py:290
  71.1 1.3 collective-permute-done.3
  73.2 1.3 collective-permute-start.12
  74.5 1.9 collective-permute-start.8
  76.4 4.8 %collective-permute-start.9 = (bf16[7,32,128]{2,1,0:T(8,128)(2,1)S(1)}, bf16[7,32,128]{2,1,0:T(8,128)(2,1)S(1)}, u32[]{:S(2)}, u32[]{:S(2)}) collective-permute-start(bf16[7,32,128]{2,1,0:T(8,128)(2,1)S(1)} %shard_map.62.refs_1_.refs_0_), channel_id=1, source_target_pairs={{453,452},{461,460},{469,468},{477,476},{454,453},{462,461},{470,4... | collective-permute-start | bytes 172040 | tf_op jit(solution)/shard_map/ppermute | solution.py:290
  83.9 1.9 collective-permute-start.10
  85.9 4.6 %collective-permute-start.11 = (bf16[7,32,128]{2,1,0:T(8,128)(2,1)S(1)}, bf16[7,32,128]{2,1,0:T(8,128)(2,1)S(1)}, u32[]{:S(2)}, u32[]{:S(2)}) collective-permute-start(bf16[7,32,128]{2,1,0:T(8,128)(2,1)S(1)} %shard_map.63.refs_1_.refs_0_.refs_2_), channel_id=1, source_target_pairs={{453,452},{461,460},{469,468},{477,476},{454,453},{462,461},{470,4... | collective-permute-start | bytes 172040 | tf_op jit(solution)/shard_map/ppermute | solution.py:290
  90.7 1.3 collective-permute-start.16
  92.5 1.9 collective-permute-start.17
  94.4 4.9 %collective-permute-start.18 = (bf16[7,32,128]{2,1,0:T(8,128)(2,1)S(1)}, bf16[7,32,128]{2,1,0:T(8,128)(2,1)S(1)}, u32[]{:S(2)}, u32[]{:S(2)}) collective-permute-start(bf16[7,32,128]{2,1,0:T(8,128)(2,1)S(1)} %shard_map.64.refs_1_.refs_0_.refs_3_), channel_id=1, source_target_pairs={{453,452},{461,460},{469,468},{477,476},{454,453},{462,461},{470,4... | collective-permute-start | bytes 172040 | tf_op jit(solution)/shard_map/ppermute | solution.py:290
  99.3 1.5 collective-permute-done.16.shards_ref
  101.3 1.9 collective-permute-start.19
  103.2 4.9 %collective-permute-start.20 = (bf16[7,32,128]{2,1,0:T(8,128)(2,1)S(1)}, bf16[7,32,128]{2,1,0:T(8,128)(2,1)S(1)}, u32[]{:S(2)}, u32[]{:S(2)}) collective-permute-start(bf16[7,32,128]{2,1,0:T(8,128)(2,1)S(1)} %shard_map.65.refs_1_.refs_0_.refs_4_), channel_id=1, source_target_pairs={{453,452},{461,460},{469,468},{477,476},{454,453},{462,461},{470,4... | collective-permute-start | bytes 172040 | tf_op jit(solution)/shard_map/ppermute | solution.py:290
  109.8 1.9 collective-permute-start.21
  111.8 4.9 %collective-permute-start.22 = (bf16[7,32,128]{2,1,0:T(8,128)(2,1)S(1)}, bf16[7,32,128]{2,1,0:T(8,128)(2,1)S(1)}, u32[]{:S(2)}, u32[]{:S(2)}) collective-permute-start(bf16[7,32,128]{2,1,0:T(8,128)(2,1)S(1)} %shard_map.66.refs_1_.refs_0_.refs_5_), channel_id=1, source_target_pairs={{453,452},{461,460},{469,468},{477,476},{454,453},{462,461},{470,4... | collective-permute-start | bytes 172040 | tf_op jit(solution)/shard_map/ppermute | solution.py:290
  118.4 1.9 collective-permute-start.23
  120.3 4.9 %collective-permute-start.24 = (bf16[7,32,128]{2,1,0:T(8,128)(2,1)S(1)}, bf16[7,32,128]{2,1,0:T(8,128)(2,1)S(1)}, u32[]{:S(2)}, u32[]{:S(2)}) collective-permute-start(bf16[7,32,128]{2,1,0:T(8,128)(2,1)S(1)} %shard_map.67.refs_1_.refs_0_.refs_6_), channel_id=1, source_target_pairs={{453,452},{461,460},{469,468},{477,476},{454,453},{462,461},{470,4... | collective-permute-start | bytes 172040 | tf_op jit(solution)/shard_map/ppermute | solution.py:290
  127.6 1.9 collective-permute-start.25
  129.5 4.9 %collective-permute-start.26 = (bf16[7,32,128]{2,1,0:T(8,128)(2,1)S(1)}, bf16[7,32,128]{2,1,0:T(8,128)(2,1)S(1)}, u32[]{:S(2)}, u32[]{:S(2)}) collective-permute-start(bf16[7,32,128]{2,1,0:T(8,128)(2,1)S(1)} %get-tuple-element.58), channel_id=1, source_target_pairs={{453,452},{461,460},{469,468},{477,476},{454,453},{462,461},{470,4... | collective-permute-start | bytes 172040 | tf_op jit(solution)/shard_map/ppermute | solution.py:290
  136.3 1.9 collective-permute-start.27
  138.2 4.9 %collective-permute-start.28 = (bf16[7,32,128]{2,1,0:T(8,128)(2,1)S(1)}, bf16[7,32,128]{2,1,0:T(8,128)(2,1)S(1)}, u32[]{:S(2)}, u32[]{:S(2)}) collective-permute-start(bf16[7,32,128]{2,1,0:T(8,128)(2,1)S(1)} %get-tuple-element.56), channel_id=1, source_target_pairs={{453,452},{461,460},{469,468},{477,476},{454,453},{462,461},{470,4... | collective-permute-start | bytes 172040 | tf_op jit(solution)/shard_map/ppermute | solution.py:290
  143.1 1.2 collective-permute-done.28.refs_3_
  144.9 1.9 collective-permute-start.29
  146.9 4.9 %collective-permute-start.30 = (bf16[7,32,128]{2,1,0:T(8,128)(2,1)S(1)}, bf16[7,32,128]{2,1,0:T(8,128)(2,1)S(1)}, u32[]{:S(2)}, u32[]{:S(2)}) collective-permute-start(bf16[7,32,128]{2,1,0:T(8,128)(2,1)S(1)} %get-tuple-element.54), channel_id=1, source_target_pairs={{453,452},{461,460},{469,468},{477,476},{454,453},{462,461},{470,4... | collective-permute-start | bytes 172040 | tf_op jit(solution)/shard_map/ppermute | solution.py:290
  153.6 1.9 collective-permute-start.31
  155.6 4.9 %collective-permute-start.32 = (bf16[7,32,128]{2,1,0:T(8,128)(2,1)S(1)}, bf16[7,32,128]{2,1,0:T(8,128)(2,1)S(1)}, u32[]{:S(2)}, u32[]{:S(2)}) collective-permute-start(bf16[7,32,128]{2,1,0:T(8,128)(2,1)S(1)} %get-tuple-element.52), channel_id=1, source_target_pairs={{453,452},{461,460},{469,468},{477,476},{454,453},{462,461},{470,4... | collective-permute-start | bytes 172040 | tf_op jit(solution)/shard_map/ppermute | solution.py:290
  160.5 1.2 collective-permute-done.32.refs_3_
  162.3 1.9 collective-permute-start.33
  164.3 5.0 %collective-permute-start.34 = (bf16[7,32,128]{2,1,0:T(8,128)(2,1)S(1)}, bf16[7,32,128]{2,1,0:T(8,128)(2,1)S(1)}, u32[]{:S(2)}, u32[]{:S(2)}) collective-permute-start(bf16[7,32,128]{2,1,0:T(8,128)(2,1)S(1)} %get-tuple-element.50), channel_id=1, source_target_pairs={{453,452},{461,460},{469,468},{477,476},{454,453},{462,461},{470,4... | collective-permute-start | bytes 172040 | tf_op jit(solution)/shard_map/ppermute | solution.py:290
  169.3 1.2 collective-permute-done.34.refs_3_
  171.2 1.9 collective-permute-start.35
  173.1 5.0 %collective-permute-start.36 = (bf16[7,32,128]{2,1,0:T(8,128)(2,1)S(1)}, bf16[7,32,128]{2,1,0:T(8,128)(2,1)S(1)}, u32[]{:S(2)}, u32[]{:S(2)}) collective-permute-start(bf16[7,32,128]{2,1,0:T(8,128)(2,1)S(1)} %get-tuple-element.48), channel_id=1, source_target_pairs={{453,452},{461,460},{469,468},{477,476},{454,453},{462,461},{470,4... | collective-permute-start | bytes 172040 | tf_op jit(solution)/shard_map/ppermute | solution.py:290
  178.2 1.2 collective-permute-done.36.refs_3_
  180.0 1.9 collective-permute-start.37
  181.9 4.9 %collective-permute-start.38 = (bf16[7,32,128]{2,1,0:T(8,128)(2,1)S(1)}, bf16[7,32,128]{2,1,0:T(8,128)(2,1)S(1)}, u32[]{:S(2)}, u32[]{:S(2)}) collective-permute-start(bf16[7,32,128]{2,1,0:T(8,128)(2,1)S(1)} %get-tuple-element.46), channel_id=1, source_target_pairs={{453,452},{461,460},{469,468},{477,476},{454,453},{462,461},{470,4... | collective-permute-start | bytes 172040 | tf_op jit(solution)/shard_map/ppermute | solution.py:290
  188.2 1.3 collective-permute-start.39
  189.5 1.4 collective-permute-done.39
  191.0 12.3 %all_to_all.11 = bf16[8,2,7,16,128]{4,3,2,1,0:T(8,128)(2,1)S(1)} all-to-all(bf16[8,2,7,16,128]{4,3,2,1,0:T(8,128)(2,1)S(1)} %broadcast_select_fusion), channel_id=1, replica_groups={{452,460,468,476,448,456,464,472},{508,484,492,500,504,480,488,496},{20..., dimensions={0} | all-to-all | bytes 917504 | tf_op jit(solution)/shard_map/all_to_all | solution.py:373
  203.2 8.6 %collective-permute-start.40 = (bf16[8,2,7,16,128]{4,3,2,1,0:T(8,128)(2,1)S(1)}, bf16[8,2,7,16,128]{4,3,2,1,0:T(8,128)(2,1)S(1)}, u32[]{:S(2)}, u32[]{:S(2)}) collective-permute-start(bf16[8,2,7,16,128]{4,3,2,1,0:T(8,128)(2,1)S(1)} %all_to_all.11), channel_id=1, source_target_pairs={{452,416},{453,417},{454,418},{455,419},{511,420},{510,421},{509,4... | collective-permute-start | bytes 1376264 | tf_op jit(solution)/shard_map/ppermute | solution.py:374
  211.9 32.3 %collective-permute-done.40.parts_ref = bf16[8,2,7,16,128]{4,3,2,1,0:T(8,128)(2,1)S(1)} collective-permute-done((bf16[8,2,7,16,128]{4,3,2,1,0:T(8,128)(2,1)S(1)}, bf16[8,2,7,16,128]{4,3,2,1,0:T(8,128)(2,1)S(1)}, u32[]{:S(2)}, u32[]{:S(2)}) %collective-permute-start.40) | collective-permute-done | bytes 458784 | tf_op jit(solution)/shard_map/ppermute | solution.py:374
  (92 shorter events, 24.4 us)
Async XLA Ops:
  0.7 0.9 copy-start
  2.9 20.7 %collective-permute-start.4 = (bf16[8,7,16,128]{3,2,1,0:T(8,128)(2,1)S(1)}, bf16[8,7,16,128]{3,2,1,0:T(8,128)(2,1)S(1)}, u32[]{:S(2)}, u32[]{:S(2)}) collective-permute-start(bf16[8,7,16,128]{3,2,1,0:T(8,128)(2,1)S(1)} %shard_map.61), channel_id=1, source_target_pairs={{416,452},{417,453},{418,454},{419,455},{420,511},{421,510},{422,5... | collective-permute-start | bytes 688136 | tf_op jit(solution)/shard_map/ppermute | solution.py:304
  16.4 1.1 copy-start.3
  18.6 38.3 %collective-permute-start = (bf16[1392,128]{1,0:T(8,128)(2,1)S(1)}, bf16[1392,128]{1,0:T(8,128)(2,1)S(1)}, u32[]{:S(2)}, u32[]{:S(2)}) collective-permute-start(bf16[1392,128]{1,0:T(8,128)(2,1)S(1)} %shard_map.59), channel_id=1, source_target_pairs={{480,460},{481,461},{482,462},{483,463},{484,487},{485,486},{486,4... | collective-permute-start | bytes 1069064 | tf_op jit(solution)/shard_map/ppermute | solution.py:305
  55.6 8.8 %collective-permute-start.5 = (bf16[8,7,16,128]{3,2,1,0:T(8,128)(2,1)S(1)}, bf16[8,7,16,128]{3,2,1,0:T(8,128)(2,1)S(1)}, u32[]{:S(2)}, u32[]{:S(2)}) collective-permute-start(bf16[8,7,16,128]{3,2,1,0:T(8,128)(2,1)S(1)} %all_to_all.10), channel_id=1, source_target_pairs={{0,4},{8,12},{16,20},{24,28},{32,36},{40,44},{48,52},{56,60},{64,6... | collective-permute-start | bytes 688136 | tf_op jit(solution)/shard_map/ppermute | solution.py:320
  56.9 14.1 %collective-permute-start.1 = (bf16[1392,128]{1,0:T(8,128)(2,1)S(1)}, bf16[1392,128]{1,0:T(8,128)(2,1)S(1)}, u32[]{:S(2)}, u32[]{:S(2)}) collective-permute-start(bf16[1392,128]{1,0:T(8,128)(2,1)S(1)} %shard_map.60), channel_id=1, source_target_pairs={{4,12},{12,20},{20,28},{28,4},{36,44},{44,52},{52,60},{60,36},{68,... | collective-permute-start | bytes 1069064 | tf_op jit(solution)/shard_map/ppermute | solution.py:312
  59.0 12.1 %collective-permute-start.2 = (bf16[1392,128]{1,0:T(8,128)(2,1)S(1)}, bf16[1392,128]{1,0:T(8,128)(2,1)S(1)}, u32[]{:S(2)}, u32[]{:S(2)}) collective-permute-start(bf16[1392,128]{1,0:T(8,128)(2,1)S(1)} %shard_map.60), channel_id=1, source_target_pairs={{4,20},{12,28},{20,4},{28,12},{36,52},{44,60},{52,36},{60,44},{68,... | collective-permute-start | bytes 1069064 | tf_op jit(solution)/shard_map/ppermute | solution.py:312
  62.5 10.0 %collective-permute-start.3 = (bf16[1392,128]{1,0:T(8,128)(2,1)S(1)}, bf16[1392,128]{1,0:T(8,128)(2,1)S(1)}, u32[]{:S(2)}, u32[]{:S(2)}) collective-permute-start(bf16[1392,128]{1,0:T(8,128)(2,1)S(1)} %shard_map.60), channel_id=1, source_target_pairs={{4,28},{12,4},{20,12},{28,20},{36,60},{44,36},{52,44},{60,52},{68,... | collective-permute-start | bytes 1069064 | tf_op jit(solution)/shard_map/ppermute | solution.py:312
  64.5 8.7 %copy-start.5 = (bf16[7,32,128]{2,1,0:T(8,128)(2,1)}, bf16[7,32,128]{2,1,0:T(8,128)(2,1)S(1)}, u32[]{:S(2)}) copy-start(bf16[7,32,128]{2,1,0:T(8,128)(2,1)S(1)} %slice_bitcast_fusion.refs_1_.refs_0_) | copy-start | bytes 172036
  64.5 7.9 %collective-permute-start.6 = (bf16[7,32,128]{2,1,0:T(8,128)(2,1)S(1)}, bf16[7,32,128]{2,1,0:T(8,128)(2,1)S(1)}, u32[]{:S(2)}, u32[]{:S(2)}) collective-permute-start(bf16[7,32,128]{2,1,0:T(8,128)(2,1)S(1)} %slice_bitcast_fusion.refs_1_.refs_0_), channel_id=1, source_target_pairs={{452,453},{460,461},{468,469},{476,477},{453,454},{461,462},{469,4... | collective-permute-start | bytes 172040 | tf_op jit(solution)/shard_map/ppermute | solution.py:290
  66.4 6.0 %collective-permute-start.7 = (bf16[7,32,128]{2,1,0:T(8,128)(2,1)S(1)}, bf16[7,32,128]{2,1,0:T(8,128)(2,1)S(1)}, u32[]{:S(2)}, u32[]{:S(2)}) collective-permute-start(bf16[7,32,128]{2,1,0:T(8,128)(2,1)S(1)} %slice_bitcast_fusion.refs_1_.refs_0_), channel_id=1, source_target_pairs={{453,452},{461,460},{469,468},{477,476},{454,453},{462,461},{470,4... | collective-permute-start | bytes 172040 | tf_op jit(solution)/shard_map/ppermute | solution.py:290
  73.2 10.7 %copy-start.7 = (bf16[7,32,128]{2,1,0:T(8,128)(2,1)}, bf16[7,32,128]{2,1,0:T(8,128)(2,1)S(1)}, u32[]{:S(2)}) copy-start(bf16[7,32,128]{2,1,0:T(8,128)(2,1)S(1)} %shard_map.62.refs_1_.refs_0_) | copy-start | bytes 172036
  73.2 8.1 %collective-permute-start.12 = (bf16[7,32,128]{2,1,0:T(8,128)(2,1)S(1)}, bf16[7,32,128]{2,1,0:T(8,128)(2,1)S(1)}, u32[]{:S(2)}, u32[]{:S(2)}) collective-permute-start(bf16[7,32,128]{2,1,0:T(8,128)(2,1)S(1)} %shard_map.62.refs_1_.refs_0_), channel_id=1, source_target_pairs={{4,0},{12,8},{20,16},{28,24},{36,32},{44,40},{52,48},{60,56},{68,6... | collective-permute-start | bytes 172040 | tf_op jit(solution)/shard_map/ppermute | solution.py:327
  74.5 8.9 %collective-permute-start.8 = (bf16[7,32,128]{2,1,0:T(8,128)(2,1)S(1)}, bf16[7,32,128]{2,1,0:T(8,128)(2,1)S(1)}, u32[]{:S(2)}, u32[]{:S(2)}) collective-permute-start(bf16[7,32,128]{2,1,0:T(8,128)(2,1)S(1)} %shard_map.62.refs_1_.refs_0_), channel_id=1, source_target_pairs={{452,453},{460,461},{468,469},{476,477},{453,454},{461,462},{469,4... | collective-permute-start | bytes 172040 | tf_op jit(solution)/shard_map/ppermute | solution.py:290
  76.4 7.0 %collective-permute-start.9 = (bf16[7,32,128]{2,1,0:T(8,128)(2,1)S(1)}, bf16[7,32,128]{2,1,0:T(8,128)(2,1)S(1)}, u32[]{:S(2)}, u32[]{:S(2)}) collective-permute-start(bf16[7,32,128]{2,1,0:T(8,128)(2,1)S(1)} %shard_map.62.refs_1_.refs_0_), channel_id=1, source_target_pairs={{453,452},{461,460},{469,468},{477,476},{454,453},{462,461},{470,4... | collective-permute-start | bytes 172040 | tf_op jit(solution)/shard_map/ppermute | solution.py:290
  81.4 9.1 %collective-permute-start.13 = (bf16[1616,128]{1,0:T(8,128)(2,1)S(1)}, bf16[1616,128]{1,0:T(8,128)(2,1)S(1)}, u32[]{:S(2)}, u32[]{:S(2)}) collective-permute-start(bf16[1616,128]{1,0:T(8,128)(2,1)S(1)} %get-tuple-element.45), channel_id=1, source_target_pairs={{0,8},{8,16},{16,24},{24,0},{32,40},{40,48},{48,56},{56,32},{64,72... | collective-permute-start | bytes 1241096 | tf_op jit(solution)/shard_map/ppermute | solution.py:312
  82.1 8.4 %collective-permute-start.14 = (bf16[1616,128]{1,0:T(8,128)(2,1)S(1)}, bf16[1616,128]{1,0:T(8,128)(2,1)S(1)}, u32[]{:S(2)}, u32[]{:S(2)}) collective-permute-start(bf16[1616,128]{1,0:T(8,128)(2,1)S(1)} %get-tuple-element.45), channel_id=1, source_target_pairs={{0,16},{8,24},{16,0},{24,8},{32,48},{40,56},{48,32},{56,40},{64,80... | collective-permute-start | bytes 1241096 | tf_op jit(solution)/shard_map/ppermute | solution.py:312
  82.8 7.7 %collective-permute-start.15 = (bf16[1616,128]{1,0:T(8,128)(2,1)S(1)}, bf16[1616,128]{1,0:T(8,128)(2,1)S(1)}, u32[]{:S(2)}, u32[]{:S(2)}) collective-permute-start(bf16[1616,128]{1,0:T(8,128)(2,1)S(1)} %get-tuple-element.45), channel_id=1, source_target_pairs={{0,24},{8,0},{16,8},{24,16},{32,56},{40,32},{48,40},{56,48},{64,88... | collective-permute-start | bytes 1241096 | tf_op jit(solution)/shard_map/ppermute | solution.py:312
  83.9 8.1 %collective-permute-start.10 = (bf16[7,32,128]{2,1,0:T(8,128)(2,1)S(1)}, bf16[7,32,128]{2,1,0:T(8,128)(2,1)S(1)}, u32[]{:S(2)}, u32[]{:S(2)}) collective-permute-start(bf16[7,32,128]{2,1,0:T(8,128)(2,1)S(1)} %shard_map.63.refs_1_.refs_0_.refs_2_), channel_id=1, source_target_pairs={{452,453},{460,461},{468,469},{476,477},{453,454},{461,462},{469,4... | collective-permute-start | bytes 172040 | tf_op jit(solution)/shard_map/ppermute | solution.py:290
  85.9 6.1 %collective-permute-start.11 = (bf16[7,32,128]{2,1,0:T(8,128)(2,1)S(1)}, bf16[7,32,128]{2,1,0:T(8,128)(2,1)S(1)}, u32[]{:S(2)}, u32[]{:S(2)}) collective-permute-start(bf16[7,32,128]{2,1,0:T(8,128)(2,1)S(1)} %shard_map.63.refs_1_.refs_0_.refs_2_), channel_id=1, source_target_pairs={{453,452},{461,460},{469,468},{477,476},{454,453},{462,461},{470,4... | collective-permute-start | bytes 172040 | tf_op jit(solution)/shard_map/ppermute | solution.py:290
  90.7 10.1 %collective-permute-start.16 = (bf16[4,1616,128]{2,1,0:T(8,128)(2,1)S(1)}, bf16[4,1616,128]{2,1,0:T(8,128)(2,1)S(1)}, u32[]{:S(2)}, u32[]{:S(2)}) collective-permute-start(bf16[4,1616,128]{2,1,0:T(8,128)(2,1)S(1)} %pad_maximum_fusion), channel_id=1, source_target_pairs={{0,4},{8,12},{16,20},{24,28},{32,36},{40,44},{48,52},{56,60},{64,6... | collective-permute-start | bytes 4964360 | tf_op jit(solution)/shard_map/ppermute | solution.py:329
  92.5 8.4 %collective-permute-start.17 = (bf16[7,32,128]{2,1,0:T(8,128)(2,1)S(1)}, bf16[7,32,128]{2,1,0:T(8,128)(2,1)S(1)}, u32[]{:S(2)}, u32[]{:S(2)}) collective-permute-start(bf16[7,32,128]{2,1,0:T(8,128)(2,1)S(1)} %shard_map.64.refs_1_.refs_0_.refs_3_), channel_id=1, source_target_pairs={{452,453},{460,461},{468,469},{476,477},{453,454},{461,462},{469,4... | collective-permute-start | bytes 172040 | tf_op jit(solution)/shard_map/ppermute | solution.py:290
  94.4 6.4 %collective-permute-start.18 = (bf16[7,32,128]{2,1,0:T(8,128)(2,1)S(1)}, bf16[7,32,128]{2,1,0:T(8,128)(2,1)S(1)}, u32[]{:S(2)}, u32[]{:S(2)}) collective-permute-start(bf16[7,32,128]{2,1,0:T(8,128)(2,1)S(1)} %shard_map.64.refs_1_.refs_0_.refs_3_), channel_id=1, source_target_pairs={{453,452},{461,460},{469,468},{477,476},{454,453},{462,461},{470,4... | collective-permute-start | bytes 172040 | tf_op jit(solution)/shard_map/ppermute | solution.py:290
  101.3 6.8 %collective-permute-start.19 = (bf16[7,32,128]{2,1,0:T(8,128)(2,1)S(1)}, bf16[7,32,128]{2,1,0:T(8,128)(2,1)S(1)}, u32[]{:S(2)}, u32[]{:S(2)}) collective-permute-start(bf16[7,32,128]{2,1,0:T(8,128)(2,1)S(1)} %shard_map.65.refs_1_.refs_0_.refs_4_), channel_id=1, source_target_pairs={{452,453},{460,461},{468,469},{476,477},{453,454},{461,462},{469,4... | collective-permute-start | bytes 172040 | tf_op jit(solution)/shard_map/ppermute | solution.py:290
  103.2 6.1 %collective-permute-start.20 = (bf16[7,32,128]{2,1,0:T(8,128)(2,1)S(1)}, bf16[7,32,128]{2,1,0:T(8,128)(2,1)S(1)}, u32[]{:S(2)}, u32[]{:S(2)}) collective-permute-start(bf16[7,32,128]{2,1,0:T(8,128)(2,1)S(1)} %shard_map.65.refs_1_.refs_0_.refs_4_), channel_id=1, source_target_pairs={{453,452},{461,460},{469,468},{477,476},{454,453},{462,461},{470,4... | collective-permute-start | bytes 172040 | tf_op jit(solution)/shard_map/ppermute | solution.py:290
  109.8 6.8 %collective-permute-start.21 = (bf16[7,32,128]{2,1,0:T(8,128)(2,1)S(1)}, bf16[7,32,128]{2,1,0:T(8,128)(2,1)S(1)}, u32[]{:S(2)}, u32[]{:S(2)}) collective-permute-start(bf16[7,32,128]{2,1,0:T(8,128)(2,1)S(1)} %shard_map.66.refs_1_.refs_0_.refs_5_), channel_id=1, source_target_pairs={{452,453},{460,461},{468,469},{476,477},{453,454},{461,462},{469,4... | collective-permute-start | bytes 172040 | tf_op jit(solution)/shard_map/ppermute | solution.py:290
  111.8 6.1 %collective-permute-start.22 = (bf16[7,32,128]{2,1,0:T(8,128)(2,1)S(1)}, bf16[7,32,128]{2,1,0:T(8,128)(2,1)S(1)}, u32[]{:S(2)}, u32[]{:S(2)}) collective-permute-start(bf16[7,32,128]{2,1,0:T(8,128)(2,1)S(1)} %shard_map.66.refs_1_.refs_0_.refs_5_), channel_id=1, source_target_pairs={{453,452},{461,460},{469,468},{477,476},{454,453},{462,461},{470,4... | collective-permute-start | bytes 172040 | tf_op jit(solution)/shard_map/ppermute | solution.py:290
  118.4 6.8 %collective-permute-start.23 = (bf16[7,32,128]{2,1,0:T(8,128)(2,1)S(1)}, bf16[7,32,128]{2,1,0:T(8,128)(2,1)S(1)}, u32[]{:S(2)}, u32[]{:S(2)}) collective-permute-start(bf16[7,32,128]{2,1,0:T(8,128)(2,1)S(1)} %shard_map.67.refs_1_.refs_0_.refs_6_), channel_id=1, source_target_pairs={{452,453},{460,461},{468,469},{476,477},{453,454},{461,462},{469,4... | collective-permute-start | bytes 172040 | tf_op jit(solution)/shard_map/ppermute | solution.py:290
  120.3 6.1 %collective-permute-start.24 = (bf16[7,32,128]{2,1,0:T(8,128)(2,1)S(1)}, bf16[7,32,128]{2,1,0:T(8,128)(2,1)S(1)}, u32[]{:S(2)}, u32[]{:S(2)}) collective-permute-start(bf16[7,32,128]{2,1,0:T(8,128)(2,1)S(1)} %shard_map.67.refs_1_.refs_0_.refs_6_), channel_id=1, source_target_pairs={{453,452},{461,460},{469,468},{477,476},{454,453},{462,461},{470,4... | collective-permute-start | bytes 172040 | tf_op jit(solution)/shard_map/ppermute | solution.py:290
  127.6 6.8 %collective-permute-start.25 = (bf16[7,32,128]{2,1,0:T(8,128)(2,1)S(1)}, bf16[7,32,128]{2,1,0:T(8,128)(2,1)S(1)}, u32[]{:S(2)}, u32[]{:S(2)}) collective-permute-start(bf16[7,32,128]{2,1,0:T(8,128)(2,1)S(1)} %get-tuple-element.59), channel_id=1, source_target_pairs={{452,453},{460,461},{468,469},{476,477},{453,454},{461,462},{469,4... | collective-permute-start | bytes 172040 | tf_op jit(solution)/shard_map/ppermute | solution.py:290
  129.5 6.1 %collective-permute-start.26 = (bf16[7,32,128]{2,1,0:T(8,128)(2,1)S(1)}, bf16[7,32,128]{2,1,0:T(8,128)(2,1)S(1)}, u32[]{:S(2)}, u32[]{:S(2)}) collective-permute-start(bf16[7,32,128]{2,1,0:T(8,128)(2,1)S(1)} %get-tuple-element.58), channel_id=1, source_target_pairs={{453,452},{461,460},{469,468},{477,476},{454,453},{462,461},{470,4... | collective-permute-start | bytes 172040 | tf_op jit(solution)/shard_map/ppermute | solution.py:290
  136.3 6.8 %collective-permute-start.27 = (bf16[7,32,128]{2,1,0:T(8,128)(2,1)S(1)}, bf16[7,32,128]{2,1,0:T(8,128)(2,1)S(1)}, u32[]{:S(2)}, u32[]{:S(2)}) collective-permute-start(bf16[7,32,128]{2,1,0:T(8,128)(2,1)S(1)} %get-tuple-element.57), channel_id=1, source_target_pairs={{452,453},{460,461},{468,469},{476,477},{453,454},{461,462},{469,4... | collective-permute-start | bytes 172040 | tf_op jit(solution)/shard_map/ppermute | solution.py:290
  138.2 6.1 %collective-permute-start.28 = (bf16[7,32,128]{2,1,0:T(8,128)(2,1)S(1)}, bf16[7,32,128]{2,1,0:T(8,128)(2,1)S(1)}, u32[]{:S(2)}, u32[]{:S(2)}) collective-permute-start(bf16[7,32,128]{2,1,0:T(8,128)(2,1)S(1)} %get-tuple-element.56), channel_id=1, source_target_pairs={{453,452},{461,460},{469,468},{477,476},{454,453},{462,461},{470,4... | collective-permute-start | bytes 172040 | tf_op jit(solution)/shard_map/ppermute | solution.py:290
  144.9 6.8 %collective-permute-start.29 = (bf16[7,32,128]{2,1,0:T(8,128)(2,1)S(1)}, bf16[7,32,128]{2,1,0:T(8,128)(2,1)S(1)}, u32[]{:S(2)}, u32[]{:S(2)}) collective-permute-start(bf16[7,32,128]{2,1,0:T(8,128)(2,1)S(1)} %get-tuple-element.55), channel_id=1, source_target_pairs={{452,453},{460,461},{468,469},{476,477},{453,454},{461,462},{469,4... | collective-permute-start | bytes 172040 | tf_op jit(solution)/shard_map/ppermute | solution.py:290
  146.9 6.1 %collective-permute-start.30 = (bf16[7,32,128]{2,1,0:T(8,128)(2,1)S(1)}, bf16[7,32,128]{2,1,0:T(8,128)(2,1)S(1)}, u32[]{:S(2)}, u32[]{:S(2)}) collective-permute-start(bf16[7,32,128]{2,1,0:T(8,128)(2,1)S(1)} %get-tuple-element.54), channel_id=1, source_target_pairs={{453,452},{461,460},{469,468},{477,476},{454,453},{462,461},{470,4... | collective-permute-start | bytes 172040 | tf_op jit(solution)/shard_map/ppermute | solution.py:290
  153.6 6.8 %collective-permute-start.31 = (bf16[7,32,128]{2,1,0:T(8,128)(2,1)S(1)}, bf16[7,32,128]{2,1,0:T(8,128)(2,1)S(1)}, u32[]{:S(2)}, u32[]{:S(2)}) collective-permute-start(bf16[7,32,128]{2,1,0:T(8,128)(2,1)S(1)} %get-tuple-element.53), channel_id=1, source_target_pairs={{452,453},{460,461},{468,469},{476,477},{453,454},{461,462},{469,4... | collective-permute-start | bytes 172040 | tf_op jit(solution)/shard_map/ppermute | solution.py:290
  155.6 6.1 %collective-permute-start.32 = (bf16[7,32,128]{2,1,0:T(8,128)(2,1)S(1)}, bf16[7,32,128]{2,1,0:T(8,128)(2,1)S(1)}, u32[]{:S(2)}, u32[]{:S(2)}) collective-permute-start(bf16[7,32,128]{2,1,0:T(8,128)(2,1)S(1)} %get-tuple-element.52), channel_id=1, source_target_pairs={{453,452},{461,460},{469,468},{477,476},{454,453},{462,461},{470,4... | collective-permute-start | bytes 172040 | tf_op jit(solution)/shard_map/ppermute | solution.py:290
  162.3 7.0 %collective-permute-start.33 = (bf16[7,32,128]{2,1,0:T(8,128)(2,1)S(1)}, bf16[7,32,128]{2,1,0:T(8,128)(2,1)S(1)}, u32[]{:S(2)}, u32[]{:S(2)}) collective-permute-start(bf16[7,32,128]{2,1,0:T(8,128)(2,1)S(1)} %get-tuple-element.51), channel_id=1, source_target_pairs={{452,453},{460,461},{468,469},{476,477},{453,454},{461,462},{469,4... | collective-permute-start | bytes 172040 | tf_op jit(solution)/shard_map/ppermute | solution.py:290
  164.3 15.1 %copy-start.8 = (bf16[7,32,128]{2,1,0:T(8,128)(2,1)S(1)}, bf16[7,32,128]{2,1,0:T(8,128)(2,1)}, u32[]{:S(2)}) copy-start(bf16[7,32,128]{2,1,0:T(8,128)(2,1)} %copy-done.7) | copy-start | bytes 172036
  164.3 6.3 %collective-permute-start.34 = (bf16[7,32,128]{2,1,0:T(8,128)(2,1)S(1)}, bf16[7,32,128]{2,1,0:T(8,128)(2,1)S(1)}, u32[]{:S(2)}, u32[]{:S(2)}) collective-permute-start(bf16[7,32,128]{2,1,0:T(8,128)(2,1)S(1)} %get-tuple-element.50), channel_id=1, source_target_pairs={{453,452},{461,460},{469,468},{477,476},{454,453},{462,461},{470,4... | collective-permute-start | bytes 172040 | tf_op jit(solution)/shard_map/ppermute | solution.py:290
  171.2 7.0 %collective-permute-start.35 = (bf16[7,32,128]{2,1,0:T(8,128)(2,1)S(1)}, bf16[7,32,128]{2,1,0:T(8,128)(2,1)S(1)}, u32[]{:S(2)}, u32[]{:S(2)}) collective-permute-start(bf16[7,32,128]{2,1,0:T(8,128)(2,1)S(1)} %get-tuple-element.49), channel_id=1, source_target_pairs={{452,453},{460,461},{468,469},{476,477},{453,454},{461,462},{469,4... | collective-permute-start | bytes 172040 | tf_op jit(solution)/shard_map/ppermute | solution.py:290
  173.1 15.0 %copy-start.6 = (bf16[7,32,128]{2,1,0:T(8,128)(2,1)S(1)}, bf16[7,32,128]{2,1,0:T(8,128)(2,1)}, u32[]{:S(2)}) copy-start(bf16[7,32,128]{2,1,0:T(8,128)(2,1)} %copy-done.5) | copy-start | bytes 172036
  173.1 6.3 %collective-permute-start.36 = (bf16[7,32,128]{2,1,0:T(8,128)(2,1)S(1)}, bf16[7,32,128]{2,1,0:T(8,128)(2,1)S(1)}, u32[]{:S(2)}, u32[]{:S(2)}) collective-permute-start(bf16[7,32,128]{2,1,0:T(8,128)(2,1)S(1)} %get-tuple-element.48), channel_id=1, source_target_pairs={{453,452},{461,460},{469,468},{477,476},{454,453},{462,461},{470,4... | collective-permute-start | bytes 172040 | tf_op jit(solution)/shard_map/ppermute | solution.py:290
  180.0 6.8 %collective-permute-start.37 = (bf16[7,32,128]{2,1,0:T(8,128)(2,1)S(1)}, bf16[7,32,128]{2,1,0:T(8,128)(2,1)S(1)}, u32[]{:S(2)}, u32[]{:S(2)}) collective-permute-start(bf16[7,32,128]{2,1,0:T(8,128)(2,1)S(1)} %get-tuple-element.47), channel_id=1, source_target_pairs={{452,453},{460,461},{468,469},{476,477},{453,454},{461,462},{469,4... | collective-permute-start | bytes 172040 | tf_op jit(solution)/shard_map/ppermute | solution.py:290
  181.9 6.1 %collective-permute-start.38 = (bf16[7,32,128]{2,1,0:T(8,128)(2,1)S(1)}, bf16[7,32,128]{2,1,0:T(8,128)(2,1)S(1)}, u32[]{:S(2)}, u32[]{:S(2)}) collective-permute-start(bf16[7,32,128]{2,1,0:T(8,128)(2,1)S(1)} %get-tuple-element.46), channel_id=1, source_target_pairs={{453,452},{461,460},{469,468},{477,476},{454,453},{462,461},{470,4... | collective-permute-start | bytes 172040 | tf_op jit(solution)/shard_map/ppermute | solution.py:290
  188.1 56.1 %copy-start.2 = (bf16[14,64,64]{2,1,0:T(8,128)(2,1)S(1)}, bf16[14,64,64]{2,1,0:T(8,128)(2,1)}, u32[]{:S(2)}) copy-start(bf16[14,64,64]{2,1,0:T(8,128)(2,1)} %diag_ref.5) | copy-start | bytes 344068
  188.2 2.7 %collective-permute-start.39 = (bf16[8,2,7,16,128]{4,3,2,1,0:T(8,128)(2,1)S(1)}, bf16[8,2,7,16,128]{4,3,2,1,0:T(8,128)(2,1)S(1)}, u32[]{:S(2)}, u32[]{:S(2)}) collective-permute-start(bf16[8,2,7,16,128]{4,3,2,1,0:T(8,128)(2,1)S(1)} %get-tuple-element.43), channel_id=1, source_target_pairs={{4,0},{12,8},{20,16},{28,24},{36,32},{44,40},{52,48},{60,56},{68,6... | collective-permute-start | bytes 1376264 | tf_op jit(solution)/shard_map/ppermute | solution.py:371
  203.2 40.9 %collective-permute-start.40 = (bf16[8,2,7,16,128]{4,3,2,1,0:T(8,128)(2,1)S(1)}, bf16[8,2,7,16,128]{4,3,2,1,0:T(8,128)(2,1)S(1)}, u32[]{:S(2)}, u32[]{:S(2)}) collective-permute-start(bf16[8,2,7,16,128]{4,3,2,1,0:T(8,128)(2,1)S(1)} %all_to_all.11), channel_id=1, source_target_pairs={{452,416},{453,417},{454,418},{455,419},{511,420},{510,421},{509,4... | collective-permute-start | bytes 1376264 | tf_op jit(solution)/shard_map/ppermute | solution.py:374
  (3 other events, 2.6 us)

commit v5 on v4

--- a/solution.py
+++ b/solution.py
@@ -63,6 +63,17 @@
     ]
 
 
+def home_pairs(same):
+    pairs = []
+    for level in range(LEVELS):
+        for rank in range(RANKS):
+            band = rank // 4
+            if (level // CHUNK == band % 2) == same:
+                source = place_slot(rank, (level - band) % 4 * 2)
+                pairs.append((source, native(level, rank) - band % 2 * 4))
+    return pairs
+
+
 def neighbour_pairs(step):
     return [
         (place_slot(rank, slot), place_slot(rank + step, slot))
@@ -130,20 +141,31 @@
         put_block(out_ref, i * ORDER, jnp.concatenate(couplings, axis=1).astype(BF16))
 
 
-def finish_kernel(shift_ref, parts_ref, diag_ref, forward_ref, backward_ref):
-    for i in range(PAIRS):
-        for kind in range(2):
-            columns = jnp.concatenate(
-                [parts_ref[turn_of_slot(j, shift_ref[0, 0]), kind, i] for j in range(COLS // PART)], axis=0
-            )
-            turned = columns.astype(F32).T.astype(BF16)
-            for n, rows in ((i, turned[:ORDER]), (i + PAIRS, turned[ORDER:])):
-                if kind == 0:
-                    forward_ref[n] = rows
-                else:
-                    backward_ref[n] = lax.dot_general(
-                        diag_ref[n], rows, (((0,), (0,)), ((), ())), preferred_element_type=F32
-                    ).astype(BF16)
+def finish_forward_kernel(home_ref, parts_ref, out_ref):
+    home = home_ref[0, 0]
+    for i in range(PAIRS):
+        columns = jnp.concatenate([parts_ref[(home + 4 - x) & 3, i] for x in range(4)], axis=0)
+        turned = columns.astype(F32).T.astype(BF16)
+        out_ref[i] = turned[:ORDER]
+        out_ref[i + PAIRS] = turned[ORDER:]
+
+
+def finish_backward_kernel(shift_ref, parts_ref, diag_ref, out_ref):
+    shift = shift_ref[0, 0]
+    for i in range(PAIRS):
+        columns = jnp.concatenate(
+            [parts_ref[turn_of_slot(j, shift), i] for j in range(COLS // PART)], axis=0
+        )
+        turned = columns.astype(F32).T.astype(BF16)
+        for n, reduced in ((i, turned[:ORDER]), (i + PAIRS, turned[ORDER:])):
+            out_ref[n] = lax.dot_general(
+                diag_ref[n], reduced, (((0,), (0,)), ((), ())), preferred_element_type=F32
+            ).astype(BF16)
+
+
+def pack_kernel(state_ref, *refs):
+    for level in range(LEVELS):
+        refs[LEVELS][(level + LEVELS - state_ref[0, 0]) & 3, level // CHUNK] = refs[level][...]
 
 
 def copy_kernel(source_ref, out_ref):
@@ -265,15 +287,14 @@
     spread(pattern, weights, reduced, sums_ref, total_ref)
 
 
-def last_kernel(sums_ref, below_ref, above_ref, *refs):
-    forward, reduced, last_ref = refs[:LEVELS], refs[LEVELS:-3], refs[-1]
-    reduce(forward[0], sums_ref, below_ref, above_ref, last_ref)
+def last_kernel(forward_ref, sums_ref, below_ref, above_ref, *refs):
+    reduced, last_ref = refs[:-3], refs[-1]
+    reduce(forward_ref, sums_ref, below_ref, above_ref, last_ref)
     for core in range(2):
         columns = pl.ds(core * PART, PART)
         for level in range(LEVELS):
-            refs[core - 3][level, 0] = forward[level][:, columns, :]
             back_ref = reduced[level - 1] if level else last_ref
-            refs[core - 3][level, 1] = back_ref[:, columns, :]
+            refs[core - 3][level] = back_ref[:, columns, :]
 
 
 def per_device(right_side, factor_blocks, diag_inverse, pattern):
@@ -352,9 +373,29 @@
             high = gather_high(latest)
     (sums,) = rest
 
+    (packed,) = call(pack_kernel, [((4, 2, PAIRS, BOTH, 128), BF16)], (state.reshape(1, 1), *forward))
+    packed = lax.ppermute(packed, "lvl", to_first)
+    band_odd, stored_low = plane % 2 == 1, (lvl + ROTATION // 4) % 128 // 16 < CHUNK
+    stored_level = (lvl + ROTATION // 4) % 128 // 16
+    home = ((stored_level + 4 - (x * 2 + core) % 4) % 4).astype(jnp.int32).reshape(1, 1)
+
     reduced = [latest]
     for level in range(LEVELS - 2, 0, -1):
         below, above = exchange(sums[2], sums[0])
+        if level == 5:
+            below, above, packed = lax.optimization_barrier((below, above, packed))
+            near_parts = [packed[0]]
+            for steps in (1, 2, 3):
+                pairs = [(i, i // 8 * 8 + (i % 8 + 2 * steps) % 8) for i in range(0, 128, 2)]
+                near_parts.append(lax.ppermute(packed[steps], "lvl", pairs))
+        if level == 3:
+            below, above, *near_parts = lax.optimization_barrier((below, above, *near_parts))
+            low_parts = jnp.stack([part[0] for part in near_parts])
+            high_parts = jnp.stack([part[1] for part in near_parts])
+            same = lax.ppermute(jnp.where(band_odd, high_parts, low_parts), AXES, home_pairs(True))
+            swapped = lax.ppermute(jnp.where(band_odd, low_parts, high_parts), AXES, home_pairs(False))
+        if level == 1:
+            below, above, same, swapped = lax.optimization_barrier((below, above, same, swapped))
         latest, sums = level_call(
             level,
             backward_step,
@@ -364,16 +405,23 @@
         )
         reduced.append(latest)
     below, above = exchange(sums[2], sums[0])
-    packed_shape = ((LEVELS, 2, PAIRS, PART, 128), BF16)
+    packed_shape = ((LEVELS, PAIRS, PART, 128), BF16)
     for_first, for_second = call(
-        last_kernel, [packed_shape] * 2, (sums, below, above, *forward, *reduced[::-1]), [VMEM(*solved_shape)]
+        last_kernel,
+        [packed_shape] * 2,
+        (forward[0], sums, below, above, *reduced[::-1]),
+        [VMEM(*solved_shape)],
     )
     packed = jnp.where(core == 1, for_second, lax.ppermute(for_first, "lvl", to_first))
-
     parts = lax.all_to_all(packed, "lvl", 0, 0, axis_index_groups=groups)
     parts = lax.ppermute(parts, AXES, to_native)
     out_shape = ((SLOTS, ORDER, COLS), BF16)
-    return call(finish_kernel, [out_shape] * 2, (shift, parts, diag_inverse))
+    (backward_out,) = call(finish_backward_kernel, [out_shape], (shift, parts, diag_inverse))
+    forward_parts = jnp.where(stored_low, same, swapped)
+    other_parts = lax.ppermute(jnp.where(stored_low, swapped, same), "lvl", to_second)
+    forward_parts = jnp.where(core == 1, other_parts, forward_parts)
+    (forward_out,) = call(finish_forward_kernel, [out_shape], (home, forward_parts))
+    return forward_out, backward_out
 
 
 def solution(mesh):

time: 247 us -> 238 us (0.964)
  the two profiles are of different devices: /device:TPU:135 before, /device:TPU:10 now
where the time goes in v5:
time: 238 us; the launch traced here: 237 us
  starting transfers between devices  112 us (47%)
  waiting for transfers between devices  78.6 us (33%)
  blocking collectives  26.5 us (11%)
  Pallas kernels  11.2 us (5%)
  local copies, waits for them, and re-layouts  4.93 us (2%)
    ppermute x1, waiting for transfers between devices, per_device(): packed = lax.ppermute(packed, 'lvl', to_first)  27.2 us
    all_to_all x1, blocking collectives, per_device(): rhs = lax.all_to_all(rhs, 'lvl', 0, 0, axis_index_groups=groups)  26.5 us
    ppermute x1, starting transfers between devices, per_device(): rhs = lax.ppermute(rhs, AXES, to_group)  16.7 us
    ppermute x1, starting transfers between devices, per_device(): parts = lax.ppermute(parts, AXES, to_native)  14.5 us
    ppermute x1, waiting for transfers between devices, gather_high(): ready = lax.ppermute(solved, 'lvl', to_first).reshape(PAIRS * BOTH, 128)  14.5 us
    ppermute x1, waiting for transfers between devices, per_device(): parts = lax.ppermute(parts, AXES, to_native)  11.2 us
    pallas_call x20, Pallas kernels, call(): pl.pallas_call(kernel, out_shape=[jax.ShapeDtypeStruct(shape, dtype) for...  11.2 us
    ppermute x3, starting transfers between devices, per_device(): near_parts.append(lax.ppermute(packed[steps], 'lvl', pairs))  10.7 us
  transfers between devices with their start and end apart: 49, of which 10 were waited for; matrix products, arithmetic and copies ran while one was open for 1% of the time, Pallas kernels for 2%

profile of v5, /device:TPU:10, one launch (start us, length us, event | category | flops | bytes accessed | tf_op | source)
XLA Modules:
  0.0 236.6 jit_solution(9978562702378095515)
XLA Ops:
  0.7 0.9 copy-done
  1.6 0.9 copy-done.4
  2.9 16.7 %collective-permute-start.4 = (bf16[8,7,16,128]{3,2,1,0:T(8,128)(2,1)S(1)}, bf16[8,7,16,128]{3,2,1,0:T(8,128)(2,1)S(1)}, u32[]{:S(2)}, u32[]{:S(2)}) collective-permute-start(bf16[8,7,16,128]{3,2,1,0:T(8,128)(2,1)S(1)} %shard_map.61), channel_id=1, source_target_pairs={{416,452},{417,453},{418,454},{419,455},{420,511},{421,510},{422,5... | collective-permute-start | bytes 688136 | tf_op jit(solution)/shard_map/ppermute | solution.py:325
  19.6 0.9 copy-done.1
  20.6 1.1 copy-done.3
  21.7 0.7 copy-done.5
  22.7 6.3 %collective-permute-start = (bf16[1392,128]{1,0:T(8,128)(2,1)S(1)}, bf16[1392,128]{1,0:T(8,128)(2,1)S(1)}, u32[]{:S(2)}, u32[]{:S(2)}) collective-permute-start(bf16[1392,128]{1,0:T(8,128)(2,1)S(1)} %shard_map.59), channel_id=1, source_target_pairs={{480,460},{481,461},{482,462},{483,463},{484,487},{485,486},{486,4... | collective-permute-start | bytes 1069064 | tf_op jit(solution)/shard_map/ppermute | solution.py:326
  29.1 26.5 %all_to_all.10 = bf16[8,7,16,128]{3,2,1,0:T(8,128)(2,1)S(1)} all-to-all(bf16[8,7,16,128]{3,2,1,0:T(8,128)(2,1)S(1)} %collective-permute-done.4), channel_id=1, replica_groups={{452,460,468,476,448,456,464,472},{508,484,492,500,504,480,488,496},{20..., dimensions={0} | all-to-all | bytes 458752 | tf_op jit(solution)/shard_map/all_to_all | solution.py:340
  55.6 1.4 collective-permute-start.5
  57.0 0.7 collective-permute-start.1
  57.7 0.7 collective-permute-start.2
  58.4 0.7 collective-permute-start.3
  59.2 0.7 collective-permute-start.6
  61.4 1.3 collective-permute-start.12
  63.4 0.7 collective-permute-start.9
  64.0 14.5 %collective-permute-done.12 = bf16[7,32,128]{2,1,0:T(8,128)(2,1)S(1)} collective-permute-done((bf16[7,32,128]{2,1,0:T(8,128)(2,1)S(1)}, bf16[7,32,128]{2,1,0:T(8,128)(2,1)S(1)}, u32[]{:S(2)}, u32[]{:S(2)}) %collective-permute-start.12) | collective-permute-done | bytes 57376 | tf_op jit(solution)/shard_map/ppermute | solution.py:348
  78.6 1.9 collective-permute-start.13
  80.5 4.8 %collective-permute-start.14 = (bf16[1616,128]{1,0:T(8,128)(2,1)S(1)}, bf16[1616,128]{1,0:T(8,128)(2,1)S(1)}, u32[]{:S(2)}, u32[]{:S(2)}) collective-permute-start(bf16[1616,128]{1,0:T(8,128)(2,1)S(1)} %get-tuple-element.77), channel_id=1, source_target_pairs={{0,16},{8,24},{16,0},{24,8},{32,48},{40,56},{48,32},{56,40},{64,80... | collective-permute-start | bytes 1241096 | tf_op jit(solution)/shard_map/ppermute | solution.py:333
  85.3 1.9 collective-permute-start.15
  89.0 3.0 %collective-permute-done.14 = bf16[1616,128]{1,0:T(8,128)(2,1)S(1)} collective-permute-done((bf16[1616,128]{1,0:T(8,128)(2,1)S(1)}, bf16[1616,128]{1,0:T(8,128)(2,1)S(1)}, u32[]{:S(2)}, u32[]{:S(2)}) %collective-permute-start.14) | collective-permute-done | bytes 413728 | tf_op jit(solution)/shard_map/ppermute | solution.py:333
  92.0 4.3 %collective-permute-done.15 = bf16[1616,128]{1,0:T(8,128)(2,1)S(1)} collective-permute-done((bf16[1616,128]{1,0:T(8,128)(2,1)S(1)}, bf16[1616,128]{1,0:T(8,128)(2,1)S(1)}, u32[]{:S(2)}, u32[]{:S(2)}) %collective-permute-start.15) | collective-permute-done | bytes 413728 | tf_op jit(solution)/shard_map/ppermute | solution.py:333
  96.5 1.4 collective-permute-start.16
  99.8 1.2 collective-permute-done.16.shards_ref
  106.5 1.2 shard_map.68
  109.2 1.3 collective-permute-start.29
  110.5 0.8 shard_map.69
  112.6 27.2 %collective-permute-done.29 = bf16[4,2,7,32,128]{4,3,2,1,0:T(8,128)(2,1)S(1)} collective-permute-done((bf16[4,2,7,32,128]{4,3,2,1,0:T(8,128)(2,1)S(1)}, bf16[4,2,7,32,128]{4,3,2,1,0:T(8,128)(2,1)S(1)}, u32[]{:S(2)}, u32[]{:S(2)}) %collective-permute-start.29) | collective-permute-done | bytes 458784 | tf_op jit(solution)/shard_map/ppermute | solution.py:377
  139.9 0.7 shard_map.71
  142.1 3.2 %collective-permute-start.34 = (bf16[2,7,32,128]{3,2,1,0:T(8,128)(2,1)S(1)}, bf16[2,7,32,128]{3,2,1,0:T(8,128)(2,1)S(1)}, u32[]{:S(2)}, u32[]{:S(2)}) collective-permute-start(bf16[2,7,32,128]{3,2,1,0:T(8,128)(2,1)S(1)} %get-tuple-element.74), channel_id=1, source_target_pairs={{0,8},{8,16},{16,24},{24,0},{32,40},{40,48},{48,56},{56,32},{64,72... | collective-permute-start | bytes 344072 | tf_op jit(solution)/shard_map/ppermute | solution.py:390
  145.3 4.3 %collective-permute-start.35 = (bf16[2,7,32,128]{3,2,1,0:T(8,128)(2,1)S(1)}, bf16[2,7,32,128]{3,2,1,0:T(8,128)(2,1)S(1)}, u32[]{:S(2)}, u32[]{:S(2)}) collective-permute-start(bf16[2,7,32,128]{3,2,1,0:T(8,128)(2,1)S(1)} %get-tuple-element.73), channel_id=1, source_target_pairs={{0,16},{8,24},{16,0},{24,8},{32,48},{40,56},{48,32},{56,40},{64,80... | collective-permute-start | bytes 344072 | tf_op jit(solution)/shard_map/ppermute | solution.py:390
  149.6 3.2 %collective-permute-start.36 = (bf16[2,7,32,128]{3,2,1,0:T(8,128)(2,1)S(1)}, bf16[2,7,32,128]{3,2,1,0:T(8,128)(2,1)S(1)}, u32[]{:S(2)}, u32[]{:S(2)}) collective-permute-start(bf16[2,7,32,128]{3,2,1,0:T(8,128)(2,1)S(1)} %get-tuple-element.72), channel_id=1, source_target_pairs={{0,24},{8,0},{16,8},{24,16},{32,56},{40,32},{48,40},{56,48},{64,88... | collective-permute-start | bytes 344072 | tf_op jit(solution)/shard_map/ppermute | solution.py:390
  152.8 0.8 shard_map.72
  155.0 1.3 collective-permute-done.36
  158.4 4.8 %collective-permute-start.41 = (bf16[4,7,32,128]{3,2,1,0:T(8,128)(2,1)S(1)}, bf16[4,7,32,128]{3,2,1,0:T(8,128)(2,1)S(1)}, u32[]{:S(2)}, u32[]{:S(2)}) collective-permute-start(bf16[4,7,32,128]{3,2,1,0:T(8,128)(2,1)S(1)} %get-tuple-element.71), channel_id=1, source_target_pairs={{448,416},{449,417},{450,418},{451,419},{16,424},{17,425},{18,426}... | collective-permute-start | bytes 688136 | tf_op jit(solution)/shard_map/ppermute | solution.py:395
  163.2 9.8 %collective-permute-start.42 = (bf16[4,7,32,128]{3,2,1,0:T(8,128)(2,1)S(1)}, bf16[4,7,32,128]{3,2,1,0:T(8,128)(2,1)S(1)}, u32[]{:S(2)}, u32[]{:S(2)}) collective-permute-start(bf16[4,7,32,128]{3,2,1,0:T(8,128)(2,1)S(1)} %get-tuple-element.70), channel_id=1, source_target_pairs={{507,416},{506,417},{505,418},{504,419},{43,424},{42,425},{41,426}... | collective-permute-start | bytes 688136 | tf_op jit(solution)/shard_map/ppermute | solution.py:396
  173.0 0.8 shard_map.74
  175.1 4.9 %collective-permute-done.41 = bf16[4,7,32,128]{3,2,1,0:T(8,128)(2,1)S(1)} collective-permute-done((bf16[4,7,32,128]{3,2,1,0:T(8,128)(2,1)S(1)}, bf16[4,7,32,128]{3,2,1,0:T(8,128)(2,1)S(1)}, u32[]{:S(2)}, u32[]{:S(2)}) %collective-permute-start.41) | collective-permute-done | bytes 229408 | tf_op jit(solution)/shard_map/ppermute | solution.py:395
  180.0 5.6 %collective-permute-done.42 = bf16[4,7,32,128]{3,2,1,0:T(8,128)(2,1)S(1)} collective-permute-done((bf16[4,7,32,128]{3,2,1,0:T(8,128)(2,1)S(1)}, bf16[4,7,32,128]{3,2,1,0:T(8,128)(2,1)S(1)}, u32[]{:S(2)}, u32[]{:S(2)}) %collective-permute-start.42) | collective-permute-done | bytes 229408 | tf_op jit(solution)/shard_map/ppermute | solution.py:396
  185.6 0.7 shard_map.76
  187.9 1.4 collective-permute-start.46
  189.3 10.1 %collective-permute-start.43 = (bf16[4,7,32,128]{3,2,1,0:T(8,128)(2,1)S(1)}, bf16[4,7,32,128]{3,2,1,0:T(8,128)(2,1)S(1)}, u32[]{:S(2)}, u32[]{:S(2)}) collective-permute-start(bf16[4,7,32,128]{3,2,1,0:T(8,128)(2,1)S(1)} %broadcast_select_fusion.3), channel_id=1, source_target_pairs={{0,4},{8,12},{16,20},{24,28},{32,36},{40,44},{48,52},{56,60},{64,6... | collective-permute-start | bytes 688136 | tf_op jit(solution)/shard_map/ppermute | solution.py:421
  199.4 0.7 broadcast_select_fusion
  200.1 3.4 %all-to-all-start.1 = ((bf16[8,7,16,128]{3,2,1,0:T(8,128)(2,1)}), bf16[8,7,16,128]{3,2,1,0:T(8,128)(2,1)S(1)}, u32[]{:S(2)}, u32[]{:S(2)}) async-start(bf16[8,7,16,128]{3,2,1,0:T(8,128)(2,1)} %broadcast_select_fusion), calls=%async_computation.1 | async-start | bytes 458752 | tf_op jit(solution)/shard_map/all_to_all | solution.py:416
  203.5 5.3 %all-to-all-done.1 = bf16[8,7,16,128]{3,2,1,0:T(8,128)(2,1)S(1)} async-done(((bf16[8,7,16,128]{3,2,1,0:T(8,128)(2,1)}), bf16[8,7,16,128]{3,2,1,0:T(8,128)(2,1)S(1)}, u32[]{:S(2)}, u32[]{:S(2)}) %all-to-all-start.1) | async-done | bytes 229408 | tf_op jit(solution)/shard_map/all_to_all | solution.py:416
  208.9 14.5 %collective-permute-start.47 = (bf16[8,7,16,128]{3,2,1,0:T(8,128)(2,1)S(1)}, bf16[8,7,16,128]{3,2,1,0:T(8,128)(2,1)S(1)}, u32[]{:S(2)}, u32[]{:S(2)}) collective-permute-start(bf16[8,7,16,128]{3,2,1,0:T(8,128)(2,1)S(1)} %all-to-all-done.1), channel_id=1, source_target_pairs={{452,416},{453,417},{454,418},{455,419},{511,420},{510,421},{509,4... | collective-permute-start | bytes 688136 | tf_op jit(solution)/shard_map/ppermute | solution.py:417
  223.5 0.9 shard_map.75
  224.3 11.2 %collective-permute-done.47.parts_ref = bf16[8,7,16,128]{3,2,1,0:T(8,128)(2,1)S(1)} collective-permute-done((bf16[8,7,16,128]{3,2,1,0:T(8,128)(2,1)S(1)}, bf16[8,7,16,128]{3,2,1,0:T(8,128)(2,1)S(1)}, u32[]{:S(2)}, u32[]{:S(2)}) %collective-permute-start.47) | collective-permute-done | bytes 229408 | tf_op jit(solution)/shard_map/ppermute | solution.py:417
  235.6 1.1 shard_map.78
  (107 shorter events, 22.6 us)
Async XLA Ops:
  2.9 26.2 %collective-permute-start.4 = (bf16[8,7,16,128]{3,2,1,0:T(8,128)(2,1)S(1)}, bf16[8,7,16,128]{3,2,1,0:T(8,128)(2,1)S(1)}, u32[]{:S(2)}, u32[]{:S(2)}) collective-permute-start(bf16[8,7,16,128]{3,2,1,0:T(8,128)(2,1)S(1)} %shard_map.61), channel_id=1, source_target_pairs={{416,452},{417,453},{418,454},{419,455},{420,511},{421,510},{422,5... | collective-permute-start | bytes 688136 | tf_op jit(solution)/shard_map/ppermute | solution.py:325
  22.7 34.3 %collective-permute-start = (bf16[1392,128]{1,0:T(8,128)(2,1)S(1)}, bf16[1392,128]{1,0:T(8,128)(2,1)S(1)}, u32[]{:S(2)}, u32[]{:S(2)}) collective-permute-start(bf16[1392,128]{1,0:T(8,128)(2,1)S(1)} %shard_map.59), channel_id=1, source_target_pairs={{480,460},{481,461},{482,462},{483,463},{484,487},{485,486},{486,4... | collective-permute-start | bytes 1069064 | tf_op jit(solution)/shard_map/ppermute | solution.py:326
  55.6 3.5 %collective-permute-start.5 = (bf16[8,7,16,128]{3,2,1,0:T(8,128)(2,1)S(1)}, bf16[8,7,16,128]{3,2,1,0:T(8,128)(2,1)S(1)}, u32[]{:S(2)}, u32[]{:S(2)}) collective-permute-start(bf16[8,7,16,128]{3,2,1,0:T(8,128)(2,1)S(1)} %all_to_all.10), channel_id=1, source_target_pairs={{0,4},{8,12},{16,20},{24,28},{32,36},{40,44},{48,52},{56,60},{64,6... | collective-permute-start | bytes 688136 | tf_op jit(solution)/shard_map/ppermute | solution.py:341
  57.0 3.6 %collective-permute-start.1 = (bf16[1392,128]{1,0:T(8,128)(2,1)S(1)}, bf16[1392,128]{1,0:T(8,128)(2,1)S(1)}, u32[]{:S(2)}, u32[]{:S(2)}) collective-permute-start(bf16[1392,128]{1,0:T(8,128)(2,1)S(1)} %shard_map.60), channel_id=1, source_target_pairs={{4,12},{12,20},{20,28},{28,4},{36,44},{44,52},{52,60},{60,36},{68,... | collective-permute-start | bytes 1069064 | tf_op jit(solution)/shard_map/ppermute | solution.py:333
  57.7 2.9 %collective-permute-start.2 = (bf16[1392,128]{1,0:T(8,128)(2,1)S(1)}, bf16[1392,128]{1,0:T(8,128)(2,1)S(1)}, u32[]{:S(2)}, u32[]{:S(2)}) collective-permute-start(bf16[1392,128]{1,0:T(8,128)(2,1)S(1)} %shard_map.60), channel_id=1, source_target_pairs={{4,20},{12,28},{20,4},{28,12},{36,52},{44,60},{52,36},{60,44},{68,... | collective-permute-start | bytes 1069064 | tf_op jit(solution)/shard_map/ppermute | solution.py:333
  58.4 2.2 collective-permute-start.3
  59.2 1.4 collective-permute-start.6
  59.9 0.8 collective-permute-start.7
  61.4 17.1 %collective-permute-start.12 = (bf16[7,32,128]{2,1,0:T(8,128)(2,1)S(1)}, bf16[7,32,128]{2,1,0:T(8,128)(2,1)S(1)}, u32[]{:S(2)}, u32[]{:S(2)}) collective-permute-start(bf16[7,32,128]{2,1,0:T(8,128)(2,1)S(1)} %shard_map.62.refs_1_.refs_0_), channel_id=1, source_target_pairs={{4,0},{12,8},{20,16},{28,24},{36,32},{44,40},{52,48},{60,56},{68,6... | collective-permute-start | bytes 172040 | tf_op jit(solution)/shard_map/ppermute | solution.py:348
  62.7 24.5 %collective-permute-start.8 = (bf16[7,32,128]{2,1,0:T(8,128)(2,1)S(1)}, bf16[7,32,128]{2,1,0:T(8,128)(2,1)S(1)}, u32[]{:S(2)}, u32[]{:S(2)}) collective-permute-start(bf16[7,32,128]{2,1,0:T(8,128)(2,1)S(1)} %shard_map.62.refs_1_.refs_0_), channel_id=1, source_target_pairs={{452,453},{460,461},{468,469},{476,477},{453,454},{461,462},{469,4... | collective-permute-start | bytes 172040 | tf_op jit(solution)/shard_map/ppermute | solution.py:311
  63.4 23.8 %collective-permute-start.9 = (bf16[7,32,128]{2,1,0:T(8,128)(2,1)S(1)}, bf16[7,32,128]{2,1,0:T(8,128)(2,1)S(1)}, u32[]{:S(2)}, u32[]{:S(2)}) collective-permute-start(bf16[7,32,128]{2,1,0:T(8,128)(2,1)S(1)} %shard_map.62.refs_1_.refs_0_), channel_id=1, source_target_pairs={{453,452},{461,460},{469,468},{477,476},{454,453},{462,461},{470,4... | collective-permute-start | bytes 172040 | tf_op jit(solution)/shard_map/ppermute | solution.py:311
  78.6 10.5 %collective-permute-start.13 = (bf16[1616,128]{1,0:T(8,128)(2,1)S(1)}, bf16[1616,128]{1,0:T(8,128)(2,1)S(1)}, u32[]{:S(2)}, u32[]{:S(2)}) collective-permute-start(bf16[1616,128]{1,0:T(8,128)(2,1)S(1)} %get-tuple-element.77), channel_id=1, source_target_pairs={{0,8},{8,16},{16,24},{24,0},{32,40},{40,48},{48,56},{56,32},{64,72... | collective-permute-start | bytes 1241096 | tf_op jit(solution)/shard_map/ppermute | solution.py:333
  80.5 11.5 %collective-permute-start.14 = (bf16[1616,128]{1,0:T(8,128)(2,1)S(1)}, bf16[1616,128]{1,0:T(8,128)(2,1)S(1)}, u32[]{:S(2)}, u32[]{:S(2)}) collective-permute-start(bf16[1616,128]{1,0:T(8,128)(2,1)S(1)} %get-tuple-element.77), channel_id=1, source_target_pairs={{0,16},{8,24},{16,0},{24,8},{32,48},{40,56},{48,32},{56,40},{64,80... | collective-permute-start | bytes 1241096 | tf_op jit(solution)/shard_map/ppermute | solution.py:333
  85.3 11.1 %collective-permute-start.15 = (bf16[1616,128]{1,0:T(8,128)(2,1)S(1)}, bf16[1616,128]{1,0:T(8,128)(2,1)S(1)}, u32[]{:S(2)}, u32[]{:S(2)}) collective-permute-start(bf16[1616,128]{1,0:T(8,128)(2,1)S(1)} %get-tuple-element.77), channel_id=1, source_target_pairs={{0,24},{8,0},{16,8},{24,16},{32,56},{40,32},{48,40},{56,48},{64,88... | collective-permute-start | bytes 1241096 | tf_op jit(solution)/shard_map/ppermute | solution.py:333
  87.7 10.3 %collective-permute-start.10 = (bf16[7,32,128]{2,1,0:T(8,128)(2,1)S(1)}, bf16[7,32,128]{2,1,0:T(8,128)(2,1)S(1)}, u32[]{:S(2)}, u32[]{:S(2)}) collective-permute-start(bf16[7,32,128]{2,1,0:T(8,128)(2,1)S(1)} %shard_map.63.refs_1_.refs_2_.refs_0_), channel_id=1, source_target_pairs={{452,453},{460,461},{468,469},{476,477},{453,454},{461,462},{469,4... | collective-permute-start | bytes 172040 | tf_op jit(solution)/shard_map/ppermute | solution.py:311
  88.3 9.6 %collective-permute-start.11 = (bf16[7,32,128]{2,1,0:T(8,128)(2,1)S(1)}, bf16[7,32,128]{2,1,0:T(8,128)(2,1)S(1)}, u32[]{:S(2)}, u32[]{:S(2)}) collective-permute-start(bf16[7,32,128]{2,1,0:T(8,128)(2,1)S(1)} %shard_map.63.refs_1_.refs_2_.refs_0_), channel_id=1, source_target_pairs={{453,452},{461,460},{469,468},{477,476},{454,453},{462,461},{470,4... | collective-permute-start | bytes 172040 | tf_op jit(solution)/shard_map/ppermute | solution.py:311
  96.5 4.4 %collective-permute-start.16 = (bf16[4,1616,128]{2,1,0:T(8,128)(2,1)S(1)}, bf16[4,1616,128]{2,1,0:T(8,128)(2,1)S(1)}, u32[]{:S(2)}, u32[]{:S(2)}) collective-permute-start(bf16[4,1616,128]{2,1,0:T(8,128)(2,1)S(1)} %pad_maximum_fusion), channel_id=1, source_target_pairs={{0,4},{8,12},{16,20},{24,28},{32,36},{40,44},{48,52},{56,60},{64,6... | collective-permute-start | bytes 4964360 | tf_op jit(solution)/shard_map/ppermute | solution.py:350
  98.4 2.6 %collective-permute-start.17 = (bf16[7,32,128]{2,1,0:T(8,128)(2,1)S(1)}, bf16[7,32,128]{2,1,0:T(8,128)(2,1)S(1)}, u32[]{:S(2)}, u32[]{:S(2)}) collective-permute-start(bf16[7,32,128]{2,1,0:T(8,128)(2,1)S(1)} %shard_map.64.refs_1_.refs_3_.refs_0_), channel_id=1, source_target_pairs={{452,453},{460,461},{468,469},{476,477},{453,454},{461,462},{469,4... | collective-permute-start | bytes 172040 | tf_op jit(solution)/shard_map/ppermute | solution.py:311
  99.1 2.0 collective-permute-start.18
  101.5 1.3 collective-permute-start.19
  102.2 0.7 collective-permute-start.20
  103.4 1.3 collective-permute-start.21
  104.0 0.7 collective-permute-start.22
  105.2 1.3 collective-permute-start.23
  105.9 0.7 collective-permute-start.24
  107.8 2.7 %collective-permute-start.25 = (bf16[7,32,128]{2,1,0:T(8,128)(2,1)S(1)}, bf16[7,32,128]{2,1,0:T(8,128)(2,1)S(1)}, u32[]{:S(2)}, u32[]{:S(2)}) collective-permute-start(bf16[7,32,128]{2,1,0:T(8,128)(2,1)S(1)} %get-tuple-element.91), channel_id=1, source_target_pairs={{452,453},{460,461},{468,469},{476,477},{453,454},{461,462},{469,4... | collective-permute-start | bytes 172040 | tf_op jit(solution)/shard_map/ppermute | solution.py:311
  108.4 2.1 collective-permute-start.26
  109.2 30.7 %collective-permute-start.29 = (bf16[4,2,7,32,128]{4,3,2,1,0:T(8,128)(2,1)S(1)}, bf16[4,2,7,32,128]{4,3,2,1,0:T(8,128)(2,1)S(1)}, u32[]{:S(2)}, u32[]{:S(2)}) collective-permute-start(bf16[4,2,7,32,128]{4,3,2,1,0:T(8,128)(2,1)S(1)} %shard_map.70), channel_id=1, source_target_pairs={{4,0},{12,8},{20,16},{28,24},{36,32},{44,40},{52,48},{60,56},{68,6... | collective-permute-start | bytes 1376264 | tf_op jit(solution)/shard_map/ppermute | solution.py:377
  111.3 1.3 collective-permute-start.27
  112.0 0.7 collective-permute-start.28
  140.7 12.1 %collective-permute-start.30 = (bf16[7,32,128]{2,1,0:T(8,128)(2,1)S(1)}, bf16[7,32,128]{2,1,0:T(8,128)(2,1)S(1)}, u32[]{:S(2)}, u32[]{:S(2)}) collective-permute-start(bf16[7,32,128]{2,1,0:T(8,128)(2,1)S(1)} %get-tuple-element.87), channel_id=1, source_target_pairs={{452,453},{460,461},{468,469},{476,477},{453,454},{461,462},{469,4... | collective-permute-start | bytes 172040 | tf_op jit(solution)/shard_map/ppermute | solution.py:311
  141.3 11.5 %collective-permute-start.31 = (bf16[7,32,128]{2,1,0:T(8,128)(2,1)S(1)}, bf16[7,32,128]{2,1,0:T(8,128)(2,1)S(1)}, u32[]{:S(2)}, u32[]{:S(2)}) collective-permute-start(bf16[7,32,128]{2,1,0:T(8,128)(2,1)S(1)} %get-tuple-element.86), channel_id=1, source_target_pairs={{453,452},{461,460},{469,468},{477,476},{454,453},{462,461},{470,4... | collective-permute-start | bytes 172040 | tf_op jit(solution)/shard_map/ppermute | solution.py:311
  142.1 12.9 %collective-permute-start.34 = (bf16[2,7,32,128]{3,2,1,0:T(8,128)(2,1)S(1)}, bf16[2,7,32,128]{3,2,1,0:T(8,128)(2,1)S(1)}, u32[]{:S(2)}, u32[]{:S(2)}) collective-permute-start(bf16[2,7,32,128]{3,2,1,0:T(8,128)(2,1)S(1)} %get-tuple-element.74), channel_id=1, source_target_pairs={{0,8},{8,16},{16,24},{24,0},{32,40},{40,48},{48,56},{56,32},{64,72... | collective-permute-start | bytes 344072 | tf_op jit(solution)/shard_map/ppermute | solution.py:390
  145.3 9.7 %collective-permute-start.35 = (bf16[2,7,32,128]{3,2,1,0:T(8,128)(2,1)S(1)}, bf16[2,7,32,128]{3,2,1,0:T(8,128)(2,1)S(1)}, u32[]{:S(2)}, u32[]{:S(2)}) collective-permute-start(bf16[2,7,32,128]{3,2,1,0:T(8,128)(2,1)S(1)} %get-tuple-element.73), channel_id=1, source_target_pairs={{0,16},{8,24},{16,0},{24,8},{32,48},{40,56},{48,32},{56,40},{64,80... | collective-permute-start | bytes 344072 | tf_op jit(solution)/shard_map/ppermute | solution.py:390
  149.6 6.7 %collective-permute-start.36 = (bf16[2,7,32,128]{3,2,1,0:T(8,128)(2,1)S(1)}, bf16[2,7,32,128]{3,2,1,0:T(8,128)(2,1)S(1)}, u32[]{:S(2)}, u32[]{:S(2)}) collective-permute-start(bf16[2,7,32,128]{3,2,1,0:T(8,128)(2,1)S(1)} %get-tuple-element.72), channel_id=1, source_target_pairs={{0,24},{8,0},{16,8},{24,16},{32,56},{40,32},{48,40},{56,48},{64,88... | collective-permute-start | bytes 344072 | tf_op jit(solution)/shard_map/ppermute | solution.py:390
  153.6 2.7 %collective-permute-start.32 = (bf16[7,32,128]{2,1,0:T(8,128)(2,1)S(1)}, bf16[7,32,128]{2,1,0:T(8,128)(2,1)S(1)}, u32[]{:S(2)}, u32[]{:S(2)}) collective-permute-start(bf16[7,32,128]{2,1,0:T(8,128)(2,1)S(1)} %get-tuple-element.85), channel_id=1, source_target_pairs={{452,453},{460,461},{468,469},{476,477},{453,454},{461,462},{469,4... | collective-permute-start | bytes 172040 | tf_op jit(solution)/shard_map/ppermute | solution.py:311
  154.3 2.0 collective-permute-start.33
  156.9 16.1 %collective-permute-start.37 = (bf16[7,32,128]{2,1,0:T(8,128)(2,1)S(1)}, bf16[7,32,128]{2,1,0:T(8,128)(2,1)S(1)}, u32[]{:S(2)}, u32[]{:S(2)}) collective-permute-start(bf16[7,32,128]{2,1,0:T(8,128)(2,1)S(1)} %get-tuple-element.83), channel_id=1, source_target_pairs={{452,453},{460,461},{468,469},{476,477},{453,454},{461,462},{469,4... | collective-permute-start | bytes 172040 | tf_op jit(solution)/shard_map/ppermute | solution.py:311
  157.6 15.4 %collective-permute-start.38 = (bf16[7,32,128]{2,1,0:T(8,128)(2,1)S(1)}, bf16[7,32,128]{2,1,0:T(8,128)(2,1)S(1)}, u32[]{:S(2)}, u32[]{:S(2)}) collective-permute-start(bf16[7,32,128]{2,1,0:T(8,128)(2,1)S(1)} %get-tuple-element.82), channel_id=1, source_target_pairs={{453,452},{461,460},{469,468},{477,476},{454,453},{462,461},{470,4... | collective-permute-start | bytes 172040 | tf_op jit(solution)/shard_map/ppermute | solution.py:311
  158.4 21.6 %collective-permute-start.41 = (bf16[4,7,32,128]{3,2,1,0:T(8,128)(2,1)S(1)}, bf16[4,7,32,128]{3,2,1,0:T(8,128)(2,1)S(1)}, u32[]{:S(2)}, u32[]{:S(2)}) collective-permute-start(bf16[4,7,32,128]{3,2,1,0:T(8,128)(2,1)S(1)} %get-tuple-element.71), channel_id=1, source_target_pairs={{448,416},{449,417},{450,418},{451,419},{16,424},{17,425},{18,426}... | collective-permute-start | bytes 688136 | tf_op jit(solution)/shard_map/ppermute | solution.py:395
  163.2 22.4 %collective-permute-start.42 = (bf16[4,7,32,128]{3,2,1,0:T(8,128)(2,1)S(1)}, bf16[4,7,32,128]{3,2,1,0:T(8,128)(2,1)S(1)}, u32[]{:S(2)}, u32[]{:S(2)}) collective-permute-start(bf16[4,7,32,128]{3,2,1,0:T(8,128)(2,1)S(1)} %get-tuple-element.70), channel_id=1, source_target_pairs={{507,416},{506,417},{505,418},{504,419},{43,424},{42,425},{41,426}... | collective-permute-start | bytes 688136 | tf_op jit(solution)/shard_map/ppermute | solution.py:396
  173.8 1.3 collective-permute-start.39
  186.4 1.4 collective-permute-start.44
  187.0 0.7 collective-permute-start.45
  187.9 11.6 %collective-permute-start.46 = (bf16[8,7,16,128]{3,2,1,0:T(8,128)(2,1)S(1)}, bf16[8,7,16,128]{3,2,1,0:T(8,128)(2,1)S(1)}, u32[]{:S(2)}, u32[]{:S(2)}) collective-permute-start(bf16[8,7,16,128]{3,2,1,0:T(8,128)(2,1)S(1)} %get-tuple-element.69), channel_id=1, source_target_pairs={{4,0},{12,8},{20,16},{28,24},{36,32},{44,40},{52,48},{60,56},{68,6... | collective-permute-start | bytes 688136 | tf_op jit(solution)/shard_map/ppermute | solution.py:415
  189.3 34.1 %collective-permute-start.43 = (bf16[4,7,32,128]{3,2,1,0:T(8,128)(2,1)S(1)}, bf16[4,7,32,128]{3,2,1,0:T(8,128)(2,1)S(1)}, u32[]{:S(2)}, u32[]{:S(2)}) collective-permute-start(bf16[4,7,32,128]{3,2,1,0:T(8,128)(2,1)S(1)} %broadcast_select_fusion.3), channel_id=1, source_target_pairs={{0,4},{8,12},{16,20},{24,28},{32,36},{40,44},{48,52},{56,60},{64,6... | collective-permute-start | bytes 688136 | tf_op jit(solution)/shard_map/ppermute | solution.py:421
  200.1 8.7 %all-to-all-start.1 = ((bf16[8,7,16,128]{3,2,1,0:T(8,128)(2,1)}), bf16[8,7,16,128]{3,2,1,0:T(8,128)(2,1)S(1)}, u32[]{:S(2)}, u32[]{:S(2)}) async-start(bf16[8,7,16,128]{3,2,1,0:T(8,128)(2,1)} %broadcast_select_fusion), calls=%async_computation.1 | async-start | bytes 458752 | tf_op jit(solution)/shard_map/all_to_all | solution.py:416
  208.9 26.7 %collective-permute-start.47 = (bf16[8,7,16,128]{3,2,1,0:T(8,128)(2,1)S(1)}, bf16[8,7,16,128]{3,2,1,0:T(8,128)(2,1)S(1)}, u32[]{:S(2)}, u32[]{:S(2)}) collective-permute-start(bf16[8,7,16,128]{3,2,1,0:T(8,128)(2,1)S(1)} %all-to-all-done.1), channel_id=1, source_target_pairs={{452,416},{453,417},{454,418},{455,419},{511,420},{510,421},{509,4... | collective-permute-start | bytes 688136 | tf_op jit(solution)/shard_map/ppermute | solution.py:417
  (7 other events, 53.0 us)
